TPU v7x, 128 devices: a whole 4x4x4 slice. The times are simulated.
128 devices in a mesh: mem: 8 (over x, core), reg: 16 (over y, z).
Axes of the slice: x: 4, y: 4, z: 4, core: 2. Of those that a mesh axis runs over, the one named last changes fastest.
Arguments:
- prior_samples: float32 [256, 512, 1024], P('mem', 'reg'), may hold values from -6 to 6
- horizontal_flow_ratio: float32 [512, 1024], P('reg'), may hold values from -0.45 to 0.45
- vertical_flow_ratio: float32 [512, 1024], P('reg'), may hold values from -0.45 to 0.45
- obs_index: int32 [16, 2048], P('reg', 'mem'), may hold values from 0 to 4095
- obs_value: float32 [16, 2048], P('reg', 'mem'), may hold values from -6 to 6
- obs_weight: float32 [16, 2048], P('reg', 'mem'), may hold values from 0.00234375 to 0.0234375
Outputs:
- analysis: float32 [256, 512, 1024], P('mem', 'reg')
All inputs are finite; a program needn't handle non-finite values.
Results may differ from a plain program's by a relative error of at most 0.0003.
Values sent between devices are 32-bit elements; how exact they have to be, the bound alone decides.
No kernel may reach another device: no remote copies, remote signals or barrier semaphores. Data moves between devices by JAX's collectives and lax.ppermute only.
A program may use at most 256 MiB of HBM per device.

v0:
```python
import functools

import jax
import jax.numpy as jnp
from jax import lax
from jax.experimental import pallas as pl
from jax.experimental.pallas import tpu as pltpu
from jax.sharding import PartitionSpec as P

SECTIONS = 4
NS_ITERS = 6
MEMBERS = 256
N_MEM = 8
N_REG = 16
OWN = MEMBERS // N_MEM
ROWS = 32
WIDTH = 1024
LANES = 128
GROUPS = WIDTH // LANES
OBS = 256
HALF_OBS = OBS * GROUPS // 2
HALO = SECTIONS
EDGE = 2 * HALO
VMEM = pl.BlockSpec(memory_space=pltpu.VMEM)
SMEM = pl.BlockSpec(memory_space=pltpu.SMEM)
PARAMS = pltpu.CompilerParams(vmem_limit_bytes=56 * 1024 * 1024)


def split(x):
    high = x.astype(jnp.bfloat16)
    return high, (x - high.astype(jnp.float32)).astype(jnp.bfloat16)


def dot3(a, b, dims=(((1,), (0,)), ((), ()))):
    dot = functools.partial(
        lax.dot_general, dimension_numbers=dims, preferred_element_type=jnp.float32
    )
    return dot(a[0], b[0]) + (dot(a[0], b[1]) + dot(a[1], b[0]))


def mul(a, b):
    return dot3(split(a), split(b))


def stencil_row(read, coef, write, i):
    lane = lax.broadcasted_iota(jnp.int32, (OWN, LANES), 1)
    middle = [read(i, j) for j in range(GROUPS)]
    right = [pltpu.roll(x, 1, 1) for x in middle]
    left = [pltpu.roll(x, LANES - 1, 1) for x in middle]
    for j in range(GROUPS):
        west = jnp.where(lane == 0, right[(j - 1) % GROUPS], right[j])
        east = jnp.where(lane == LANES - 1, left[(j + 1) % GROUPS], left[j])
        k = [coef(n, i, j) for n in range(5)]
        write(
            i,
            j,
            k[0] * middle[j]
            + k[1] * west
            + k[2] * east
            + k[3] * read(i - 1, j)
            + k[4] * read(i + 1, j),
        )


def coefficients(h, v, coef_ref, i):
    a, b = jnp.maximum(h, 0.0), jnp.minimum(h, 0.0)
    c, d = jnp.maximum(v, 0.0), jnp.minimum(v, 0.0)
    for n, k in enumerate((1.0 - a + b - c + d, a, -b, c, -d)):
        coef_ref[n, i] = jnp.broadcast_to(k, (8, WIDTH))


def sections(bufs, coef_ref, first, last, out_ref, out_at):
    def coef(n, i, j):
        k = coef_ref[n, i, :, j * LANES : (j + 1) * LANES]
        return jnp.concatenate([k] * (OWN // 8), axis=0)

    for s in range(1, SECTIONS + 1):
        src, dst = bufs[(s - 1) % 2], bufs[s % 2]

        def read(i, j):
            return src[i, :, j * LANES : (j + 1) * LANES]

        def write(i, j, x):
            if s == SECTIONS:
                out_ref[j, i + out_at] = x
            else:
                dst[i, :, j * LANES : (j + 1) * LANES] = x

        def body(i, carry):
            stencil_row(read, coef, write, i)
            return carry

        lax.fori_loop(first + s, last - s, body, 0)


def interior_kernel(prior_ref, h_ref, v_ref, out_ref, rim_ref, given, one, two, coef_ref, sems):
    copies = [
        pltpu.make_async_copy(
            prior_ref.at[:, j * LANES : (j + 1) * LANES], given.at[j], sems.at[j]
        )
        for j in range(GROUPS)
    ]
    for copy in copies:
        copy.start()
    for i in range(ROWS):
        coefficients(h_ref[i : i + 1], v_ref[i : i + 1], coef_ref, i)
    for j in range(GROUPS):
        at = slice(j * LANES, (j + 1) * LANES)
        copies[j].wait()
        for i in range(ROWS):
            x = given[j, pl.ds(i, OWN, stride=ROWS), :]
            one[i, :, at] = x
            if i < EDGE:
                rim_ref[0, i, :, at] = x
            if i >= ROWS - EDGE:
                rim_ref[1, i - ROWS + EDGE, :, at] = x
    sections((one, two), coef_ref, 0, ROWS, out_ref, -HALO)


def edge_kernel(rim_ref, low_ref, high_ref, h_ref, v_ref, out_ref, one, two, coef_ref):
    for side, (halo_ref, halo_at, own_at, own_first) in enumerate(
        ((low_ref, 0, HALO, 0), (high_ref, EDGE, 0, ROWS - EDGE))
    ):
        for i in range(HALO):
            one[halo_at + i] = halo_ref[i, :OWN]
            coefficients(
                halo_ref[i, OWN : OWN + 1], halo_ref[i, OWN + 1 : OWN + 2], coef_ref, halo_at + i
            )
        for i in range(EDGE):
            one[own_at + i] = rim_ref[side, i]
            coefficients(
                h_ref[own_first + i : own_first + i + 1],
                v_ref[own_first + i : own_first + i + 1],
                coef_ref,
                own_at + i,
            )
        sections((one, two), coef_ref, 0, HALO + EDGE, out_ref, -HALO + side * HALO)


def pick_kernel(inner_ref, edge_ref, index_ref, out_ref):
    for g in range(GROUPS):
        for t in range(OBS // LANES):
            place = index_ref[g : g + 1, t * LANES : (t + 1) * LANES]
            row = jnp.broadcast_to(place >> 7, (OWN, LANES))
            col = jnp.broadcast_to(place & (LANES - 1), (OWN, LANES))
            total = jnp.zeros((OWN, LANES), jnp.float32)
            for i in range(ROWS):
                if i < HALO:
                    x = edge_ref[g, i]
                elif i < ROWS - HALO:
                    x = inner_ref[g, i - HALO]
                else:
                    x = edge_ref[g, i - ROWS + EDGE]
                x = jnp.take_along_axis(x, col, axis=1, mode="promise_in_bounds")
                total = jnp.where(row == i, x, total)
            at = (g % 4) * OBS + t * LANES
            out_ref[g // 4, :, at : at + LANES] = total


def gram_kernel(core_ref, obs_ref, value_ref, weight_ref, keep_ref, send_ref):
    obs = obs_ref[...]
    mean = jnp.sum(obs, axis=0, keepdims=True) * (1.0 / MEMBERS)
    anomalies = obs - mean
    weighted = split(anomalies * weight_ref[...])
    innovation = jnp.broadcast_to(value_ref[...] - mean, (8, HALF_OBS))
    nt = (((1,), (1,)), ((), ()))
    gram = dot3(split(anomalies), weighted, nt)
    drive = dot3(split(innovation), weighted, nt)
    core = core_ref[0]
    half = MEMBERS // 2
    for c in range(2):

        @pl.when(core == c)
        def _():
            keep_ref[:half] = gram[c * half : (c + 1) * half]
            send_ref[:half] = gram[(1 - c) * half : (2 - c) * half]

    keep_ref[half:] = drive
    send_ref[half:] = drive


def weights_kernel(core_ref, mine_ref, other_ref, high_ref, low_ref, gram_ref):
    core = core_ref[0]
    half = MEMBERS // 2
    for c in range(2):

        @pl.when(core == c)
        def _():
            gram_ref[c * half : (c + 1) * half] = mine_ref[:half]
            gram_ref[(1 - c) * half : (2 - c) * half] = other_ref[:half]

    drive = mine_ref[half:]
    rows = lax.broadcasted_iota(jnp.int32, (MEMBERS, MEMBERS), 0)
    cols = lax.broadcasted_iota(jnp.int32, (MEMBERS, MEMBERS), 1)
    identity = (rows == cols).astype(jnp.float32)
    gram = gram_ref[...] + (MEMBERS - 1.0) * identity
    squares = jnp.sum(jnp.sum(gram * gram, axis=0, keepdims=True), axis=1, keepdims=True)
    scale = jnp.sqrt(squares)
    upper = gram / scale
    lower = 1.5 * identity - 0.5 * upper
    middle = lower
    for number in range(1, NS_ITERS):
        upper = mul(upper, middle)
        middle = 1.5 * identity - 0.5 * mul(lower, upper)
        lower = mul(middle, lower)
    lower_parts = split(lower)
    nt = (((1,), (1,)), ((), ()))
    inner = dot3(split(drive), lower_parts, nt)
    wbar = dot3(split(inner), lower_parts, nt)[:1] / scale
    weights = (MEMBERS - 1.0) ** 0.5 * lower / jnp.sqrt(scale) + wbar
    rest = (1.0 - jnp.sum(weights, axis=1, keepdims=True)) * (1.0 / MEMBERS)
    high, low = split(weights + rest)
    high_ref[...] = high
    low_ref[...] = low


def product_kernel(high_ref, low_ref, inner_ref, edge_ref, out_ref):
    weights = (high_ref[...], low_ref[...])
    cells = MEMBERS

    def pair(ref, i, r):
        parts = []
        for t in range(2):
            x = jnp.concatenate([ref[s, i + t] for s in range(N_MEM)], axis=0)
            parts.append(split(x))
        x = tuple(jnp.concatenate([parts[0][n], parts[1][n]], axis=1) for n in range(2))
        y = dot3(weights, x)
        for t in range(2):
            out_ref[pl.ds(r + t, cells, stride=ROWS), :] = y[:, t * LANES : (t + 1) * LANES]

    for i in range(0, HALO, 2):
        pair(edge_ref, i, i)
        pair(edge_ref, HALO + i, ROWS - HALO + i)

    def body(n, carry):
        pair(inner_ref, 2 * n, HALO + 2 * n)
        return carry

    lax.fori_loop(0, (ROWS - EDGE) // 2, body, 0)


def place_kernel(x_ref, out_ref, sems):
    copies = [
        pltpu.make_async_copy(
            x_ref.at[g], out_ref.at[:, :, g * LANES : (g + 1) * LANES], sems.at[g]
        )
        for g in range(GROUPS)
    ]
    for copy in copies:
        copy.start()
    for copy in copies:
        copy.wait()


def f32(*shape):
    return jax.ShapeDtypeStruct(shape, jnp.float32)


def swap(x, axis, bit):
    count = lax.axis_size(axis)
    return lax.ppermute(x, axis, [(i, i ^ bit) for i in range(count)])


def shift(x, axis, step):
    count = lax.axis_size(axis)
    return lax.ppermute(x, axis, [(i, (i + step) % count) for i in range(count)])


def local(
    prior_samples, horizontal_flow_ratio, vertical_flow_ratio, obs_index, obs_value, obs_weight
):
    h, v = horizontal_flow_ratio, vertical_flow_ratio
    mem = lax.axis_index("mem")
    core = (mem % 2).astype(jnp.int32).reshape(1)

    def rows_out(first):
        x = jnp.concatenate(
            [
                prior_samples[:, first : first + HALO],
                h[None, first : first + HALO],
                v[None, first : first + HALO],
            ],
            axis=0,
        )
        return jnp.pad(jnp.transpose(x, (1, 0, 2)), ((0, 0), (0, 6), (0, 0)))

    low = shift(rows_out(ROWS - HALO), "reg", 1)
    high = shift(rows_out(0), "reg", -1)

    facts = jnp.concatenate([obs_index.astype(jnp.float32), obs_value, obs_weight], axis=0)
    facts = lax.all_to_all(
        jnp.broadcast_to(facts[None], (N_MEM, 3, OBS)), "mem", 0, 0, tiled=True
    )
    index = facts[:, 0].astype(jnp.int32)
    half_facts = lax.dynamic_slice_in_dim(facts, core[0] * 4, 4, axis=0)
    value = half_facts[:, 1].reshape(1, HALF_OBS)
    weight = half_facts[:, 2].reshape(1, HALF_OBS)

    flat = prior_samples.reshape(OWN * ROWS, WIDTH)
    inner, rim = pl.pallas_call(
        interior_kernel,
        out_shape=[f32(GROUPS, ROWS - EDGE, OWN, LANES), f32(2, EDGE, OWN, WIDTH)],
        in_specs=[pl.BlockSpec(memory_space=pl.ANY), VMEM, VMEM],
        out_specs=[VMEM, VMEM],
        scratch_shapes=[
            pltpu.VMEM((GROUPS, OWN * ROWS, LANES), jnp.float32),
            pltpu.VMEM((ROWS, OWN, WIDTH), jnp.float32),
            pltpu.VMEM((ROWS, OWN, WIDTH), jnp.float32),
            pltpu.VMEM((5, ROWS, 8, WIDTH), jnp.float32),
            pltpu.SemaphoreType.DMA((GROUPS,)),
        ],
        compiler_params=PARAMS,
    )(flat, h, v)
    edge = pl.pallas_call(
        edge_kernel,
        out_shape=f32(GROUPS, EDGE, OWN, LANES),
        in_specs=[VMEM] * 5,
        out_specs=VMEM,
        scratch_shapes=[
            pltpu.VMEM((HALO + EDGE, OWN, WIDTH), jnp.float32),
            pltpu.VMEM((HALO + EDGE, OWN, WIDTH), jnp.float32),
            pltpu.VMEM((5, HALO + EDGE, 8, WIDTH), jnp.float32),
        ],
        compiler_params=PARAMS,
    )(rim, low, high, h, v)
    picked = pl.pallas_call(
        pick_kernel,
        out_shape=f32(2, OWN, HALF_OBS),
        in_specs=[VMEM] * 3,
        out_specs=VMEM,
        compiler_params=PARAMS,
    )(inner, edge, index)

    picked = jnp.broadcast_to(picked[None], (N_MEM // 2, 2, OWN, HALF_OBS))
    obs = lax.all_to_all(
        picked.reshape(N_MEM, OWN, HALF_OBS), "mem", 0, 0, tiled=True
    ).reshape(MEMBERS, HALF_OBS)

    inner, edge, obs = lax.optimization_barrier((inner, edge, obs))
    inner = lax.all_to_all(inner, "mem", 0, 0, tiled=True)
    edge = lax.all_to_all(edge, "mem", 0, 0, tiled=True)

    keep, send = pl.pallas_call(
        gram_kernel,
        out_shape=[f32(MEMBERS // 2 + 8, MEMBERS)] * 2,
        in_specs=[SMEM, VMEM, VMEM, VMEM],
        out_specs=[VMEM, VMEM],
        compiler_params=PARAMS,
    )(core, obs, value, weight)
    total = keep + swap(send, "mem", 1)
    for bit in (1, 2, 4, 8):
        total = total + swap(total, "reg", bit)
    other = swap(total, "mem", 1)

    bf16 = jax.ShapeDtypeStruct((MEMBERS, MEMBERS), jnp.bfloat16)
    weights = pl.pallas_call(
        weights_kernel,
        out_shape=[bf16, bf16],
        in_specs=[SMEM, VMEM, VMEM],
        out_specs=[VMEM, VMEM],
        scratch_shapes=[pltpu.VMEM((MEMBERS, MEMBERS), jnp.float32)],
        compiler_params=PARAMS,
    )(core, total, other)

    analysis = pl.pallas_call(
        product_kernel,
        out_shape=f32(MEMBERS * ROWS, LANES),
        in_specs=[VMEM] * 4,
        out_specs=VMEM,
        compiler_params=PARAMS,
    )(*weights, inner, edge)
    analysis = lax.all_to_all(
        analysis.reshape(N_MEM, OWN, ROWS, LANES), "mem", 0, 0, tiled=True
    )
    return pl.pallas_call(
        place_kernel,
        out_shape=f32(OWN, ROWS, WIDTH),
        in_specs=[pl.BlockSpec(memory_space=pl.ANY)],
        out_specs=pl.BlockSpec(memory_space=pl.ANY),
        scratch_shapes=[pltpu.SemaphoreType.DMA((GROUPS,))],
        compiler_params=PARAMS,
    )(analysis)


def solution(mesh):
    placed = (
        P("mem", "reg", None),
        P("reg", None),
        P("reg", None),
        P("reg", "mem"),
        P("reg", "mem"),
        P("reg", "mem"),
    )
    return jax.shard_map(
        local, mesh=mesh, in_specs=placed, out_specs=P("mem", "reg", None), check_vma=False
    )
```

profile of v0, /device:TPU:1, one launch (start us, length us, event | category | flops | bytes accessed | tf_op | source)
XLA Modules:
  0.0 336.2 jit_solution(13808843417297796378)
XLA Ops:
  1.6 1.8 fusion.1
  3.9 2.5 collective-permute-start
  6.9 4.7 %collective-permute-start.1 = (f32[4,40,1024]{2,1,0:T(8,128)S(1)}, f32[4,40,1024]{2,1,0:T(8,128)S(1)}, u32[]{:S(2)}, u32[]{:S(2)}) collective-permute-start(f32[4,40,1024]{2,1,0:T(8,128)S(1)} %pad.8), channel_id=1, source_target_pairs={{0,15},{1,0},{2,1},{3,2},{4,3},{5,4},{6,5},{7,6},{8,7},{9,8},{10,9... | collective-permute-start | bytes 1966088 | tf_op jit(solution)/shard_map/ppermute | solution.py:266
  12.2 5.3 %all-to-all-start = ((f32[8,3,256]{2,1,0:T(4,128)}), f32[8,3,256]{2,1,0:T(4,128)S(1)}, u32[]{:S(2)}, u32[]{:S(2)}) async-start(f32[8,3,256]{2,1,0:T(4,128)} %broadcast_in_dim.28), calls=%async_computation | async-start | bytes 65536 | tf_op jit(solution)/shard_map/all_to_all | solution.py:291
  17.5 22.4 %shard_map.64 = (f32[8,24,32,128]{3,2,1,0:T(8,128)}, f32[2,8,32,1024]{3,2,1,0:T(8,128)}) custom-call(f32[1024,1024]{1,0:T(8,128)} %bitcast.14, f32[32,1024]{1,0:T(8,128)} %h_ref.3, f32[32,1024]{1,0:T(8,128)} %v_ref.3), custom_call_target="tpu_custom_call" | custom-call | tf_op jit(solution)/shard_map/pallas_call | solution.py:300
  41.6 11.5 %shard_map.65.edge_ref = f32[8,8,32,128]{3,2,1,0:T(8,128)} custom-call(f32[2,8,32,1024]{3,2,1,0:T(8,128)} %get-tuple-element.15.rim_ref, f32[4,40,1024]{2,1,0:T(8,128)} %copy-done.2, f32[4,40,1024]{2,1,0:T(8,128)} %copy-done.3, f32[32,1024]{1,0:T(8,128)} %h_ref.3, f32[32,1024]{1,0:T(8,128)} %v_ref.3), custom_call_target="tpu_custom_call" | custom-call | tf_op jit(solution)/shard_map/pallas_call | solution.py:314
  53.1 5.3 %shard_map.66 = f32[2,32,1024]{2,1,0:T(8,128)} custom-call(f32[8,24,32,128]{3,2,1,0:T(8,128)} %get-tuple-element.21.inner_ref, f32[8,8,32,128]{3,2,1,0:T(8,128)} %shard_map.65.edge_ref, s32[8,256]{1,0:T(8,128)} %fusion.index_ref), custom_call_target="tpu_custom_call" | custom-call | tf_op jit(solution)/shard_map/pallas_call | solution.py:326
  58.4 1.1 broadcast_in_dim.29
  59.4 19.8 %all_to_all.25 = f32[8,32,1024]{2,1,0:T(8,128)} all-to-all(f32[8,32,1024]{2,1,0:T(8,128)S(1)} %bitcast.15), channel_id=1, replica_groups=mesh['mem'=8,'reg'=16] {'mem'}, dimensions={0} | all-to-all | bytes 2097152 | tf_op jit(solution)/shard_map/all_to_all | solution.py:335
  79.2 19.2 %all_to_all.26.edge_ref = f32[8,8,32,128]{3,2,1,0:T(8,128)} all-to-all(f32[8,8,32,128]{3,2,1,0:T(8,128)S(1)} %copy-done.1), channel_id=1, replica_groups=mesh['mem'=8,'reg'=16] {'mem'}, dimensions={0} | all-to-all | bytes 2097152 | tf_op jit(solution)/shard_map/all_to_all | solution.py:341
  98.4 4.6 %all-to-all-start.2 = ((f32[8,24,32,128]{3,2,1,0:T(8,128)}), f32[8,24,32,128]{3,2,1,0:T(8,128)S(1)}, u32[]{:S(2)}, u32[]{:S(2)}) async-start(f32[8,24,32,128]{3,2,1,0:T(8,128)} %get-tuple-element.21.inner_ref), calls=%async_computation.2 | async-start | bytes 6291456 | tf_op jit(solution)/shard_map/all_to_all | solution.py:340
  103.6 3.0 shard_map.67
  106.7 1.5 collective-permute-done.2
  109.2 5.1 %collective-permute-done.3 = f32[136,256]{1,0:T(8,128)S(1)} collective-permute-done((f32[136,256]{1,0:T(8,128)S(1)}, f32[136,256]{1,0:T(8,128)S(1)}, u32[]{:S(2)}, u32[]{:S(2)}) %collective-permute-start.3) | collective-permute-done | bytes 139296 | tf_op jit(solution)/shard_map/ppermute | solution.py:261
  114.4 5.7 %collective-permute-done.4 = f32[136,256]{1,0:T(8,128)S(1)} collective-permute-done((f32[136,256]{1,0:T(8,128)S(1)}, f32[136,256]{1,0:T(8,128)S(1)}, u32[]{:S(2)}, u32[]{:S(2)}) %collective-permute-start.4) | collective-permute-done | bytes 139296 | tf_op jit(solution)/shard_map/ppermute | solution.py:261
  120.3 4.2 %collective-permute-done.5 = f32[136,256]{1,0:T(8,128)S(1)} collective-permute-done((f32[136,256]{1,0:T(8,128)S(1)}, f32[136,256]{1,0:T(8,128)S(1)}, u32[]{:S(2)}, u32[]{:S(2)}) %collective-permute-start.5) | collective-permute-done | bytes 139296 | tf_op jit(solution)/shard_map/ppermute | solution.py:261
  125.3 4.9 %collective-permute-done.6 = f32[136,256]{1,0:T(8,128)S(1)} collective-permute-done((f32[136,256]{1,0:T(8,128)S(1)}, f32[136,256]{1,0:T(8,128)S(1)}, u32[]{:S(2)}, u32[]{:S(2)}) %collective-permute-start.6) | collective-permute-done | bytes 139296 | tf_op jit(solution)/shard_map/ppermute | solution.py:261
  130.2 4.0 %collective-permute-start.7 = (f32[136,256]{1,0:T(8,128)S(1)}, f32[136,256]{1,0:T(8,128)S(1)}, u32[]{:S(2)}, u32[]{:S(2)}) collective-permute-start(f32[136,256]{1,0:T(8,128)S(1)} %add.32.mine_ref), channel_id=1, source_target_pairs={{0,16},{16,0},{32,48},{48,32},{64,80},{80,64},{96,112},{112,96},{1... | collective-permute-start | bytes 417800 | tf_op jit(solution)/shard_map/ppermute | solution.py:261
  134.1 1.0 collective-permute-done.7.other_ref
  135.8 5.9 %shard_map.68 = (bf16[256,256]{1,0:T(8,128)(2,1)}, bf16[256,256]{1,0:T(8,128)(2,1)}) custom-call(s32[1]{0:T(128)} %bitcast.core_ref, f32[136,256]{1,0:T(8,128)} %copy-done.4, f32[136,256]{1,0:T(8,128)} %copy-done.5), custom_call_target="tpu_custom_call" | custom-call | tf_op jit(solution)/shard_map/pallas_call | solution.py:356
  141.7 1.6 copy-done
  143.4 10.1 %shard_map.69 = f32[8192,128]{1,0:T(8,128)} custom-call(bf16[256,256]{1,0:T(8,128)(2,1)} %get-tuple-element.19.high_ref, bf16[256,256]{1,0:T(8,128)(2,1)} %get-tuple-element.20.low_ref, f32[8,24,32,128]{3,2,1,0:T(8,128)} %copy-done, f32[8,8,32,128]{3,2,1,0:T(8,128)} %all_to_all.26.edge_ref), custom_call_target="tpu_custom_call" | custom-call | tf_op jit(solution)/shard_map/pallas_call | solution.py:365
  153.5 54.3 %all_to_all.27.x_ref = f32[8,32,32,128]{3,2,1,0:T(8,128)} all-to-all(f32[8,32,32,128]{3,2,1,0:T(8,128)} %bitcast.13), channel_id=1, replica_groups=mesh['mem'=8,'reg'=16] {'mem'}, dimensions={0} | all-to-all | bytes 8388608 | tf_op jit(solution)/shard_map/all_to_all | solution.py:372
  207.8 128.2 %shard_map.70 = f32[32,32,1024]{2,1,0:T(8,128)} custom-call(f32[8,32,32,128]{3,2,1,0:T(8,128)} %all_to_all.27.x_ref), custom_call_target="tpu_custom_call" | custom-call | tf_op jit(solution)/shard_map/pallas_call | solution.py:375
  (49 shorter events, 8.2 us)
Async XLA Ops:
  1.6 10.0 %copy-start.8 = (s32[1,256]{1,0:T(1,128)S(1)}, s32[1,256]{1,0:T(1,128)}, u32[]{:S(2)}) copy-start(s32[1,256]{1,0:T(1,128)} %param.9) | copy-start | bytes 3076
  1.6 10.0 %copy-start.6 = (f32[1,256]{1,0:T(1,128)S(1)}, f32[1,256]{1,0:T(1,128)}, u32[]{:S(2)}) copy-start(f32[1,256]{1,0:T(1,128)} %param.11) | copy-start | bytes 3076
  1.6 10.0 %copy-start.7 = (f32[1,256]{1,0:T(1,128)S(1)}, f32[1,256]{1,0:T(1,128)}, u32[]{:S(2)}) copy-start(f32[1,256]{1,0:T(1,128)} %param.10) | copy-start | bytes 3076
  3.9 36.6 %collective-permute-start = (f32[4,40,1024]{2,1,0:T(8,128)S(1)}, f32[4,40,1024]{2,1,0:T(8,128)S(1)}, u32[]{:S(2)}, u32[]{:S(2)}) collective-permute-start(f32[4,40,1024]{2,1,0:T(8,128)S(1)} %pad.7), channel_id=1, source_target_pairs={{0,1},{1,2},{2,3},{3,4},{4,5},{5,6},{6,7},{7,8},{8,9},{9,10},{10,1... | collective-permute-start | bytes 1966088 | tf_op jit(solution)/shard_map/ppermute | solution.py:266
  6.9 33.6 %collective-permute-start.1 = (f32[4,40,1024]{2,1,0:T(8,128)S(1)}, f32[4,40,1024]{2,1,0:T(8,128)S(1)}, u32[]{:S(2)}, u32[]{:S(2)}) collective-permute-start(f32[4,40,1024]{2,1,0:T(8,128)S(1)} %pad.8), channel_id=1, source_target_pairs={{0,15},{1,0},{2,1},{3,2},{4,3},{5,4},{6,5},{7,6},{8,7},{9,8},{10,9... | collective-permute-start | bytes 1966088 | tf_op jit(solution)/shard_map/ppermute | solution.py:266
  12.2 27.7 %all-to-all-start = ((f32[8,3,256]{2,1,0:T(4,128)}), f32[8,3,256]{2,1,0:T(4,128)S(1)}, u32[]{:S(2)}, u32[]{:S(2)}) async-start(f32[8,3,256]{2,1,0:T(4,128)} %broadcast_in_dim.28), calls=%async_computation | async-start | bytes 65536 | tf_op jit(solution)/shard_map/all_to_all | solution.py:291
  40.5 0.8 copy-start.2
  40.5 1.1 copy-start.3
  53.1 26.1 %copy-start.1 = (f32[8,8,32,128]{3,2,1,0:T(8,128)S(1)}, f32[8,8,32,128]{3,2,1,0:T(8,128)}, u32[]{:S(2)}) copy-start(f32[8,8,32,128]{3,2,1,0:T(8,128)} %shard_map.65.edge_ref) | copy-start | bytes 3145732
  98.4 43.3 %all-to-all-start.2 = ((f32[8,24,32,128]{3,2,1,0:T(8,128)}), f32[8,24,32,128]{3,2,1,0:T(8,128)S(1)}, u32[]{:S(2)}, u32[]{:S(2)}) async-start(f32[8,24,32,128]{3,2,1,0:T(8,128)} %get-tuple-element.21.inner_ref), calls=%async_computation.2 | async-start | bytes 6291456 | tf_op jit(solution)/shard_map/all_to_all | solution.py:340
  106.6 1.6 collective-permute-start.2
  109.1 5.2 %collective-permute-start.3 = (f32[136,256]{1,0:T(8,128)S(1)}, f32[136,256]{1,0:T(8,128)S(1)}, u32[]{:S(2)}, u32[]{:S(2)}) collective-permute-start(f32[136,256]{1,0:T(8,128)S(1)} %add.28), channel_id=1, source_target_pairs={{0,1},{1,0},{2,3},{3,2},{4,5},{5,4},{6,7},{7,6},{8,9},{9,8},{10,11... | collective-permute-start | bytes 417800 | tf_op jit(solution)/shard_map/ppermute | solution.py:261
  114.3 5.8 %collective-permute-start.4 = (f32[136,256]{1,0:T(8,128)S(1)}, f32[136,256]{1,0:T(8,128)S(1)}, u32[]{:S(2)}, u32[]{:S(2)}) collective-permute-start(f32[136,256]{1,0:T(8,128)S(1)} %add.29), channel_id=1, source_target_pairs={{0,2},{1,3},{2,0},{3,1},{4,6},{5,7},{6,4},{7,5},{8,10},{9,11},{10,... | collective-permute-start | bytes 417800 | tf_op jit(solution)/shard_map/ppermute | solution.py:261
  120.2 4.3 %collective-permute-start.5 = (f32[136,256]{1,0:T(8,128)S(1)}, f32[136,256]{1,0:T(8,128)S(1)}, u32[]{:S(2)}, u32[]{:S(2)}) collective-permute-start(f32[136,256]{1,0:T(8,128)S(1)} %add.30), channel_id=1, source_target_pairs={{0,4},{1,5},{2,6},{3,7},{4,0},{5,1},{6,2},{7,3},{8,12},{9,13},{10,... | collective-permute-start | bytes 417800 | tf_op jit(solution)/shard_map/ppermute | solution.py:261
  124.5 5.7 %collective-permute-start.6 = (f32[136,256]{1,0:T(8,128)S(1)}, f32[136,256]{1,0:T(8,128)S(1)}, u32[]{:S(2)}, u32[]{:S(2)}) collective-permute-start(f32[136,256]{1,0:T(8,128)S(1)} %add.31), channel_id=1, source_target_pairs={{0,8},{1,9},{2,10},{3,11},{4,12},{5,13},{6,14},{7,15},{8,0},{9,1},... | collective-permute-start | bytes 417800 | tf_op jit(solution)/shard_map/ppermute | solution.py:261
  130.2 5.0 %copy-start.4 = (f32[136,256]{1,0:T(8,128)}, f32[136,256]{1,0:T(8,128)S(1)}, u32[]{:S(2)}) copy-start(f32[136,256]{1,0:T(8,128)S(1)} %add.32.mine_ref) | copy-start | bytes 417796
  130.2 5.0 %collective-permute-start.7 = (f32[136,256]{1,0:T(8,128)S(1)}, f32[136,256]{1,0:T(8,128)S(1)}, u32[]{:S(2)}, u32[]{:S(2)}) collective-permute-start(f32[136,256]{1,0:T(8,128)S(1)} %add.32.mine_ref), channel_id=1, source_target_pairs={{0,16},{16,0},{32,48},{48,32},{64,80},{80,64},{96,112},{112,96},{1... | collective-permute-start | bytes 417800 | tf_op jit(solution)/shard_map/ppermute | solution.py:261
  135.1 0.7 copy-start.5
  141.7 1.6 copy-start
where the time goes:
time: 337 us; the launch traced here: 336 us
  Pallas kernels  186 us (55%)
  blocking collectives  93.3 us (28%)
  waiting for transfers between devices  22.3 us (7%)
  starting transfers between devices  22.2 us (7%)
  local copies, waits for them, and re-layouts  9.78 us (3%)
    pallas_call x1, Pallas kernels, local(): pl.pallas_call(place_kernel, out_shape=f32(OWN, ROWS, WIDTH), in_specs=[p...  128 us
    all_to_all x1, blocking collectives, local(): lax.all_to_all(analysis.reshape(N_MEM, OWN, ROWS, LANES), 'mem', 0, 0, ti...  54.3 us
    pallas_call x1, Pallas kernels, local(): pl.pallas_call(interior_kernel, out_shape=[f32(GROUPS, ROWS - EDGE, OWN,...  22.4 us
    ppermute x6, waiting for transfers between devices, swap(): return lax.ppermute(x, axis, [(i, i ^ bit) for i in range(count)])  22.3 us
    all_to_all x1, blocking collectives, local(): lax.all_to_all(picked.reshape(N_MEM, OWN, HALF_OBS), 'mem', 0, 0, tiled=T...  19.8 us
    all_to_all x1, blocking collectives, local(): edge = lax.all_to_all(edge, 'mem', 0, 0, tiled=True)  19.2 us
    pallas_call x1, Pallas kernels, local(): pl.pallas_call(edge_kernel, out_shape=f32(GROUPS, EDGE, OWN, LANES), in_s...  11.5 us
    pallas_call x1, Pallas kernels, local(): pl.pallas_call(product_kernel, out_shape=f32(MEMBERS * ROWS, LANES), in_s...  10.1 us
  transfers between devices with their start and end apart: 10, of which 6 were waited for; matrix products, arithmetic and copies ran while one was open for 1% of the time, Pallas kernels for 9%

commit v1 on v0

--- a/solution.py
+++ b/solution.py
@@ -44,29 +44,32 @@
 
 def stencil_row(read, coef, write, i):
     lane = lax.broadcasted_iota(jnp.int32, (OWN, LANES), 1)
-    middle = [read(i, j) for j in range(GROUPS)]
-    right = [pltpu.roll(x, 1, 1) for x in middle]
-    left = [pltpu.roll(x, LANES - 1, 1) for x in middle]
+    first = read(i, 0)
+    left_first = pltpu.roll(first, LANES - 1, 1)
+    right_before = pltpu.roll(read(i, GROUPS - 1), 1, 1)
+    middle, left = first, left_first
     for j in range(GROUPS):
-        west = jnp.where(lane == 0, right[(j - 1) % GROUPS], right[j])
-        east = jnp.where(lane == LANES - 1, left[(j + 1) % GROUPS], left[j])
-        k = [coef(n, i, j) for n in range(5)]
-        write(
-            i,
-            j,
-            k[0] * middle[j]
-            + k[1] * west
-            + k[2] * east
-            + k[3] * read(i - 1, j)
-            + k[4] * read(i + 1, j),
+        if j + 1 < GROUPS:
+            after = read(i, j + 1)
+            left_after = pltpu.roll(after, LANES - 1, 1)
+        else:
+            after, left_after = first, left_first
+        right = pltpu.roll(middle, 1, 1)
+        h, v = coef(0, i, j), coef(1, i, j)
+        side = jnp.where(
+            h > 0.0,
+            jnp.where(lane == 0, right_before, right),
+            jnp.where(lane == LANES - 1, left_after, left),
         )
+        below = jnp.where(v > 0.0, read(i - 1, j), read(i + 1, j))
+        ah, av = jnp.abs(h), jnp.abs(v)
+        write(i, j, (1.0 - ah - av) * middle + ah * side + av * below)
+        middle, left, right_before = after, left_after, right
 
 
 def coefficients(h, v, coef_ref, i):
-    a, b = jnp.maximum(h, 0.0), jnp.minimum(h, 0.0)
-    c, d = jnp.maximum(v, 0.0), jnp.minimum(v, 0.0)
-    for n, k in enumerate((1.0 - a + b - c + d, a, -b, c, -d)):
-        coef_ref[n, i] = jnp.broadcast_to(k, (8, WIDTH))
+    coef_ref[0, i] = jnp.broadcast_to(h, (8, WIDTH))
+    coef_ref[1, i] = jnp.broadcast_to(v, (8, WIDTH))
 
 
 def sections(bufs, coef_ref, first, last, out_ref, out_at):
@@ -216,40 +219,29 @@
 
 def product_kernel(high_ref, low_ref, inner_ref, edge_ref, out_ref):
     weights = (high_ref[...], low_ref[...])
-    cells = MEMBERS
-
-    def pair(ref, i, r):
-        parts = []
-        for t in range(2):
-            x = jnp.concatenate([ref[s, i + t] for s in range(N_MEM)], axis=0)
-            parts.append(split(x))
-        x = tuple(jnp.concatenate([parts[0][n], parts[1][n]], axis=1) for n in range(2))
+
+    def rows(ref, i, r):
+        parts = [
+            split(jnp.concatenate([ref[s, i + t] for s in range(N_MEM)], axis=0))
+            for t in range(HALO)
+        ]
+        x = tuple(jnp.concatenate([p[n] for p in parts], axis=1) for n in range(2))
         y = dot3(weights, x)
-        for t in range(2):
-            out_ref[pl.ds(r + t, cells, stride=ROWS), :] = y[:, t * LANES : (t + 1) * LANES]
-
-    for i in range(0, HALO, 2):
-        pair(edge_ref, i, i)
-        pair(edge_ref, HALO + i, ROWS - HALO + i)
+        for t in range(HALO):
+            out_ref[pl.ds(r + t, MEMBERS, stride=ROWS), :] = y[:, t * LANES : (t + 1) * LANES]
+
+    rows(edge_ref, 0, 0)
+    rows(edge_ref, HALO, ROWS - HALO)
 
     def body(n, carry):
-        pair(inner_ref, 2 * n, HALO + 2 * n)
+        rows(inner_ref, HALO * n, HALO + HALO * n)
         return carry
 
-    lax.fori_loop(0, (ROWS - EDGE) // 2, body, 0)
-
-
-def place_kernel(x_ref, out_ref, sems):
-    copies = [
-        pltpu.make_async_copy(
-            x_ref.at[g], out_ref.at[:, :, g * LANES : (g + 1) * LANES], sems.at[g]
-        )
-        for g in range(GROUPS)
-    ]
-    for copy in copies:
-        copy.start()
-    for copy in copies:
-        copy.wait()
+    lax.fori_loop(0, (ROWS - EDGE) // HALO, body, 0)
+
+
+def place_kernel(x_ref, out_ref):
+    out_ref[...] = x_ref[0]
 
 
 def f32(*shape):
@@ -306,7 +298,7 @@
             pltpu.VMEM((GROUPS, OWN * ROWS, LANES), jnp.float32),
             pltpu.VMEM((ROWS, OWN, WIDTH), jnp.float32),
             pltpu.VMEM((ROWS, OWN, WIDTH), jnp.float32),
-            pltpu.VMEM((5, ROWS, 8, WIDTH), jnp.float32),
+            pltpu.VMEM((2, ROWS, 8, WIDTH), jnp.float32),
             pltpu.SemaphoreType.DMA((GROUPS,)),
         ],
         compiler_params=PARAMS,
@@ -319,7 +311,7 @@
         scratch_shapes=[
             pltpu.VMEM((HALO + EDGE, OWN, WIDTH), jnp.float32),
             pltpu.VMEM((HALO + EDGE, OWN, WIDTH), jnp.float32),
-            pltpu.VMEM((5, HALO + EDGE, 8, WIDTH), jnp.float32),
+            pltpu.VMEM((2, HALO + EDGE, 8, WIDTH), jnp.float32),
         ],
         compiler_params=PARAMS,
     )(rim, low, high, h, v)
@@ -374,10 +366,10 @@
     )
     return pl.pallas_call(
         place_kernel,
+        grid=(GROUPS,),
         out_shape=f32(OWN, ROWS, WIDTH),
-        in_specs=[pl.BlockSpec(memory_space=pl.ANY)],
-        out_specs=pl.BlockSpec(memory_space=pl.ANY),
-        scratch_shapes=[pltpu.SemaphoreType.DMA((GROUPS,))],
+        in_specs=[pl.BlockSpec((1, OWN, ROWS, LANES), lambda g: (g, 0, 0, 0))],
+        out_specs=pl.BlockSpec((OWN, ROWS, LANES), lambda g: (0, 0, g)),
         compiler_params=PARAMS,
     )(analysis)
 

time: 337 us -> 214 us (0.64)
  Pallas kernels: 186 us -> 63.6 us
    pallas_call x1, Pallas kernels: 128 us -> 6.58 us  [local(): pl.pallas_call(place_kernel, grid=(GROUPS,), out_shape=f32(OWN, ROWS, WID...]
  transfers between devices with their start and end apart: 10 -> 10, of which waited for: 6 -> 6; matrix products, arithmetic and copies ran while one was open for 1% -> 2% of each run, Pallas kernels for 9% -> 15%
where the time goes in v1:
time: 214 us; the launch traced here: 213 us
  blocking collectives  93.5 us (44%)
  Pallas kernels  63.6 us (30%)
  waiting for transfers between devices  22.3 us (10%)
  starting transfers between devices  22.2 us (10%)
  local copies, waits for them, and re-layouts  9.78 us (5%)
    all_to_all x1, blocking collectives, local(): lax.all_to_all(analysis.reshape(N_MEM, OWN, ROWS, LANES), 'mem', 0, 0, ti...  54.5 us
    pallas_call x1, Pallas kernels, local(): pl.pallas_call(interior_kernel, out_shape=[f32(GROUPS, ROWS - EDGE, OWN,...  22.4 us
    ppermute x6, waiting for transfers between devices, swap(): return lax.ppermute(x, axis, [(i, i ^ bit) for i in range(count)])  22.3 us
    all_to_all x1, blocking collectives, local(): lax.all_to_all(picked.reshape(N_MEM, OWN, HALF_OBS), 'mem', 0, 0, tiled=T...  19.8 us
    all_to_all x1, blocking collectives, local(): edge = lax.all_to_all(edge, 'mem', 0, 0, tiled=True)  19.2 us
    pallas_call x1, Pallas kernels, local(): pl.pallas_call(edge_kernel, out_shape=f32(GROUPS, EDGE, OWN, LANES), in_s...  11.3 us
    pallas_call x1, Pallas kernels, local(): pl.pallas_call(product_kernel, out_shape=f32(MEMBERS * ROWS, LANES), in_s...  9.04 us
    ppermute x2, starting transfers between devices, shift(): lax.ppermute(x, axis, [(i, (i + step) % count) for i in range(count)])  7.19 us
  transfers between devices with their start and end apart: 10, of which 6 were waited for; matrix products, arithmetic and copies ran while one was open for 2% of the time, Pallas kernels for 15%

profile of v1, /device:TPU:1, one launch (start us, length us, event | category | flops | bytes accessed | tf_op | source)
XLA Modules:
  0.0 213.3 jit_solution(1799354097372015096)
XLA Ops:
  1.6 1.8 fusion.1
  3.9 2.5 %collective-permute-start = (f32[4,40,1024]{2,1,0:T(8,128)S(1)}, f32[4,40,1024]{2,1,0:T(8,128)S(1)}, u32[]{:S(2)}, u32[]{:S(2)}) collective-permute-start(f32[4,40,1024]{2,1,0:T(8,128)S(1)} %pad.7), channel_id=1, source_target_pairs={{0,1},{1,2},{2,3},{3,4},{4,5},{5,6},{6,7},{7,8},{8,9},{9,10},{10,1... | collective-permute-start | bytes 1966088 | tf_op jit(solution)/shard_map/ppermute | solution.py:258
  6.9 4.7 %collective-permute-start.1 = (f32[4,40,1024]{2,1,0:T(8,128)S(1)}, f32[4,40,1024]{2,1,0:T(8,128)S(1)}, u32[]{:S(2)}, u32[]{:S(2)}) collective-permute-start(f32[4,40,1024]{2,1,0:T(8,128)S(1)} %pad.8), channel_id=1, source_target_pairs={{0,15},{1,0},{2,1},{3,2},{4,3},{5,4},{6,5},{7,6},{8,7},{9,8},{10,9... | collective-permute-start | bytes 1966088 | tf_op jit(solution)/shard_map/ppermute | solution.py:258
  12.2 5.3 %all-to-all-start = ((f32[8,3,256]{2,1,0:T(4,128)}), f32[8,3,256]{2,1,0:T(4,128)S(1)}, u32[]{:S(2)}, u32[]{:S(2)}) async-start(f32[8,3,256]{2,1,0:T(4,128)} %broadcast_in_dim.28), calls=%async_computation | async-start | bytes 65536 | tf_op jit(solution)/shard_map/all_to_all | solution.py:283
  17.5 22.4 %shard_map.64 = (f32[8,24,32,128]{3,2,1,0:T(8,128)}, f32[2,8,32,1024]{3,2,1,0:T(8,128)}) custom-call(f32[1024,1024]{1,0:T(8,128)} %bitcast.14, f32[32,1024]{1,0:T(8,128)} %h_ref.3, f32[32,1024]{1,0:T(8,128)} %v_ref.3), custom_call_target="tpu_custom_call" | custom-call | tf_op jit(solution)/shard_map/pallas_call | solution.py:292
  41.6 11.3 %shard_map.65.edge_ref = f32[8,8,32,128]{3,2,1,0:T(8,128)} custom-call(f32[2,8,32,1024]{3,2,1,0:T(8,128)} %get-tuple-element.15.rim_ref, f32[4,40,1024]{2,1,0:T(8,128)} %copy-done.2, f32[4,40,1024]{2,1,0:T(8,128)} %copy-done.3, f32[32,1024]{1,0:T(8,128)} %h_ref.3, f32[32,1024]{1,0:T(8,128)} %v_ref.3), custom_call_target="tpu_custom_call" | custom-call | tf_op jit(solution)/shard_map/pallas_call | solution.py:306
  52.9 5.3 %shard_map.66 = f32[2,32,1024]{2,1,0:T(8,128)} custom-call(f32[8,24,32,128]{3,2,1,0:T(8,128)} %get-tuple-element.21.inner_ref, f32[8,8,32,128]{3,2,1,0:T(8,128)} %shard_map.65.edge_ref, s32[8,256]{1,0:T(8,128)} %fusion.index_ref), custom_call_target="tpu_custom_call" | custom-call | tf_op jit(solution)/shard_map/pallas_call | solution.py:318
  58.2 1.1 broadcast_in_dim.29
  59.3 19.8 %all_to_all.25 = f32[8,32,1024]{2,1,0:T(8,128)} all-to-all(f32[8,32,1024]{2,1,0:T(8,128)S(1)} %bitcast.15), channel_id=1, replica_groups=mesh['mem'=8,'reg'=16] {'mem'}, dimensions={0} | all-to-all | bytes 2097152 | tf_op jit(solution)/shard_map/all_to_all | solution.py:327
  79.0 19.2 %all_to_all.26.edge_ref = f32[8,8,32,128]{3,2,1,0:T(8,128)} all-to-all(f32[8,8,32,128]{3,2,1,0:T(8,128)S(1)} %copy-done.1), channel_id=1, replica_groups=mesh['mem'=8,'reg'=16] {'mem'}, dimensions={0} | all-to-all | bytes 2097152 | tf_op jit(solution)/shard_map/all_to_all | solution.py:333
  98.2 4.6 %all-to-all-start.2 = ((f32[8,24,32,128]{3,2,1,0:T(8,128)}), f32[8,24,32,128]{3,2,1,0:T(8,128)S(1)}, u32[]{:S(2)}, u32[]{:S(2)}) async-start(f32[8,24,32,128]{3,2,1,0:T(8,128)} %get-tuple-element.21.inner_ref), calls=%async_computation.2 | async-start | bytes 6291456 | tf_op jit(solution)/shard_map/all_to_all | solution.py:332
  103.4 3.0 %shard_map.67 = (f32[136,256]{1,0:T(8,128)}, f32[136,256]{1,0:T(8,128)}) custom-call(s32[1]{0:T(128)} %bitcast.core_ref, f32[256,1024]{1,0:T(8,128)} %bitcast.16, f32[1,1024]{1,0:T(1,128)} %bitcast.18, f32[1,1024]{1,0:T(1,128)} %bitcast.17), custom_call_target="tpu_custom_call" | custom-call | tf_op jit(solution)/shard_map/pallas_call | solution.py:335
  106.5 1.5 collective-permute-done.2
  109.0 5.1 %collective-permute-done.3 = f32[136,256]{1,0:T(8,128)S(1)} collective-permute-done((f32[136,256]{1,0:T(8,128)S(1)}, f32[136,256]{1,0:T(8,128)S(1)}, u32[]{:S(2)}, u32[]{:S(2)}) %collective-permute-start.3) | collective-permute-done | bytes 139296 | tf_op jit(solution)/shard_map/ppermute | solution.py:253
  114.3 5.7 %collective-permute-done.4 = f32[136,256]{1,0:T(8,128)S(1)} collective-permute-done((f32[136,256]{1,0:T(8,128)S(1)}, f32[136,256]{1,0:T(8,128)S(1)}, u32[]{:S(2)}, u32[]{:S(2)}) %collective-permute-start.4) | collective-permute-done | bytes 139296 | tf_op jit(solution)/shard_map/ppermute | solution.py:253
  120.1 4.2 %collective-permute-done.5 = f32[136,256]{1,0:T(8,128)S(1)} collective-permute-done((f32[136,256]{1,0:T(8,128)S(1)}, f32[136,256]{1,0:T(8,128)S(1)}, u32[]{:S(2)}, u32[]{:S(2)}) %collective-permute-start.5) | collective-permute-done | bytes 139296 | tf_op jit(solution)/shard_map/ppermute | solution.py:253
  124.9 4.9 %collective-permute-done.6 = f32[136,256]{1,0:T(8,128)S(1)} collective-permute-done((f32[136,256]{1,0:T(8,128)S(1)}, f32[136,256]{1,0:T(8,128)S(1)}, u32[]{:S(2)}, u32[]{:S(2)}) %collective-permute-start.6) | collective-permute-done | bytes 139296 | tf_op jit(solution)/shard_map/ppermute | solution.py:253
  129.8 4.1 %collective-permute-start.7 = (f32[136,256]{1,0:T(8,128)S(1)}, f32[136,256]{1,0:T(8,128)S(1)}, u32[]{:S(2)}, u32[]{:S(2)}) collective-permute-start(f32[136,256]{1,0:T(8,128)S(1)} %add.32.mine_ref), channel_id=1, source_target_pairs={{0,16},{16,0},{32,48},{48,32},{64,80},{80,64},{96,112},{112,96},{1... | collective-permute-start | bytes 417800 | tf_op jit(solution)/shard_map/ppermute | solution.py:253
  133.9 1.0 collective-permute-done.7.other_ref
  135.6 5.9 %shard_map.68 = (bf16[256,256]{1,0:T(8,128)(2,1)}, bf16[256,256]{1,0:T(8,128)(2,1)}) custom-call(s32[1]{0:T(128)} %bitcast.core_ref, f32[136,256]{1,0:T(8,128)} %copy-done.4, f32[136,256]{1,0:T(8,128)} %copy-done.5), custom_call_target="tpu_custom_call" | custom-call | tf_op jit(solution)/shard_map/pallas_call | solution.py:348
  141.6 1.6 copy-done
  143.2 9.0 %shard_map.69 = f32[8192,128]{1,0:T(8,128)} custom-call(bf16[256,256]{1,0:T(8,128)(2,1)} %get-tuple-element.19.high_ref, bf16[256,256]{1,0:T(8,128)(2,1)} %get-tuple-element.20.low_ref, f32[8,24,32,128]{3,2,1,0:T(8,128)} %copy-done, f32[8,8,32,128]{3,2,1,0:T(8,128)} %all_to_all.26.edge_ref), custom_call_target="tpu_custom_call" | custom-call | tf_op jit(solution)/shard_map/pallas_call | solution.py:357
  152.2 54.5 %all_to_all.27.x_ref = f32[8,32,32,128]{3,2,1,0:T(8,128)} all-to-all(f32[8,32,32,128]{3,2,1,0:T(8,128)} %bitcast.13), channel_id=1, replica_groups=mesh['mem'=8,'reg'=16] {'mem'}, dimensions={0} | all-to-all | bytes 8388608 | tf_op jit(solution)/shard_map/all_to_all | solution.py:364
  206.8 6.6 %shard_map.70 = f32[32,32,1024]{2,1,0:T(8,128)} custom-call(f32[8,32,32,128]{3,2,1,0:T(8,128)} %all_to_all.27.x_ref), custom_call_target="tpu_custom_call" | custom-call | tf_op jit(solution)/shard_map/pallas_call | solution.py:367
  (49 shorter events, 8.1 us)
Async XLA Ops:
  1.6 10.0 %copy-start.8 = (s32[1,256]{1,0:T(1,128)S(1)}, s32[1,256]{1,0:T(1,128)}, u32[]{:S(2)}) copy-start(s32[1,256]{1,0:T(1,128)} %param.9) | copy-start | bytes 3076
  1.6 10.0 %copy-start.6 = (f32[1,256]{1,0:T(1,128)S(1)}, f32[1,256]{1,0:T(1,128)}, u32[]{:S(2)}) copy-start(f32[1,256]{1,0:T(1,128)} %param.11) | copy-start | bytes 3076
  1.6 10.0 %copy-start.7 = (f32[1,256]{1,0:T(1,128)S(1)}, f32[1,256]{1,0:T(1,128)}, u32[]{:S(2)}) copy-start(f32[1,256]{1,0:T(1,128)} %param.10) | copy-start | bytes 3076
  3.9 36.6 %collective-permute-start = (f32[4,40,1024]{2,1,0:T(8,128)S(1)}, f32[4,40,1024]{2,1,0:T(8,128)S(1)}, u32[]{:S(2)}, u32[]{:S(2)}) collective-permute-start(f32[4,40,1024]{2,1,0:T(8,128)S(1)} %pad.7), channel_id=1, source_target_pairs={{0,1},{1,2},{2,3},{3,4},{4,5},{5,6},{6,7},{7,8},{8,9},{9,10},{10,1... | collective-permute-start | bytes 1966088 | tf_op jit(solution)/shard_map/ppermute | solution.py:258
  6.9 33.6 %collective-permute-start.1 = (f32[4,40,1024]{2,1,0:T(8,128)S(1)}, f32[4,40,1024]{2,1,0:T(8,128)S(1)}, u32[]{:S(2)}, u32[]{:S(2)}) collective-permute-start(f32[4,40,1024]{2,1,0:T(8,128)S(1)} %pad.8), channel_id=1, source_target_pairs={{0,15},{1,0},{2,1},{3,2},{4,3},{5,4},{6,5},{7,6},{8,7},{9,8},{10,9... | collective-permute-start | bytes 1966088 | tf_op jit(solution)/shard_map/ppermute | solution.py:258
  12.2 27.7 %all-to-all-start = ((f32[8,3,256]{2,1,0:T(4,128)}), f32[8,3,256]{2,1,0:T(4,128)S(1)}, u32[]{:S(2)}, u32[]{:S(2)}) async-start(f32[8,3,256]{2,1,0:T(4,128)} %broadcast_in_dim.28), calls=%async_computation | async-start | bytes 65536 | tf_op jit(solution)/shard_map/all_to_all | solution.py:283
  40.5 0.8 copy-start.2
  40.5 1.1 copy-start.3
  52.9 26.1 %copy-start.1 = (f32[8,8,32,128]{3,2,1,0:T(8,128)S(1)}, f32[8,8,32,128]{3,2,1,0:T(8,128)}, u32[]{:S(2)}) copy-start(f32[8,8,32,128]{3,2,1,0:T(8,128)} %shard_map.65.edge_ref) | copy-start | bytes 3145732
  98.2 43.3 %all-to-all-start.2 = ((f32[8,24,32,128]{3,2,1,0:T(8,128)}), f32[8,24,32,128]{3,2,1,0:T(8,128)S(1)}, u32[]{:S(2)}, u32[]{:S(2)}) async-start(f32[8,24,32,128]{3,2,1,0:T(8,128)} %get-tuple-element.21.inner_ref), calls=%async_computation.2 | async-start | bytes 6291456 | tf_op jit(solution)/shard_map/all_to_all | solution.py:332
  106.4 1.6 collective-permute-start.2
  108.9 5.2 %collective-permute-start.3 = (f32[136,256]{1,0:T(8,128)S(1)}, f32[136,256]{1,0:T(8,128)S(1)}, u32[]{:S(2)}, u32[]{:S(2)}) collective-permute-start(f32[136,256]{1,0:T(8,128)S(1)} %add.28), channel_id=1, source_target_pairs={{0,1},{1,0},{2,3},{3,2},{4,5},{5,4},{6,7},{7,6},{8,9},{9,8},{10,11... | collective-permute-start | bytes 417800 | tf_op jit(solution)/shard_map/ppermute | solution.py:253
  114.2 5.8 %collective-permute-start.4 = (f32[136,256]{1,0:T(8,128)S(1)}, f32[136,256]{1,0:T(8,128)S(1)}, u32[]{:S(2)}, u32[]{:S(2)}) collective-permute-start(f32[136,256]{1,0:T(8,128)S(1)} %add.29), channel_id=1, source_target_pairs={{0,2},{1,3},{2,0},{3,1},{4,6},{5,7},{6,4},{7,5},{8,10},{9,11},{10,... | collective-permute-start | bytes 417800 | tf_op jit(solution)/shard_map/ppermute | solution.py:253
  120.0 4.3 %collective-permute-start.5 = (f32[136,256]{1,0:T(8,128)S(1)}, f32[136,256]{1,0:T(8,128)S(1)}, u32[]{:S(2)}, u32[]{:S(2)}) collective-permute-start(f32[136,256]{1,0:T(8,128)S(1)} %add.30), channel_id=1, source_target_pairs={{0,4},{1,5},{2,6},{3,7},{4,0},{5,1},{6,2},{7,3},{8,12},{9,13},{10,... | collective-permute-start | bytes 417800 | tf_op jit(solution)/shard_map/ppermute | solution.py:253
  124.3 5.5 %collective-permute-start.6 = (f32[136,256]{1,0:T(8,128)S(1)}, f32[136,256]{1,0:T(8,128)S(1)}, u32[]{:S(2)}, u32[]{:S(2)}) collective-permute-start(f32[136,256]{1,0:T(8,128)S(1)} %add.31), channel_id=1, source_target_pairs={{0,8},{1,9},{2,10},{3,11},{4,12},{5,13},{6,14},{7,15},{8,0},{9,1},... | collective-permute-start | bytes 417800 | tf_op jit(solution)/shard_map/ppermute | solution.py:253
  129.8 5.1 %copy-start.4 = (f32[136,256]{1,0:T(8,128)}, f32[136,256]{1,0:T(8,128)S(1)}, u32[]{:S(2)}) copy-start(f32[136,256]{1,0:T(8,128)S(1)} %add.32.mine_ref) | copy-start | bytes 417796
  129.8 5.1 %collective-permute-start.7 = (f32[136,256]{1,0:T(8,128)S(1)}, f32[136,256]{1,0:T(8,128)S(1)}, u32[]{:S(2)}, u32[]{:S(2)}) collective-permute-start(f32[136,256]{1,0:T(8,128)S(1)} %add.32.mine_ref), channel_id=1, source_target_pairs={{0,16},{16,0},{32,48},{48,32},{64,80},{80,64},{96,112},{112,96},{1... | collective-permute-start | bytes 417800 | tf_op jit(solution)/shard_map/ppermute | solution.py:253
  134.9 0.7 copy-start.5
  141.5 1.6 copy-start

commit v2 on v1

--- a/solution.py
+++ b/solution.py
@@ -21,6 +21,7 @@
 HALF_OBS = OBS * GROUPS // 2
 HALO = SECTIONS
 EDGE = 2 * HALO
+CHUNK = 8
 VMEM = pl.BlockSpec(memory_space=pltpu.VMEM)
 SMEM = pl.BlockSpec(memory_space=pltpu.SMEM)
 PARAMS = pltpu.CompilerParams(vmem_limit_bytes=56 * 1024 * 1024)
@@ -96,7 +97,9 @@
         lax.fori_loop(first + s, last - s, body, 0)
 
 
-def interior_kernel(prior_ref, h_ref, v_ref, out_ref, rim_ref, given, one, two, coef_ref, sems):
+def interior_kernel(
+    prior_ref, h_ref, v_ref, out_ref, early_ref, rim_ref, given, one, two, coef_ref, sems
+):
     copies = [
         pltpu.make_async_copy(
             prior_ref.at[:, j * LANES : (j + 1) * LANES], given.at[j], sems.at[j]
@@ -118,9 +121,15 @@
             if i >= ROWS - EDGE:
                 rim_ref[1, i - ROWS + EDGE, :, at] = x
     sections((one, two), coef_ref, 0, ROWS, out_ref, -HALO)
-
-
-def edge_kernel(rim_ref, low_ref, high_ref, h_ref, v_ref, out_ref, one, two, coef_ref):
+    early_ref[...] = out_ref[:, CHUNK - HALO : 2 * CHUNK - HALO]
+
+
+def edge_kernel(
+    inner_ref, rim_ref, low_ref, high_ref, h_ref, v_ref, index_ref,
+    obs_ref, rest_ref, field, one, two, coef_ref, in_sem, out_sems,
+):
+    load = pltpu.make_async_copy(inner_ref, field.at[:, HALO : ROWS - HALO], in_sem)
+    load.start()
     for side, (halo_ref, halo_at, own_at, own_first) in enumerate(
         ((low_ref, 0, HALO, 0), (high_ref, EDGE, 0, ROWS - EDGE))
     ):
@@ -137,10 +146,19 @@
                 coef_ref,
                 own_at + i,
             )
-        sections((one, two), coef_ref, 0, HALO + EDGE, out_ref, -HALO + side * HALO)
-
-
-def pick_kernel(inner_ref, edge_ref, index_ref, out_ref):
+        at = -HALO if side == 0 else ROWS - EDGE
+        sections((one, two), coef_ref, 0, HALO + EDGE, field, at)
+    load.wait()
+    stores = [
+        pltpu.make_async_copy(
+            field.at[:, first : first + count], rest_ref.at[:, to : to + count], out_sems.at[n]
+        )
+        for n, (first, count, to) in enumerate(
+            ((0, CHUNK, 0), (2 * CHUNK, ROWS - 2 * CHUNK, CHUNK))
+        )
+    ]
+    for store in stores:
+        store.start()
     for g in range(GROUPS):
         for t in range(OBS // LANES):
             place = index_ref[g : g + 1, t * LANES : (t + 1) * LANES]
@@ -148,16 +166,13 @@
             col = jnp.broadcast_to(place & (LANES - 1), (OWN, LANES))
             total = jnp.zeros((OWN, LANES), jnp.float32)
             for i in range(ROWS):
-                if i < HALO:
-                    x = edge_ref[g, i]
-                elif i < ROWS - HALO:
-                    x = inner_ref[g, i - HALO]
-                else:
-                    x = edge_ref[g, i - ROWS + EDGE]
-                x = jnp.take_along_axis(x, col, axis=1, mode="promise_in_bounds")
+                x = jnp.take_along_axis(field[g, i], col, axis=1, mode="promise_in_bounds")
                 total = jnp.where(row == i, x, total)
             at = (g % 4) * OBS + t * LANES
-            out_ref[g // 4, :, at : at + LANES] = total
+            for x in range(N_MEM // 2):
+                obs_ref[2 * x + g // 4, :, at : at + LANES] = total
+    for store in stores:
+        store.wait()
 
 
 def gram_kernel(core_ref, obs_ref, value_ref, weight_ref, keep_ref, send_ref):
@@ -217,27 +232,26 @@
     low_ref[...] = low
 
 
-def product_kernel(high_ref, low_ref, inner_ref, edge_ref, out_ref):
+def product_kernel(high_ref, low_ref, early_ref, rest_ref, out_ref):
     weights = (high_ref[...], low_ref[...])
-
-    def rows(ref, i, r):
-        parts = [
-            split(jnp.concatenate([ref[s, i + t] for s in range(N_MEM)], axis=0))
-            for t in range(HALO)
-        ]
-        x = tuple(jnp.concatenate([p[n] for p in parts], axis=1) for n in range(2))
-        y = dot3(weights, x)
-        for t in range(HALO):
-            out_ref[pl.ds(r + t, MEMBERS, stride=ROWS), :] = y[:, t * LANES : (t + 1) * LANES]
-
-    rows(edge_ref, 0, 0)
-    rows(edge_ref, HALO, ROWS - HALO)
-
-    def body(n, carry):
-        rows(inner_ref, HALO * n, HALO + HALO * n)
-        return carry
-
-    lax.fori_loop(0, (ROWS - EDGE) // HALO, body, 0)
+    flat = out_ref.reshape(MEMBERS * CHUNK, LANES)
+
+    def rows(ref):
+        for half in range(0, CHUNK, HALO):
+            parts = [
+                split(jnp.concatenate([ref[s, half + t] for s in range(N_MEM)], axis=0))
+                for t in range(HALO)
+            ]
+            x = tuple(jnp.concatenate([p[n] for p in parts], axis=1) for n in range(2))
+            y = dot3(weights, x)
+            for t in range(HALO):
+                flat[pl.ds(half + t, MEMBERS, stride=CHUNK), :] = y[
+                    :, t * LANES : (t + 1) * LANES
+                ]
+
+    step = pl.program_id(0)
+    pl.when(step == 1)(lambda: rows(early_ref))
+    pl.when(step != 1)(lambda: rows(rest_ref))
 
 
 def place_kernel(x_ref, out_ref):
@@ -289,11 +303,16 @@
     weight = half_facts[:, 2].reshape(1, HALF_OBS)
 
     flat = prior_samples.reshape(OWN * ROWS, WIDTH)
-    inner, rim = pl.pallas_call(
+    anywhere = pl.BlockSpec(memory_space=pl.ANY)
+    inner, early, rim = pl.pallas_call(
         interior_kernel,
-        out_shape=[f32(GROUPS, ROWS - EDGE, OWN, LANES), f32(2, EDGE, OWN, WIDTH)],
-        in_specs=[pl.BlockSpec(memory_space=pl.ANY), VMEM, VMEM],
-        out_specs=[VMEM, VMEM],
+        out_shape=[
+            f32(GROUPS, ROWS - EDGE, OWN, LANES),
+            f32(GROUPS, CHUNK, OWN, LANES),
+            f32(2, EDGE, OWN, WIDTH),
+        ],
+        in_specs=[anywhere, VMEM, VMEM],
+        out_specs=[VMEM, VMEM, VMEM],
         scratch_shapes=[
             pltpu.VMEM((GROUPS, OWN * ROWS, LANES), jnp.float32),
             pltpu.VMEM((ROWS, OWN, WIDTH), jnp.float32),
@@ -303,34 +322,26 @@
         ],
         compiler_params=PARAMS,
     )(flat, h, v)
-    edge = pl.pallas_call(
+    early = lax.all_to_all(early, "mem", 0, 0, tiled=True)
+    obs, rest = pl.pallas_call(
         edge_kernel,
-        out_shape=f32(GROUPS, EDGE, OWN, LANES),
-        in_specs=[VMEM] * 5,
-        out_specs=VMEM,
+        out_shape=[
+            f32(N_MEM, OWN, HALF_OBS),
+            f32(GROUPS, ROWS - CHUNK, OWN, LANES),
+        ],
+        in_specs=[anywhere] + [VMEM] * 6,
+        out_specs=[VMEM, anywhere],
         scratch_shapes=[
+            pltpu.VMEM((GROUPS, ROWS, OWN, LANES), jnp.float32),
             pltpu.VMEM((HALO + EDGE, OWN, WIDTH), jnp.float32),
             pltpu.VMEM((HALO + EDGE, OWN, WIDTH), jnp.float32),
             pltpu.VMEM((2, HALO + EDGE, 8, WIDTH), jnp.float32),
+            pltpu.SemaphoreType.DMA,
+            pltpu.SemaphoreType.DMA((2,)),
         ],
         compiler_params=PARAMS,
-    )(rim, low, high, h, v)
-    picked = pl.pallas_call(
-        pick_kernel,
-        out_shape=f32(2, OWN, HALF_OBS),
-        in_specs=[VMEM] * 3,
-        out_specs=VMEM,
-        compiler_params=PARAMS,
-    )(inner, edge, index)
-
-    picked = jnp.broadcast_to(picked[None], (N_MEM // 2, 2, OWN, HALF_OBS))
-    obs = lax.all_to_all(
-        picked.reshape(N_MEM, OWN, HALF_OBS), "mem", 0, 0, tiled=True
-    ).reshape(MEMBERS, HALF_OBS)
-
-    inner, edge, obs = lax.optimization_barrier((inner, edge, obs))
-    inner = lax.all_to_all(inner, "mem", 0, 0, tiled=True)
-    edge = lax.all_to_all(edge, "mem", 0, 0, tiled=True)
+    )(inner, rim, low, high, h, v, index)
+    obs = lax.all_to_all(obs, "mem", 0, 0, tiled=True).reshape(MEMBERS, HALF_OBS)
 
     keep, send = pl.pallas_call(
         gram_kernel,
@@ -339,6 +350,8 @@
         out_specs=[VMEM, VMEM],
         compiler_params=PARAMS,
     )(core, obs, value, weight)
+    rest, send = lax.optimization_barrier((rest, send))
+    rest = lax.all_to_all(rest, "mem", 0, 0, tiled=True)
     total = keep + swap(send, "mem", 1)
     for bit in (1, 2, 4, 8):
         total = total + swap(total, "reg", bit)
@@ -354,16 +367,22 @@
         compiler_params=PARAMS,
     )(core, total, other)
 
+    whole = pl.BlockSpec((MEMBERS, MEMBERS), lambda n: (0, 0))
+    block = (N_MEM, CHUNK, OWN, LANES)
     analysis = pl.pallas_call(
         product_kernel,
-        out_shape=f32(MEMBERS * ROWS, LANES),
-        in_specs=[VMEM] * 4,
-        out_specs=VMEM,
-        compiler_params=PARAMS,
-    )(*weights, inner, edge)
-    analysis = lax.all_to_all(
-        analysis.reshape(N_MEM, OWN, ROWS, LANES), "mem", 0, 0, tiled=True
-    )
+        grid=(ROWS // CHUNK,),
+        out_shape=f32(N_MEM, OWN, ROWS, LANES),
+        in_specs=[
+            whole,
+            whole,
+            pl.BlockSpec(block, lambda n: (0, 0, 0, 0)),
+            pl.BlockSpec(block, lambda n: (0, jnp.maximum(n - 1, 0), 0, 0)),
+        ],
+        out_specs=pl.BlockSpec((N_MEM, OWN, CHUNK, LANES), lambda n: (0, 0, n, 0)),
+        compiler_params=PARAMS,
+    )(*weights, early, rest)
+    analysis = lax.all_to_all(analysis, "mem", 0, 0, tiled=True)
     return pl.pallas_call(
         place_kernel,
         grid=(GROUPS,),

time: 214 us -> 208 us (0.972)
  blocking collectives: 93.5 us -> 74.6 us
  waiting for transfers between devices: 22.3 us -> 36.8 us
  Pallas kernels: 63.6 us -> 58.5 us
  starting transfers between devices: 22.2 us -> 26.7 us
    all_to_all x3 -> x2, blocking collectives: 93.5 us -> 74.6 us  [the longest x1 54.6 us: local(): analysis = lax.all_to_all(analysis, 'mem', 0, 0, tiled=True)]
    all_to_all x1 -> x2, waiting for transfers between devices: 0.01 us -> 14.8 us  [the longest x1 11.5 us: local(): early = lax.all_to_all(early, 'mem', 0, 0, tiled=True)]
    pallas_call x3 -> x2, Pallas kernels: 25.7 us -> 19.9 us  [the longest x1 13.6 us: local(): pl.pallas_call(edge_kernel, out_shape=[f32(N_MEM, OWN, HALF_OBS), f32(GRO...]
    all_to_all x1 -> x2, starting transfers between devices: 4.59 us -> 8.92 us  [the longest x1 4.5 us: local(): early = lax.all_to_all(early, 'mem', 0, 0, tiled=True)]
    unnamed x20 -> x24, local copies, waits for them, and re-layouts: 3.99 us -> 5.07 us
  transfers between devices with their start and end apart: 10 -> 11, of which waited for: 6 -> 8; matrix products, arithmetic and copies ran while one was open for 2% -> 1% of each run, Pallas kernels for 15% -> 15%
where the time goes in v2:
time: 208 us
  blocking collectives  74.6 us (36%)
  Pallas kernels  58.5 us (28%)
  waiting for transfers between devices  36.8 us (18%)
  starting transfers between devices  26.7 us (13%)
  local copies, waits for them, and re-layouts  9.81 us (5%)
    all_to_all x1, blocking collectives, local(): analysis = lax.all_to_all(analysis, 'mem', 0, 0, tiled=True)  54.6 us
    pallas_call x1, Pallas kernels, local(): pl.pallas_call(interior_kernel, out_shape=[f32(GROUPS, ROWS - EDGE, OWN,...  22.9 us
    ppermute x6, waiting for transfers between devices, swap(): return lax.ppermute(x, axis, [(i, i ^ bit) for i in range(count)])  21.9 us
    all_to_all x1, blocking collectives, local(): lax.all_to_all(obs, 'mem', 0, 0, tiled=True).reshape(MEMBERS, HALF_OBS)  20 us
    pallas_call x1, Pallas kernels, local(): pl.pallas_call(edge_kernel, out_shape=[f32(N_MEM, OWN, HALF_OBS), f32(GRO...  13.6 us
    all_to_all x1, waiting for transfers between devices, local(): early = lax.all_to_all(early, 'mem', 0, 0, tiled=True)  11.5 us
    ppermute x2, starting transfers between devices, shift(): lax.ppermute(x, axis, [(i, (i + step) % count) for i in range(count)])  7.19 us
    pallas_call x1, Pallas kernels, local(): pl.pallas_call(place_kernel, grid=(GROUPS,), out_shape=f32(OWN, ROWS, WID...  6.58 us
  transfers between devices with their start and end apart: 11, of which 8 were waited for; matrix products, arithmetic and copies ran while one was open for 1% of the time, Pallas kernels for 15%

profile of v2, /device:TPU:1, one launch (start us, length us, event | category | flops | bytes accessed | tf_op | source)
XLA Modules:
  0.0 207.5 jit_solution(2576356567759126202)
XLA Ops:
  1.6 1.8 fusion.1
  3.9 2.5 %collective-permute-start = (f32[4,40,1024]{2,1,0:T(8,128)S(1)}, f32[4,40,1024]{2,1,0:T(8,128)S(1)}, u32[]{:S(2)}, u32[]{:S(2)}) collective-permute-start(f32[4,40,1024]{2,1,0:T(8,128)S(1)} %pad.7), channel_id=1, source_target_pairs={{0,1},{1,2},{2,3},{3,4},{4,5},{5,6},{6,7},{7,8},{8,9},{9,10},{10,1... | collective-permute-start | bytes 1966088 | tf_op jit(solution)/shard_map/ppermute | solution.py:272
  6.9 4.7 %collective-permute-start.1 = (f32[4,40,1024]{2,1,0:T(8,128)S(1)}, f32[4,40,1024]{2,1,0:T(8,128)S(1)}, u32[]{:S(2)}, u32[]{:S(2)}) collective-permute-start(f32[4,40,1024]{2,1,0:T(8,128)S(1)} %pad.8), channel_id=1, source_target_pairs={{0,15},{1,0},{2,1},{3,2},{4,3},{5,4},{6,5},{7,6},{8,7},{9,8},{10,9... | collective-permute-start | bytes 1966088 | tf_op jit(solution)/shard_map/ppermute | solution.py:272
  12.2 5.3 %all-to-all-start = ((f32[8,3,256]{2,1,0:T(4,128)}), f32[8,3,256]{2,1,0:T(4,128)S(1)}, u32[]{:S(2)}, u32[]{:S(2)}) async-start(f32[8,3,256]{2,1,0:T(4,128)} %broadcast_in_dim.22), calls=%async_computation | async-start | bytes 65536 | tf_op jit(solution)/shard_map/all_to_all | solution.py:297
  17.5 22.9 %shard_map.64 = (f32[8,24,32,128]{3,2,1,0:T(8,128)}, f32[8,8,32,128]{3,2,1,0:T(8,128)}, f32[2,8,32,1024]{3,2,1,0:T(8,128)}) custom-call(f32[1024,1024]{1,0:T(8,128)} %bitcast.11, f32[32,1024]{1,0:T(8,128)} %h_ref.3, f32[32,1024]{1,0:T(8,128)} %v_ref.3), custom_call_target="tpu_custom_call" | custom-call | tf_op jit(solution)/shard_map/pallas_call | solution.py:307
  42.2 13.6 %shard_map.65 = (f32[8,32,1024]{2,1,0:T(8,128)}, f32[8,24,32,128]{3,2,1,0:T(8,128)}) custom-call(f32[8,24,32,128]{3,2,1,0:T(8,128)} %get-tuple-element.16.inner_ref, f32[2,8,32,1024]{3,2,1,0:T(8,128)} %get-tuple-element.17.rim_ref, f32[4,40,1024]{2,1,0:T(8,128)} %copy-done.2, f32[4,40,1024]{2,1,0:T(8,128)} %copy-done.3, f32[32,1024]{1,0:T(8,128)} %h_ref.3, ...), custom_call_target="tpu_custom_call" | custom-call | tf_op jit(solution)/shard_map/pallas_call | solution.py:326
  55.8 20.0 %all_to_all.25 = f32[8,32,1024]{2,1,0:T(8,128)} all-to-all(f32[8,32,1024]{2,1,0:T(8,128)} %get-tuple-element.18), channel_id=1, replica_groups=mesh['mem'=8,'reg'=16] {'mem'}, dimensions={0} | all-to-all | bytes 2097152 | tf_op jit(solution)/shard_map/all_to_all | solution.py:344
  75.8 4.5 %all-to-all-start.2 = ((f32[8,8,32,128]{3,2,1,0:T(8,128)}), f32[8,8,32,128]{3,2,1,0:T(8,128)S(1)}, u32[]{:S(2)}, u32[]{:S(2)}) async-start(f32[8,8,32,128]{3,2,1,0:T(8,128)} %get-tuple-element.25), calls=%async_computation.2 | async-start | bytes 2097152 | tf_op jit(solution)/shard_map/all_to_all | solution.py:325
  80.9 3.0 %shard_map.66 = (f32[136,256]{1,0:T(8,128)}, f32[136,256]{1,0:T(8,128)}) custom-call(s32[1]{0:T(128)} %bitcast.core_ref, f32[256,1024]{1,0:T(8,128)} %bitcast.12, f32[1,1024]{1,0:T(1,128)} %bitcast.14, f32[1,1024]{1,0:T(1,128)} %bitcast.13), custom_call_target="tpu_custom_call" | custom-call | tf_op jit(solution)/shard_map/pallas_call | solution.py:346
  83.9 11.5 %all-to-all-done.2.early_ref = f32[8,8,32,128]{3,2,1,0:T(8,128)S(1)} async-done(((f32[8,8,32,128]{3,2,1,0:T(8,128)}), f32[8,8,32,128]{3,2,1,0:T(8,128)S(1)}, u32[]{:S(2)}, u32[]{:S(2)}) %all-to-all-start.2) | async-done | bytes 1048608 | tf_op jit(solution)/shard_map/all_to_all | solution.py:325
  96.4 4.4 %all-to-all-start.3 = ((f32[8,24,32,128]{3,2,1,0:T(8,128)}), f32[8,24,32,128]{3,2,1,0:T(8,128)S(1)}, u32[]{:S(2)}, u32[]{:S(2)}) async-start(f32[8,24,32,128]{3,2,1,0:T(8,128)} %get-tuple-element.26), calls=%async_computation.3 | async-start | bytes 6291456 | tf_op jit(solution)/shard_map/all_to_all | solution.py:354
  101.0 1.3 collective-permute-done.2
  102.5 4.9 %collective-permute-done.3 = f32[136,256]{1,0:T(8,128)S(1)} collective-permute-done((f32[136,256]{1,0:T(8,128)S(1)}, f32[136,256]{1,0:T(8,128)S(1)}, u32[]{:S(2)}, u32[]{:S(2)}) %collective-permute-start.3) | collective-permute-done | bytes 139296 | tf_op jit(solution)/shard_map/ppermute | solution.py:267
  107.5 5.7 %collective-permute-done.4 = f32[136,256]{1,0:T(8,128)S(1)} collective-permute-done((f32[136,256]{1,0:T(8,128)S(1)}, f32[136,256]{1,0:T(8,128)S(1)}, u32[]{:S(2)}, u32[]{:S(2)}) %collective-permute-start.4) | collective-permute-done | bytes 139296 | tf_op jit(solution)/shard_map/ppermute | solution.py:267
  113.2 4.2 %collective-permute-done.5 = f32[136,256]{1,0:T(8,128)S(1)} collective-permute-done((f32[136,256]{1,0:T(8,128)S(1)}, f32[136,256]{1,0:T(8,128)S(1)}, u32[]{:S(2)}, u32[]{:S(2)}) %collective-permute-start.5) | collective-permute-done | bytes 139296 | tf_op jit(solution)/shard_map/ppermute | solution.py:267
  118.1 4.9 %collective-permute-done.6 = f32[136,256]{1,0:T(8,128)S(1)} collective-permute-done((f32[136,256]{1,0:T(8,128)S(1)}, f32[136,256]{1,0:T(8,128)S(1)}, u32[]{:S(2)}, u32[]{:S(2)}) %collective-permute-start.6) | collective-permute-done | bytes 139296 | tf_op jit(solution)/shard_map/ppermute | solution.py:267
  123.0 4.3 %collective-permute-start.7 = (f32[136,256]{1,0:T(8,128)S(1)}, f32[136,256]{1,0:T(8,128)S(1)}, u32[]{:S(2)}, u32[]{:S(2)}) collective-permute-start(f32[136,256]{1,0:T(8,128)S(1)} %add.32.mine_ref), channel_id=1, source_target_pairs={{0,16},{16,0},{32,48},{48,32},{64,80},{80,64},{96,112},{112,96},{1... | collective-permute-start | bytes 417800 | tf_op jit(solution)/shard_map/ppermute | solution.py:267
  127.3 1.0 collective-permute-done.7.other_ref
  128.9 6.1 %shard_map.67 = (bf16[256,256]{1,0:T(8,128)(2,1)}, bf16[256,256]{1,0:T(8,128)(2,1)}) custom-call(s32[1]{0:T(128)} %bitcast.core_ref, f32[136,256]{1,0:T(8,128)} %copy-done.4, f32[136,256]{1,0:T(8,128)} %copy-done.6), custom_call_target="tpu_custom_call" | custom-call | tf_op jit(solution)/shard_map/pallas_call | solution.py:361
  135.1 3.3 %all-to-all-done.3.rest_ref = f32[8,24,32,128]{3,2,1,0:T(8,128)S(1)} async-done(((f32[8,24,32,128]{3,2,1,0:T(8,128)}), f32[8,24,32,128]{3,2,1,0:T(8,128)S(1)}, u32[]{:S(2)}, u32[]{:S(2)}) %all-to-all-start.3) | async-done | bytes 3145760 | tf_op jit(solution)/shard_map/all_to_all | solution.py:354
  138.4 1.6 copy-done
  140.0 6.3 %shard_map.68 = f32[8,32,32,128]{3,2,1,0:T(8,128)} custom-call(bf16[256,256]{1,0:T(8,128)(2,1)} %get-tuple-element.23.high_ref, bf16[256,256]{1,0:T(8,128)(2,1)} %get-tuple-element.24.low_ref, f32[8,8,32,128]{3,2,1,0:T(8,128)} %copy-done.1, f32[8,24,32,128]{3,2,1,0:T(8,128)} %copy-done), custom_call_target="tpu_custom_call" | custom-call | tf_op jit(solution)/shard_map/pallas_call | solution.py:372
  146.3 54.6 %all_to_all.26.x_ref = f32[8,32,32,128]{3,2,1,0:T(8,128)} all-to-all(f32[8,32,32,128]{3,2,1,0:T(8,128)} %shard_map.68), channel_id=1, replica_groups=mesh['mem'=8,'reg'=16] {'mem'}, dimensions={0} | all-to-all | bytes 8388608 | tf_op jit(solution)/shard_map/all_to_all | solution.py:385
  201.0 6.6 %shard_map.69 = f32[32,32,1024]{2,1,0:T(8,128)} custom-call(f32[8,32,32,128]{3,2,1,0:T(8,128)} %all_to_all.26.x_ref), custom_call_target="tpu_custom_call" | custom-call | tf_op jit(solution)/shard_map/pallas_call | solution.py:386
  (52 shorter events, 8.3 us)
Async XLA Ops:
  1.6 10.0 %copy-start.9 = (s32[1,256]{1,0:T(1,128)S(1)}, s32[1,256]{1,0:T(1,128)}, u32[]{:S(2)}) copy-start(s32[1,256]{1,0:T(1,128)} %param.9) | copy-start | bytes 3076
  1.6 10.0 %copy-start.7 = (f32[1,256]{1,0:T(1,128)S(1)}, f32[1,256]{1,0:T(1,128)}, u32[]{:S(2)}) copy-start(f32[1,256]{1,0:T(1,128)} %param.11) | copy-start | bytes 3076
  1.6 10.0 %copy-start.8 = (f32[1,256]{1,0:T(1,128)S(1)}, f32[1,256]{1,0:T(1,128)}, u32[]{:S(2)}) copy-start(f32[1,256]{1,0:T(1,128)} %param.10) | copy-start | bytes 3076
  3.9 37.1 %collective-permute-start = (f32[4,40,1024]{2,1,0:T(8,128)S(1)}, f32[4,40,1024]{2,1,0:T(8,128)S(1)}, u32[]{:S(2)}, u32[]{:S(2)}) collective-permute-start(f32[4,40,1024]{2,1,0:T(8,128)S(1)} %pad.7), channel_id=1, source_target_pairs={{0,1},{1,2},{2,3},{3,4},{4,5},{5,6},{6,7},{7,8},{8,9},{9,10},{10,1... | collective-permute-start | bytes 1966088 | tf_op jit(solution)/shard_map/ppermute | solution.py:272
  6.9 34.1 %collective-permute-start.1 = (f32[4,40,1024]{2,1,0:T(8,128)S(1)}, f32[4,40,1024]{2,1,0:T(8,128)S(1)}, u32[]{:S(2)}, u32[]{:S(2)}) collective-permute-start(f32[4,40,1024]{2,1,0:T(8,128)S(1)} %pad.8), channel_id=1, source_target_pairs={{0,15},{1,0},{2,1},{3,2},{4,3},{5,4},{6,5},{7,6},{8,7},{9,8},{10,9... | collective-permute-start | bytes 1966088 | tf_op jit(solution)/shard_map/ppermute | solution.py:272
  12.2 28.2 %all-to-all-start = ((f32[8,3,256]{2,1,0:T(4,128)}), f32[8,3,256]{2,1,0:T(4,128)S(1)}, u32[]{:S(2)}, u32[]{:S(2)}) async-start(f32[8,3,256]{2,1,0:T(4,128)} %broadcast_in_dim.22), calls=%async_computation | async-start | bytes 65536 | tf_op jit(solution)/shard_map/all_to_all | solution.py:297
  41.0 0.9 copy-start.2
  41.0 1.2 copy-start.3
  75.8 19.6 %all-to-all-start.2 = ((f32[8,8,32,128]{3,2,1,0:T(8,128)}), f32[8,8,32,128]{3,2,1,0:T(8,128)S(1)}, u32[]{:S(2)}, u32[]{:S(2)}) async-start(f32[8,8,32,128]{3,2,1,0:T(8,128)} %get-tuple-element.25), calls=%async_computation.2 | async-start | bytes 2097152 | tf_op jit(solution)/shard_map/all_to_all | solution.py:325
  83.9 16.9 %copy-start.10 = (f32[136,256]{1,0:T(8,128)S(1)}, f32[136,256]{1,0:T(8,128)}, u32[]{:S(2)}) copy-start(f32[136,256]{1,0:T(8,128)} %get-tuple-element.22) | copy-start | bytes 417796
  83.9 18.5 %copy-start.5 = (f32[136,256]{1,0:T(8,128)S(1)}, f32[136,256]{1,0:T(8,128)}, u32[]{:S(2)}) copy-start(f32[136,256]{1,0:T(8,128)} %get-tuple-element.19) | copy-start | bytes 417796
  95.4 1.0 copy-start.1
  96.4 42.0 %all-to-all-start.3 = ((f32[8,24,32,128]{3,2,1,0:T(8,128)}), f32[8,24,32,128]{3,2,1,0:T(8,128)S(1)}, u32[]{:S(2)}, u32[]{:S(2)}) async-start(f32[8,24,32,128]{3,2,1,0:T(8,128)} %get-tuple-element.26), calls=%async_computation.3 | async-start | bytes 6291456 | tf_op jit(solution)/shard_map/all_to_all | solution.py:354
  100.8 1.5 collective-permute-start.2
  102.4 5.0 %collective-permute-start.3 = (f32[136,256]{1,0:T(8,128)S(1)}, f32[136,256]{1,0:T(8,128)S(1)}, u32[]{:S(2)}, u32[]{:S(2)}) collective-permute-start(f32[136,256]{1,0:T(8,128)S(1)} %add.28), channel_id=1, source_target_pairs={{0,1},{1,0},{2,3},{3,2},{4,5},{5,4},{6,7},{7,6},{8,9},{9,8},{10,11... | collective-permute-start | bytes 417800 | tf_op jit(solution)/shard_map/ppermute | solution.py:267
  107.4 5.7 %collective-permute-start.4 = (f32[136,256]{1,0:T(8,128)S(1)}, f32[136,256]{1,0:T(8,128)S(1)}, u32[]{:S(2)}, u32[]{:S(2)}) collective-permute-start(f32[136,256]{1,0:T(8,128)S(1)} %add.29), channel_id=1, source_target_pairs={{0,2},{1,3},{2,0},{3,1},{4,6},{5,7},{6,4},{7,5},{8,10},{9,11},{10,... | collective-permute-start | bytes 417800 | tf_op jit(solution)/shard_map/ppermute | solution.py:267
  113.2 4.3 %collective-permute-start.5 = (f32[136,256]{1,0:T(8,128)S(1)}, f32[136,256]{1,0:T(8,128)S(1)}, u32[]{:S(2)}, u32[]{:S(2)}) collective-permute-start(f32[136,256]{1,0:T(8,128)S(1)} %add.30), channel_id=1, source_target_pairs={{0,4},{1,5},{2,6},{3,7},{4,0},{5,1},{6,2},{7,3},{8,12},{9,13},{10,... | collective-permute-start | bytes 417800 | tf_op jit(solution)/shard_map/ppermute | solution.py:267
  117.5 5.5 %collective-permute-start.6 = (f32[136,256]{1,0:T(8,128)S(1)}, f32[136,256]{1,0:T(8,128)S(1)}, u32[]{:S(2)}, u32[]{:S(2)}) collective-permute-start(f32[136,256]{1,0:T(8,128)S(1)} %add.31), channel_id=1, source_target_pairs={{0,8},{1,9},{2,10},{3,11},{4,12},{5,13},{6,14},{7,15},{8,0},{9,1},... | collective-permute-start | bytes 417800 | tf_op jit(solution)/shard_map/ppermute | solution.py:267
  123.0 5.3 %copy-start.4 = (f32[136,256]{1,0:T(8,128)}, f32[136,256]{1,0:T(8,128)S(1)}, u32[]{:S(2)}) copy-start(f32[136,256]{1,0:T(8,128)S(1)} %add.32.mine_ref) | copy-start | bytes 417796
  123.0 5.3 %collective-permute-start.7 = (f32[136,256]{1,0:T(8,128)S(1)}, f32[136,256]{1,0:T(8,128)S(1)}, u32[]{:S(2)}, u32[]{:S(2)}) collective-permute-start(f32[136,256]{1,0:T(8,128)S(1)} %add.32.mine_ref), channel_id=1, source_target_pairs={{0,16},{16,0},{32,48},{48,32},{64,80},{80,64},{96,112},{112,96},{1... | collective-permute-start | bytes 417800 | tf_op jit(solution)/shard_map/ppermute | solution.py:267
  128.3 0.7 copy-start.6
  138.4 1.6 copy-start

commit v3 on v2

--- a/solution.py
+++ b/solution.py
@@ -22,9 +22,17 @@
 HALO = SECTIONS
 EDGE = 2 * HALO
 CHUNK = 8
+PATHS = ((0, 0), (2, 0), (1, 0), (3, 0), (2, 1), (1, 1), (3, 1), (0, 1))
 VMEM = pl.BlockSpec(memory_space=pltpu.VMEM)
 SMEM = pl.BlockSpec(memory_space=pltpu.SMEM)
-PARAMS = pltpu.CompilerParams(vmem_limit_bytes=56 * 1024 * 1024)
+
+
+def params(mib):
+    return pltpu.CompilerParams(vmem_limit_bytes=mib * 1024 * 1024)
+
+
+def cost(us):
+    return pl.CostEstimate(flops=0, bytes_accessed=us * 3_000_000, transcendentals=0)
 
 
 def split(x):
@@ -197,7 +205,7 @@
     send_ref[half:] = drive
 
 
-def weights_kernel(core_ref, mine_ref, other_ref, high_ref, low_ref, gram_ref):
+def weights_kernel(core_ref, order_ref, mine_ref, other_ref, high_ref, low_ref, gram_ref):
     core = core_ref[0]
     half = MEMBERS // 2
     for c in range(2):
@@ -227,14 +235,16 @@
     wbar = dot3(split(inner), lower_parts, nt)[:1] / scale
     weights = (MEMBERS - 1.0) ** 0.5 * lower / jnp.sqrt(scale) + wbar
     rest = (1.0 - jnp.sum(weights, axis=1, keepdims=True)) * (1.0 / MEMBERS)
-    high, low = split(weights + rest)
-    high_ref[...] = high
-    low_ref[...] = low
-
-
-def product_kernel(high_ref, low_ref, early_ref, rest_ref, out_ref):
+    gram_ref[...] = weights + rest
+    for n in range(N_MEM):
+        high, low = split(gram_ref[pl.ds(pl.multiple_of(order_ref[n] * OWN, OWN), OWN), :])
+        high_ref[n * OWN : (n + 1) * OWN] = high
+        low_ref[n * OWN : (n + 1) * OWN] = low
+
+
+def product_kernel(high_ref, low_ref, early_ref, rest_ref, *out_refs):
     weights = (high_ref[...], low_ref[...])
-    flat = out_ref.reshape(MEMBERS * CHUNK, LANES)
+    flat = [ref.reshape(OWN * CHUNK, LANES) for ref in out_refs]
 
     def rows(ref):
         for half in range(0, CHUNK, HALO):
@@ -245,17 +255,40 @@
             x = tuple(jnp.concatenate([p[n] for p in parts], axis=1) for n in range(2))
             y = dot3(weights, x)
             for t in range(HALO):
-                flat[pl.ds(half + t, MEMBERS, stride=CHUNK), :] = y[
-                    :, t * LANES : (t + 1) * LANES
-                ]
+                for n in range(N_MEM):
+                    flat[n][pl.ds(half + t, OWN, stride=CHUNK), :] = y[
+                        n * OWN : (n + 1) * OWN, t * LANES : (t + 1) * LANES
+                    ]
 
     step = pl.program_id(0)
     pl.when(step == 1)(lambda: rows(early_ref))
     pl.when(step != 1)(lambda: rows(rest_ref))
 
 
-def place_kernel(x_ref, out_ref):
-    out_ref[...] = x_ref[0]
+def place_first_kernel(group_ref, x_ref, out_ref):
+    out_ref[...] = x_ref[...]
+
+
+def place_kernel(group_ref, x_ref, before_ref, out_ref):
+    out_ref[...] = x_ref[...]
+
+
+def place(x, group, before=None):
+    spec = pltpu.PrefetchScalarGridSpec(
+        num_scalar_prefetch=1,
+        grid=(1,),
+        in_specs=[pl.BlockSpec((OWN, ROWS, LANES), lambda n, g: (0, 0, 0))]
+        + ([] if before is None else [pl.BlockSpec(memory_space=pl.ANY)]),
+        out_specs=pl.BlockSpec((OWN, ROWS, LANES), lambda n, g: (0, 0, g[0])),
+    )
+    return pl.pallas_call(
+        place_first_kernel if before is None else place_kernel,
+        grid_spec=spec,
+        out_shape=f32(OWN, ROWS, WIDTH),
+        input_output_aliases={} if before is None else {2: 0},
+        compiler_params=params(8),
+        cost_estimate=cost(1),
+    )(group, x, *([] if before is None else [before]))
 
 
 def f32(*shape):
@@ -278,6 +311,13 @@
     h, v = horizontal_flow_ratio, vertical_flow_ratio
     mem = lax.axis_index("mem")
     core = (mem % 2).astype(jnp.int32).reshape(1)
+    order = jnp.stack(
+        [((mem // 2 + a) % 4) * 2 + (mem % 2 + b) % 2 for a, b in PATHS]
+    ).astype(jnp.int32)
+    sources = [
+        (((mem // 2 - a) % 4) * 2 + (mem % 2 + b) % 2).astype(jnp.int32).reshape(1)
+        for a, b in PATHS
+    ]
 
     def rows_out(first):
         x = jnp.concatenate(
@@ -290,8 +330,12 @@
         )
         return jnp.pad(jnp.transpose(x, (1, 0, 2)), ((0, 0), (0, 6), (0, 0)))
 
-    low = shift(rows_out(ROWS - HALO), "reg", 1)
-    high = shift(rows_out(0), "reg", -1)
+    bottom, top = rows_out(0), rows_out(ROWS - HALO)
+    bottom, top, prior_samples, h, v = lax.optimization_barrier(
+        (bottom, top, prior_samples, h, v)
+    )
+    low = shift(top, "reg", 1)
+    high = shift(bottom, "reg", -1)
 
     facts = jnp.concatenate([obs_index.astype(jnp.float32), obs_value, obs_weight], axis=0)
     facts = lax.all_to_all(
@@ -320,8 +364,10 @@
             pltpu.VMEM((2, ROWS, 8, WIDTH), jnp.float32),
             pltpu.SemaphoreType.DMA((GROUPS,)),
         ],
-        compiler_params=PARAMS,
+        compiler_params=params(56),
+        cost_estimate=cost(22),
     )(flat, h, v)
+    early, low, high = lax.optimization_barrier((early, low, high))
     early = lax.all_to_all(early, "mem", 0, 0, tiled=True)
     obs, rest = pl.pallas_call(
         edge_kernel,
@@ -339,8 +385,10 @@
             pltpu.SemaphoreType.DMA,
             pltpu.SemaphoreType.DMA((2,)),
         ],
-        compiler_params=PARAMS,
+        compiler_params=params(56),
+        cost_estimate=cost(13),
     )(inner, rim, low, high, h, v, index)
+    early, obs = lax.optimization_barrier((early, obs))
     obs = lax.all_to_all(obs, "mem", 0, 0, tiled=True).reshape(MEMBERS, HALF_OBS)
 
     keep, send = pl.pallas_call(
@@ -348,7 +396,8 @@
         out_shape=[f32(MEMBERS // 2 + 8, MEMBERS)] * 2,
         in_specs=[SMEM, VMEM, VMEM, VMEM],
         out_specs=[VMEM, VMEM],
-        compiler_params=PARAMS,
+        compiler_params=params(12),
+        cost_estimate=cost(3),
     )(core, obs, value, weight)
     rest, send = lax.optimization_barrier((rest, send))
     rest = lax.all_to_all(rest, "mem", 0, 0, tiled=True)
@@ -361,36 +410,36 @@
     weights = pl.pallas_call(
         weights_kernel,
         out_shape=[bf16, bf16],
-        in_specs=[SMEM, VMEM, VMEM],
+        in_specs=[SMEM, SMEM, VMEM, VMEM],
         out_specs=[VMEM, VMEM],
         scratch_shapes=[pltpu.VMEM((MEMBERS, MEMBERS), jnp.float32)],
-        compiler_params=PARAMS,
-    )(core, total, other)
+        compiler_params=params(16),
+        cost_estimate=cost(6),
+    )(core, order, total, other)
 
     whole = pl.BlockSpec((MEMBERS, MEMBERS), lambda n: (0, 0))
     block = (N_MEM, CHUNK, OWN, LANES)
     analysis = pl.pallas_call(
         product_kernel,
         grid=(ROWS // CHUNK,),
-        out_shape=f32(N_MEM, OWN, ROWS, LANES),
+        out_shape=[f32(OWN, ROWS, LANES)] * N_MEM,
         in_specs=[
             whole,
             whole,
             pl.BlockSpec(block, lambda n: (0, 0, 0, 0)),
             pl.BlockSpec(block, lambda n: (0, jnp.maximum(n - 1, 0), 0, 0)),
         ],
-        out_specs=pl.BlockSpec((N_MEM, OWN, CHUNK, LANES), lambda n: (0, 0, n, 0)),
-        compiler_params=PARAMS,
+        out_specs=[pl.BlockSpec((OWN, CHUNK, LANES), lambda n: (0, n, 0))] * N_MEM,
+        compiler_params=params(20),
+        cost_estimate=cost(6),
     )(*weights, early, rest)
-    analysis = lax.all_to_all(analysis, "mem", 0, 0, tiled=True)
-    return pl.pallas_call(
-        place_kernel,
-        grid=(GROUPS,),
-        out_shape=f32(OWN, ROWS, WIDTH),
-        in_specs=[pl.BlockSpec((1, OWN, ROWS, LANES), lambda g: (g, 0, 0, 0))],
-        out_specs=pl.BlockSpec((OWN, ROWS, LANES), lambda g: (0, 0, g)),
-        compiler_params=PARAMS,
-    )(analysis)
+    result = place(analysis[0], sources[0])
+    for x, (a, b), source in zip(analysis[1:], PATHS[1:], sources[1:]):
+        arrived = lax.ppermute(
+            x, "mem", [(i, ((i // 2 + a) % 4) * 2 + (i + b) % 2) for i in range(N_MEM)]
+        )
+        result = place(arrived, source, result)
+    return result
 
 
 def solution(mesh):

time: 208 us -> 182 us (0.88)
  blocking collectives: 74.6 us -> 0 us
  waiting for transfers between devices: 36.8 us -> 73.1 us
  starting transfers between devices: 26.7 us -> 42 us
  Pallas kernels: 58.5 us -> 53.3 us
  local copies, waits for them, and re-layouts: 9.81 us -> 11.9 us
    all_to_all x2 -> x0, blocking collectives: 74.6 us -> none  [the longest x1 54.6 us: local(): analysis = lax.all_to_all(analysis, 'mem', 0, 0, tiled=True)]
    ppermute x0 -> x7, waiting for transfers between devices: none -> 32 us  [local(): lax.ppermute(x, 'mem', [(i, (i // 2 + a) % 4 * 2 + (i + b) % 2) for i in...]
    all_to_all x0 -> x1, waiting for transfers between devices: none -> 15.1 us  [local(): lax.all_to_all(obs, 'mem', 0, 0, tiled=True).reshape(MEMBERS, HALF_OBS)]
    ppermute x0 -> x7, starting transfers between devices: none -> 10.7 us  [local(): lax.ppermute(x, 'mem', [(i, (i // 2 + a) % 4 * 2 + (i + b) % 2) for i in...]
    all_to_all x1, waiting for transfers between devices: 11.5 us -> 0.84 us  [local(): early = lax.all_to_all(early, 'mem', 0, 0, tiled=True)]
    all_to_all x0 -> x1, starting transfers between devices: none -> 4.33 us  [local(): lax.all_to_all(obs, 'mem', 0, 0, tiled=True).reshape(MEMBERS, HALF_OBS)]
    pallas_call x3 -> x10, Pallas kernels: 19 us -> 15.7 us  [the longest x8 6.62 us: place(): pl.pallas_call(place_first_kernel if before is None else place_kernel, gr...]
    unnamed x24 -> x30, local copies, waits for them, and re-layouts: 5.07 us -> 7.12 us
  transfers between devices with their start and end apart: 11 -> 19, of which waited for: 8 -> 13; matrix products, arithmetic and copies ran while one was open for 1% -> 1% of each run, Pallas kernels for 15% -> 26%
where the time goes in v3:
time: 182 us; the launch traced here: 181 us
  waiting for transfers between devices  73.1 us (40%)
  Pallas kernels  53.3 us (29%)
  starting transfers between devices  42 us (23%)
  local copies, waits for them, and re-layouts  11.9 us (7%)
    ppermute x7, waiting for transfers between devices, local(): lax.ppermute(x, 'mem', [(i, (i // 2 + a) % 4 * 2 + (i + b) % 2) for i in...  32 us
    pallas_call x1, Pallas kernels, local(): pl.pallas_call(interior_kernel, out_shape=[f32(GROUPS, ROWS - EDGE, OWN,...  22.9 us
    ppermute x6, waiting for transfers between devices, swap(): return lax.ppermute(x, axis, [(i, i ^ bit) for i in range(count)])  21.3 us
    all_to_all x1, waiting for transfers between devices, local(): lax.all_to_all(obs, 'mem', 0, 0, tiled=True).reshape(MEMBERS, HALF_OBS)  15.1 us
    pallas_call x1, Pallas kernels, local(): pl.pallas_call(edge_kernel, out_shape=[f32(N_MEM, OWN, HALF_OBS), f32(GRO...  13.6 us
    ppermute x7, starting transfers between devices, local(): lax.ppermute(x, 'mem', [(i, (i // 2 + a) % 4 * 2 + (i + b) % 2) for i in...  10.7 us
    ppermute x2, starting transfers between devices, shift(): lax.ppermute(x, axis, [(i, (i + step) % count) for i in range(count)])  7.19 us
    unnamed x30, local copies, waits for them, and re-layouts  7.12 us
  transfers between devices with their start and end apart: 19, of which 13 were waited for; matrix products, arithmetic and copies ran while one was open for 1% of the time, Pallas kernels for 26%

profile of v3, /device:TPU:1, one launch (start us, length us, event | category | flops | bytes accessed | tf_op | source)
XLA Modules:
  0.0 181.4 jit_solution(5661652102552793465)
XLA Ops:
  0.0 1.8 fusion.1
  4.4 2.5 %collective-permute-start = (f32[4,40,1024]{2,1,0:T(8,128)S(1)}, f32[4,40,1024]{2,1,0:T(8,128)S(1)}, u32[]{:S(2)}, u32[]{:S(2)}) collective-permute-start(f32[4,40,1024]{2,1,0:T(8,128)S(1)} %pad.8), channel_id=1, source_target_pairs={{0,1},{1,2},{2,3},{3,4},{4,5},{5,6},{6,7},{7,8},{8,9},{9,10},{10,1... | collective-permute-start | bytes 1966088 | tf_op jit(solution)/shard_map/ppermute | solution.py:305
  6.9 4.7 %collective-permute-start.1 = (f32[4,40,1024]{2,1,0:T(8,128)S(1)}, f32[4,40,1024]{2,1,0:T(8,128)S(1)}, u32[]{:S(2)}, u32[]{:S(2)}) collective-permute-start(f32[4,40,1024]{2,1,0:T(8,128)S(1)} %pad.7), channel_id=1, source_target_pairs={{0,15},{1,0},{2,1},{3,2},{4,3},{5,4},{6,5},{7,6},{8,7},{9,8},{10,9... | collective-permute-start | bytes 1966088 | tf_op jit(solution)/shard_map/ppermute | solution.py:305
  12.2 5.3 %all-to-all-start.1 = ((f32[8,3,256]{2,1,0:T(4,128)}), f32[8,3,256]{2,1,0:T(4,128)S(1)}, u32[]{:S(2)}, u32[]{:S(2)}) async-start(f32[8,3,256]{2,1,0:T(4,128)} %broadcast_in_dim.22), calls=%async_computation.1 | async-start | bytes 65536 | tf_op jit(solution)/shard_map/all_to_all | solution.py:341
  17.5 22.9 %shard_map.64 = (f32[8,24,32,128]{3,2,1,0:T(8,128)}, f32[8,8,32,128]{3,2,1,0:T(8,128)}, f32[2,8,32,1024]{3,2,1,0:T(8,128)}) custom-call(f32[1024,1024]{1,0:T(8,128)} %bitcast.28, f32[32,1024]{1,0:T(8,128)} %h_ref.1, f32[32,1024]{1,0:T(8,128)} %v_ref.1), custom_call_target="tpu_custom_call" | custom-call | bytes 66000000 | tf_op jit(solution)/shard_map/pallas_call | solution.py:351
  40.4 4.8 %all-to-all-start = ((f32[8,8,32,128]{3,2,1,0:T(8,128)}), f32[8,8,32,128]{3,2,1,0:T(8,128)S(1)}, u32[]{:S(2)}, u32[]{:S(2)}) async-start(f32[8,8,32,128]{3,2,1,0:T(8,128)} %get-tuple-element.40), calls=%async_computation | async-start | bytes 2097152 | tf_op jit(solution)/shard_map/all_to_all | solution.py:371
  45.8 13.6 %shard_map.65 = (f32[8,32,1024]{2,1,0:T(8,128)}, f32[8,24,32,128]{3,2,1,0:T(8,128)}) custom-call(f32[8,24,32,128]{3,2,1,0:T(8,128)} %get-tuple-element.41.inner_ref, f32[2,8,32,1024]{3,2,1,0:T(8,128)} %get-tuple-element.42.rim_ref, f32[4,40,1024]{2,1,0:T(8,128)} %copy-done.9, f32[4,40,1024]{2,1,0:T(8,128)} %copy-done.10, f32[32,1024]{1,0:T(8,128)} %h_ref.1, ...), custom_call_target="tpu_custom_call" | custom-call | bytes 39000000 | tf_op jit(solution)/shard_map/pallas_call | solution.py:372
  60.3 4.3 %all-to-all-start.2 = ((f32[8,32,1024]{2,1,0:T(8,128)}), f32[8,32,1024]{2,1,0:T(8,128)S(1)}, u32[]{:S(2)}, u32[]{:S(2)}) async-start(f32[8,32,1024]{2,1,0:T(8,128)} %get-tuple-element.46), calls=%async_computation.2 | async-start | bytes 2097152 | tf_op jit(solution)/shard_map/all_to_all | solution.py:392
  64.7 15.1 %all-to-all-done.2 = f32[8,32,1024]{2,1,0:T(8,128)S(1)} async-done(((f32[8,32,1024]{2,1,0:T(8,128)}), f32[8,32,1024]{2,1,0:T(8,128)S(1)}, u32[]{:S(2)}, u32[]{:S(2)}) %all-to-all-start.2) | async-done | bytes 1048608 | tf_op jit(solution)/shard_map/all_to_all | solution.py:392
  80.9 4.4 %all-to-all-start.3 = ((f32[8,24,32,128]{3,2,1,0:T(8,128)}), f32[8,24,32,128]{3,2,1,0:T(8,128)S(1)}, u32[]{:S(2)}, u32[]{:S(2)}) async-start(f32[8,24,32,128]{3,2,1,0:T(8,128)} %get-tuple-element.54), calls=%async_computation.3 | async-start | bytes 6291456 | tf_op jit(solution)/shard_map/all_to_all | solution.py:403
  86.9 4.9 %collective-permute-done.3 = f32[136,256]{1,0:T(8,128)S(1)} collective-permute-done((f32[136,256]{1,0:T(8,128)S(1)}, f32[136,256]{1,0:T(8,128)S(1)}, u32[]{:S(2)}, u32[]{:S(2)}) %collective-permute-start.3) | collective-permute-done | bytes 139296 | tf_op jit(solution)/shard_map/ppermute | solution.py:300
  91.9 5.7 %collective-permute-done.4 = f32[136,256]{1,0:T(8,128)S(1)} collective-permute-done((f32[136,256]{1,0:T(8,128)S(1)}, f32[136,256]{1,0:T(8,128)S(1)}, u32[]{:S(2)}, u32[]{:S(2)}) %collective-permute-start.4) | collective-permute-done | bytes 139296 | tf_op jit(solution)/shard_map/ppermute | solution.py:300
  97.7 4.2 %collective-permute-done.5 = f32[136,256]{1,0:T(8,128)S(1)} collective-permute-done((f32[136,256]{1,0:T(8,128)S(1)}, f32[136,256]{1,0:T(8,128)S(1)}, u32[]{:S(2)}, u32[]{:S(2)}) %collective-permute-start.5) | collective-permute-done | bytes 139296 | tf_op jit(solution)/shard_map/ppermute | solution.py:300
  102.5 4.9 %collective-permute-done.6 = f32[136,256]{1,0:T(8,128)S(1)} collective-permute-done((f32[136,256]{1,0:T(8,128)S(1)}, f32[136,256]{1,0:T(8,128)S(1)}, u32[]{:S(2)}, u32[]{:S(2)}) %collective-permute-start.6) | collective-permute-done | bytes 139296 | tf_op jit(solution)/shard_map/ppermute | solution.py:300
  107.4 4.3 %collective-permute-start.7 = (f32[136,256]{1,0:T(8,128)S(1)}, f32[136,256]{1,0:T(8,128)S(1)}, u32[]{:S(2)}, u32[]{:S(2)}) collective-permute-start(f32[136,256]{1,0:T(8,128)S(1)} %add.186.mine_ref), channel_id=1, source_target_pairs={{0,16},{16,0},{32,48},{48,32},{64,80},{80,64},{96,112},{112,96},{1... | collective-permute-start | bytes 417800 | tf_op jit(solution)/shard_map/ppermute | solution.py:300
  113.4 5.0 %shard_map.67 = (bf16[256,256]{1,0:T(8,128)(2,1)S(1)}, bf16[256,256]{1,0:T(8,128)(2,1)S(1)}) custom-call(s32[1]{0:T(128)} %bitcast.1.core_ref, s32[8]{0:T(128)S(1)} %copy-done.8, f32[136,256]{1,0:T(8,128)S(1)} %add.186.mine_ref, f32[136,256]{1,0:T(8,128)S(1)} %collective-permute-done.7.other_ref), custom_call_target="tpu_custom_call" | custom-call | bytes 18000000 | tf_op jit(solution)/shard_map/pallas_call | solution.py:410
  119.0 3.8 %all-to-all-done.3.rest_ref = f32[8,24,32,128]{3,2,1,0:T(8,128)S(1)} async-done(((f32[8,24,32,128]{3,2,1,0:T(8,128)}), f32[8,24,32,128]{3,2,1,0:T(8,128)S(1)}, u32[]{:S(2)}, u32[]{:S(2)}) %all-to-all-start.3) | async-done | bytes 3145760 | tf_op jit(solution)/shard_map/all_to_all | solution.py:403
  125.0 4.1 %shard_map.68 = (f32[32,32,128]{2,1,0:T(8,128)S(1)}, f32[32,32,128]{2,1,0:T(8,128)S(1)}, f32[32,32,128]{2,1,0:T(8,128)S(1)}, f32[32,32,128]{2,1,0:T(8,128)}, f32...) custom-call(bf16[256,256]{1,0:T(8,128)(2,1)S(1)} %get-tuple-element.51.high_ref, ...), custom_call_target="tpu_custom_call" | custom-call | bytes 18000000 | tf_op jit(solution)/shard_map/pallas_call | solution.py:422
  132.8 3.1 %collective-permute-start.11 = (f32[32,32,128]{2,1,0:T(8,128)}, f32[32,32,128]{2,1,0:T(8,128)S(1)}, u32[]{:S(2)}, u32[]{:S(2)}) collective-permute-start(f32[32,32,128]{2,1,0:T(8,128)} %get-tuple-element.58), channel_id=1, source_target_pairs={{0,80},{16,64},{32,112},{48,96},{64,16},{80,0},{96,48},{112,32},{1... | collective-permute-start | bytes 1572872 | tf_op jit(solution)/shard_map/ppermute | solution.py:438
  135.9 8.1 %collective-permute-done.14.x_ref = f32[32,32,128]{2,1,0:T(8,128)S(1)} collective-permute-done((f32[32,32,128]{2,1,0:T(8,128)S(1)}, f32[32,32,128]{2,1,0:T(8,128)S(1)}, u32[]{:S(2)}, u32[]{:S(2)}) %collective-permute-start.14) | collective-permute-done | bytes 524320 | tf_op jit(solution)/shard_map/ppermute | solution.py:438
  144.0 3.9 %collective-permute-start.9 = (f32[32,32,128]{2,1,0:T(8,128)}, f32[32,32,128]{2,1,0:T(8,128)S(1)}, u32[]{:S(2)}, u32[]{:S(2)}) collective-permute-start(f32[32,32,128]{2,1,0:T(8,128)} %get-tuple-element.56), channel_id=1, source_target_pairs={{0,112},{16,96},{32,16},{48,0},{64,48},{80,32},{96,80},{112,64},{1... | collective-permute-start | bytes 1572872 | tf_op jit(solution)/shard_map/ppermute | solution.py:438
  147.9 9.8 %collective-permute-done.13.x_ref = f32[32,32,128]{2,1,0:T(8,128)S(1)} collective-permute-done((f32[32,32,128]{2,1,0:T(8,128)S(1)}, f32[32,32,128]{2,1,0:T(8,128)S(1)}, u32[]{:S(2)}, u32[]{:S(2)}) %collective-permute-start.13) | collective-permute-done | bytes 524320 | tf_op jit(solution)/shard_map/ppermute | solution.py:438
  164.0 5.0 %collective-permute-done.11.x_ref = f32[32,32,128]{2,1,0:T(8,128)S(1)} collective-permute-done((f32[32,32,128]{2,1,0:T(8,128)}, f32[32,32,128]{2,1,0:T(8,128)S(1)}, u32[]{:S(2)}, u32[]{:S(2)}) %collective-permute-start.11) | collective-permute-done | bytes 524320 | tf_op jit(solution)/shard_map/ppermute | solution.py:438
  169.8 9.1 %collective-permute-done.10.x_ref = f32[32,32,128]{2,1,0:T(8,128)S(1)} collective-permute-done((f32[32,32,128]{2,1,0:T(8,128)}, f32[32,32,128]{2,1,0:T(8,128)S(1)}, u32[]{:S(2)}, u32[]{:S(2)}) %collective-permute-start.10) | collective-permute-done | bytes 524320 | tf_op jit(solution)/shard_map/ppermute | solution.py:438
  (80 shorter events, 25.9 us)
Async XLA Ops:
  1.8 9.8 %copy-start.13 = (s32[1,256]{1,0:T(1,128)S(1)}, s32[1,256]{1,0:T(1,128)}, u32[]{:S(2)}) copy-start(s32[1,256]{1,0:T(1,128)} %param.9) | copy-start | bytes 3076
  1.8 9.8 %copy-start.11 = (f32[1,256]{1,0:T(1,128)S(1)}, f32[1,256]{1,0:T(1,128)}, u32[]{:S(2)}) copy-start(f32[1,256]{1,0:T(1,128)} %param.11) | copy-start | bytes 3076
  1.8 9.8 %copy-start.12 = (f32[1,256]{1,0:T(1,128)S(1)}, f32[1,256]{1,0:T(1,128)}, u32[]{:S(2)}) copy-start(f32[1,256]{1,0:T(1,128)} %param.10) | copy-start | bytes 3076
  4.4 36.0 %collective-permute-start = (f32[4,40,1024]{2,1,0:T(8,128)S(1)}, f32[4,40,1024]{2,1,0:T(8,128)S(1)}, u32[]{:S(2)}, u32[]{:S(2)}) collective-permute-start(f32[4,40,1024]{2,1,0:T(8,128)S(1)} %pad.8), channel_id=1, source_target_pairs={{0,1},{1,2},{2,3},{3,4},{4,5},{5,6},{6,7},{7,8},{8,9},{9,10},{10,1... | collective-permute-start | bytes 1966088 | tf_op jit(solution)/shard_map/ppermute | solution.py:305
  6.9 33.5 %collective-permute-start.1 = (f32[4,40,1024]{2,1,0:T(8,128)S(1)}, f32[4,40,1024]{2,1,0:T(8,128)S(1)}, u32[]{:S(2)}, u32[]{:S(2)}) collective-permute-start(f32[4,40,1024]{2,1,0:T(8,128)S(1)} %pad.7), channel_id=1, source_target_pairs={{0,15},{1,0},{2,1},{3,2},{4,3},{5,4},{6,5},{7,6},{8,7},{9,8},{10,9... | collective-permute-start | bytes 1966088 | tf_op jit(solution)/shard_map/ppermute | solution.py:305
  12.2 28.2 %all-to-all-start.1 = ((f32[8,3,256]{2,1,0:T(4,128)}), f32[8,3,256]{2,1,0:T(4,128)S(1)}, u32[]{:S(2)}, u32[]{:S(2)}) async-start(f32[8,3,256]{2,1,0:T(4,128)} %broadcast_in_dim.22), calls=%async_computation.1 | async-start | bytes 65536 | tf_op jit(solution)/shard_map/all_to_all | solution.py:341
  40.4 5.5 %copy-start.9 = (f32[4,40,1024]{2,1,0:T(8,128)}, f32[4,40,1024]{2,1,0:T(8,128)S(1)}, u32[]{:S(2)}) copy-start(f32[4,40,1024]{2,1,0:T(8,128)S(1)} %collective-permute-done.low_ref) | copy-start | bytes 1966084
  40.4 19.9 %all-to-all-start = ((f32[8,8,32,128]{3,2,1,0:T(8,128)}), f32[8,8,32,128]{3,2,1,0:T(8,128)S(1)}, u32[]{:S(2)}, u32[]{:S(2)}) async-start(f32[8,8,32,128]{3,2,1,0:T(8,128)} %get-tuple-element.40), calls=%async_computation | async-start | bytes 2097152 | tf_op jit(solution)/shard_map/all_to_all | solution.py:371
  60.3 20.5 %copy-start = (f32[8,8,32,128]{3,2,1,0:T(8,128)}, f32[8,8,32,128]{3,2,1,0:T(8,128)S(1)}, u32[]{:S(2)}) copy-start(f32[8,8,32,128]{3,2,1,0:T(8,128)S(1)} %all-to-all-done.early_ref) | copy-start | bytes 3145732
  60.3 19.4 %all-to-all-start.2 = ((f32[8,32,1024]{2,1,0:T(8,128)}), f32[8,32,1024]{2,1,0:T(8,128)S(1)}, u32[]{:S(2)}, u32[]{:S(2)}) async-start(f32[8,32,1024]{2,1,0:T(8,128)} %get-tuple-element.46), calls=%async_computation.2 | async-start | bytes 2097152 | tf_op jit(solution)/shard_map/all_to_all | solution.py:392
  80.9 42.0 %all-to-all-start.3 = ((f32[8,24,32,128]{3,2,1,0:T(8,128)}), f32[8,24,32,128]{3,2,1,0:T(8,128)S(1)}, u32[]{:S(2)}, u32[]{:S(2)}) async-start(f32[8,24,32,128]{3,2,1,0:T(8,128)} %get-tuple-element.54), calls=%async_computation.3 | async-start | bytes 6291456 | tf_op jit(solution)/shard_map/all_to_all | solution.py:403
  85.3 1.5 collective-permute-start.2
  86.8 5.0 %collective-permute-start.3 = (f32[136,256]{1,0:T(8,128)S(1)}, f32[136,256]{1,0:T(8,128)S(1)}, u32[]{:S(2)}, u32[]{:S(2)}) collective-permute-start(f32[136,256]{1,0:T(8,128)S(1)} %add.182), channel_id=1, source_target_pairs={{0,1},{1,0},{2,3},{3,2},{4,5},{5,4},{6,7},{7,6},{8,9},{9,8},{10,11... | collective-permute-start | bytes 417800 | tf_op jit(solution)/shard_map/ppermute | solution.py:300
  91.8 5.8 %collective-permute-start.4 = (f32[136,256]{1,0:T(8,128)S(1)}, f32[136,256]{1,0:T(8,128)S(1)}, u32[]{:S(2)}, u32[]{:S(2)}) collective-permute-start(f32[136,256]{1,0:T(8,128)S(1)} %add.183), channel_id=1, source_target_pairs={{0,2},{1,3},{2,0},{3,1},{4,6},{5,7},{6,4},{7,5},{8,10},{9,11},{10,... | collective-permute-start | bytes 417800 | tf_op jit(solution)/shard_map/ppermute | solution.py:300
  97.6 4.3 %collective-permute-start.5 = (f32[136,256]{1,0:T(8,128)S(1)}, f32[136,256]{1,0:T(8,128)S(1)}, u32[]{:S(2)}, u32[]{:S(2)}) collective-permute-start(f32[136,256]{1,0:T(8,128)S(1)} %add.184), channel_id=1, source_target_pairs={{0,4},{1,5},{2,6},{3,7},{4,0},{5,1},{6,2},{7,3},{8,12},{9,13},{10,... | collective-permute-start | bytes 417800 | tf_op jit(solution)/shard_map/ppermute | solution.py:300
  101.9 5.5 %collective-permute-start.6 = (f32[136,256]{1,0:T(8,128)S(1)}, f32[136,256]{1,0:T(8,128)S(1)}, u32[]{:S(2)}, u32[]{:S(2)}) collective-permute-start(f32[136,256]{1,0:T(8,128)S(1)} %add.185), channel_id=1, source_target_pairs={{0,8},{1,9},{2,10},{3,11},{4,12},{5,13},{6,14},{7,15},{8,0},{9,1},... | collective-permute-start | bytes 417800 | tf_op jit(solution)/shard_map/ppermute | solution.py:300
  107.4 5.3 %collective-permute-start.7 = (f32[136,256]{1,0:T(8,128)S(1)}, f32[136,256]{1,0:T(8,128)S(1)}, u32[]{:S(2)}, u32[]{:S(2)}) collective-permute-start(f32[136,256]{1,0:T(8,128)S(1)} %add.186.mine_ref), channel_id=1, source_target_pairs={{0,16},{16,0},{32,48},{48,32},{64,80},{80,64},{96,112},{112,96},{1... | collective-permute-start | bytes 417800 | tf_op jit(solution)/shard_map/ppermute | solution.py:300
  129.9 14.1 %collective-permute-start.14 = (f32[32,32,128]{2,1,0:T(8,128)S(1)}, f32[32,32,128]{2,1,0:T(8,128)S(1)}, u32[]{:S(2)}, u32[]{:S(2)}) collective-permute-start(f32[32,32,128]{2,1,0:T(8,128)S(1)} %get-tuple-element.61), channel_id=1, source_target_pairs={{0,64},{16,80},{32,96},{48,112},{64,0},{80,16},{96,32},{112,48},{1... | collective-permute-start | bytes 1572872 | tf_op jit(solution)/shard_map/ppermute | solution.py:438
  130.2 27.5 %collective-permute-start.13 = (f32[32,32,128]{2,1,0:T(8,128)S(1)}, f32[32,32,128]{2,1,0:T(8,128)S(1)}, u32[]{:S(2)}, u32[]{:S(2)}) collective-permute-start(f32[32,32,128]{2,1,0:T(8,128)S(1)} %get-tuple-element.60), channel_id=1, source_target_pairs={{0,32},{16,48},{32,64},{48,80},{64,96},{80,112},{96,0},{112,16},{1... | collective-permute-start | bytes 1572872 | tf_op jit(solution)/shard_map/ppermute | solution.py:438
  131.3 31.9 %collective-permute-start.12 = (f32[32,32,128]{2,1,0:T(8,128)}, f32[32,32,128]{2,1,0:T(8,128)S(1)}, u32[]{:S(2)}, u32[]{:S(2)}) collective-permute-start(f32[32,32,128]{2,1,0:T(8,128)} %get-tuple-element.59), channel_id=1, source_target_pairs={{0,96},{16,112},{32,0},{48,16},{64,32},{80,48},{96,64},{112,80},{1... | collective-permute-start | bytes 1572872 | tf_op jit(solution)/shard_map/ppermute | solution.py:438
  132.8 36.1 %collective-permute-start.11 = (f32[32,32,128]{2,1,0:T(8,128)}, f32[32,32,128]{2,1,0:T(8,128)S(1)}, u32[]{:S(2)}, u32[]{:S(2)}) collective-permute-start(f32[32,32,128]{2,1,0:T(8,128)} %get-tuple-element.58), channel_id=1, source_target_pairs={{0,80},{16,64},{32,112},{48,96},{64,16},{80,0},{96,48},{112,32},{1... | collective-permute-start | bytes 1572872 | tf_op jit(solution)/shard_map/ppermute | solution.py:438
  135.9 43.0 %collective-permute-start.10 = (f32[32,32,128]{2,1,0:T(8,128)}, f32[32,32,128]{2,1,0:T(8,128)S(1)}, u32[]{:S(2)}, u32[]{:S(2)}) collective-permute-start(f32[32,32,128]{2,1,0:T(8,128)} %get-tuple-element.57), channel_id=1, source_target_pairs={{0,48},{16,32},{32,80},{48,64},{64,112},{80,96},{96,16},{112,0},{1... | collective-permute-start | bytes 1572872 | tf_op jit(solution)/shard_map/ppermute | solution.py:438
  144.0 35.8 %collective-permute-start.9 = (f32[32,32,128]{2,1,0:T(8,128)}, f32[32,32,128]{2,1,0:T(8,128)S(1)}, u32[]{:S(2)}, u32[]{:S(2)}) collective-permute-start(f32[32,32,128]{2,1,0:T(8,128)} %get-tuple-element.56), channel_id=1, source_target_pairs={{0,112},{16,96},{32,16},{48,0},{64,48},{80,32},{96,80},{112,64},{1... | collective-permute-start | bytes 1572872 | tf_op jit(solution)/shard_map/ppermute | solution.py:438
  158.5 22.1 %collective-permute-start.8 = (f32[32,32,128]{2,1,0:T(8,128)}, f32[32,32,128]{2,1,0:T(8,128)S(1)}, u32[]{:S(2)}, u32[]{:S(2)}) collective-permute-start(f32[32,32,128]{2,1,0:T(8,128)} %get-tuple-element.55), channel_id=1, source_target_pairs={{0,16},{16,0},{32,48},{48,32},{64,80},{80,64},{96,112},{112,96},{1... | collective-permute-start | bytes 1572872 | tf_op jit(solution)/shard_map/ppermute | solution.py:438
  (9 other events, 12.8 us)

commit v4 on v3

v4 whole, which is shorter than its diff:
```python
import functools

import jax
import jax.numpy as jnp
from jax import lax
from jax.experimental import pallas as pl
from jax.experimental.pallas import tpu as pltpu
from jax.sharding import PartitionSpec as P

SECTIONS = 4
NS_ITERS = 6
MEMBERS = 256
N_MEM = 8
N_REG = 16
OWN = MEMBERS // N_MEM
ROWS = 32
WIDTH = 1024
LANES = 128
GROUPS = WIDTH // LANES
OBS = 256
HALF_OBS = OBS * GROUPS // 2
HALO = SECTIONS
EDGE = 2 * HALO
CHUNK = 8
SUB = 8
PATHS = ((0, 0), (2, 0), (1, 0), (3, 0), (2, 1), (1, 1), (3, 1), (0, 1))
VMEM = pl.BlockSpec(memory_space=pltpu.VMEM)
SMEM = pl.BlockSpec(memory_space=pltpu.SMEM)


def params(mib):
    return pltpu.CompilerParams(vmem_limit_bytes=mib * 1024 * 1024)


def cost(us):
    return pl.CostEstimate(flops=0, bytes_accessed=us * 3_000_000, transcendentals=0)


def split(x):
    high = x.astype(jnp.bfloat16)
    return high, (x - high.astype(jnp.float32)).astype(jnp.bfloat16)


def dot3(a, b, dims=(((1,), (0,)), ((), ()))):
    dot = functools.partial(
        lax.dot_general, dimension_numbers=dims, preferred_element_type=jnp.float32
    )
    return dot(a[0], b[0]) + (dot(a[0], b[1]) + dot(a[1], b[0]))


def mul(a, b):
    return dot3(split(a), split(b))


def coefficients(h, v, coef_ref, i):
    coef_ref[0, i] = jnp.broadcast_to(h, (SUB, WIDTH))
    coef_ref[1, i] = jnp.broadcast_to(v, (SUB, WIDTH))


def advance(src, dst, coef_ref, first, last, at, grouped):
    lane = lax.broadcasted_iota(jnp.int32, (SUB, LANES), 1)

    def tile(i, m):
        def read(row, j):
            return src[row, m : m + SUB, j * LANES : (j + 1) * LANES]

        middle = [read(i, j) for j in range(GROUPS)]
        right = [pltpu.roll(x, 1, 1) for x in middle]
        left = [pltpu.roll(x, LANES - 1, 1) for x in middle]
        results = []
        for j in range(GROUPS):
            h = coef_ref[0, i, :, j * LANES : (j + 1) * LANES]
            v = coef_ref[1, i, :, j * LANES : (j + 1) * LANES]
            side = jnp.where(
                h > 0.0,
                jnp.where(lane == 0, right[j - 1], right[j]),
                jnp.where(lane == LANES - 1, left[(j + 1) % GROUPS], left[j]),
            )
            below = jnp.where(v > 0.0, read(i - 1, j), read(i + 1, j))
            ah, av = jnp.abs(h), jnp.abs(v)
            results.append((1.0 - ah - av) * middle[j] + ah * side + av * below)
        for j, x in enumerate(results):
            if grouped:
                dst[j, i + at, m : m + SUB] = x
            else:
                dst[i + at, m : m + SUB, j * LANES : (j + 1) * LANES] = x

    def body(n, carry):
        start = jnp.minimum(first + n * HALO, last - HALO)
        for q in range(HALO):
            for m in range(0, OWN, SUB):
                tile(start + q, m)
        return carry

    lax.fori_loop(0, -(-(last - first) // HALO), body, 0)


def pack_kernel(parity_ref, prior_ref, h_ref, v_ref, a_ref, b_ref, given, sems):
    copies = []
    for side in range(2):
        rows = slice(side * (ROWS - SUB), side * (ROWS - SUB) + SUB)
        copies.append(
            [
                pltpu.make_async_copy(
                    prior_ref.at[:, rows, j * LANES : (j + 1) * LANES],
                    given.at[side, j],
                    sems.at[side, j],
                )
                for j in range(GROUPS)
            ]
        )
    for j in range(GROUPS):
        for side in range(2):
            copies[side][j].start()
    for side in range(2):
        for copy in copies[side]:
            copy.wait()
    parity = parity_ref[0]
    for even in range(2):

        @pl.when(parity == 1 - even)
        def _():
            for side in range(2):
                out_ref = a_ref if side == even else b_ref
                first = side * (ROWS - HALO)
                for i in range(HALO):
                    for j in range(GROUPS):
                        x = given.at[side, j].reshape(OWN * SUB, LANES)[
                            pl.ds(side * (SUB - HALO) + i, OWN, stride=SUB), :
                        ]
                        out_ref[i, :OWN, j * LANES : (j + 1) * LANES] = x
                    out_ref[i, OWN : OWN + 1] = h_ref[first + i : first + i + 1]
                    out_ref[i, OWN + 1 : OWN + 2] = v_ref[first + i : first + i + 1]


def interior_kernel(
    prior_ref, h_ref, v_ref,
    inner_ref, early_ref, rim_ref, given, one, two, field, coef_ref, sems, out_sems,
):
    copies = [
        pltpu.make_async_copy(
            prior_ref.at[:, j * LANES : (j + 1) * LANES], given.at[j], sems.at[j]
        )
        for j in range(GROUPS)
    ]
    for copy in copies:
        copy.start()
    for i in range(ROWS):
        coefficients(h_ref[i : i + 1], v_ref[i : i + 1], coef_ref, i)
    for j in range(GROUPS):
        at = slice(j * LANES, (j + 1) * LANES)
        copies[j].wait()
        for i in range(ROWS):
            one[i, :, at] = given[j, pl.ds(i, OWN, stride=ROWS), :]
    rims = [
        pltpu.make_async_copy(
            one.at[side * (ROWS - EDGE) : side * (ROWS - EDGE) + EDGE],
            rim_ref.at[side],
            out_sems.at[side],
        )
        for side in range(2)
    ]
    for copy in rims:
        copy.start()
    advance(one, two, coef_ref, 1, ROWS - 1, 0, False)
    for copy in rims:
        copy.wait()
    advance(two, one, coef_ref, 2, ROWS - 2, 0, False)
    advance(one, two, coef_ref, 3, ROWS - 3, 0, False)
    advance(two, field, coef_ref, CHUNK, 2 * CHUNK, -HALO, True)
    early = pltpu.make_async_copy(
        field.at[:, CHUNK - HALO : 2 * CHUNK - HALO], early_ref, out_sems.at[2]
    )
    early.start()
    advance(two, field, coef_ref, HALO, CHUNK, -HALO, True)
    middle = 2 * CHUNK - HALO
    upper = pltpu.make_async_copy(field.at[:, :middle], inner_ref.at[:, :middle], out_sems.at[3])
    upper.start()
    advance(two, field, coef_ref, 2 * CHUNK, ROWS - HALO, -HALO, True)
    lower = pltpu.make_async_copy(field.at[:, middle:], inner_ref.at[:, middle:], out_sems.at[4])
    lower.start()
    early.wait()
    upper.wait()
    lower.wait()


def edge_kernel(
    parity_ref, inner_ref, rim_ref, a_ref, b_ref, h_ref, v_ref, index_ref,
    obs_ref, rest_ref, field, one, two, coef_ref, in_sem, out_sems,
):
    load = pltpu.make_async_copy(inner_ref, field.at[:, HALO : ROWS - HALO], in_sem)
    load.start()
    odd = parity_ref[0] == 1
    for side, (near_ref, far_ref, halo_at, own_at, own_first) in enumerate(
        ((a_ref, b_ref, 0, HALO, 0), (b_ref, a_ref, EDGE, 0, ROWS - EDGE))
    ):
        for i in range(HALO):
            halo = jnp.where(odd, near_ref[i], far_ref[i])
            one[halo_at + i] = halo[:OWN]
            coefficients(halo[OWN : OWN + 1], halo[OWN + 1 : OWN + 2], coef_ref, halo_at + i)
        for i in range(EDGE):
            one[own_at + i] = rim_ref[side, i]
            coefficients(
                h_ref[own_first + i : own_first + i + 1],
                v_ref[own_first + i : own_first + i + 1],
                coef_ref,
                own_at + i,
            )
        last = HALO + EDGE
        advance(one, two, coef_ref, 1, last - 1, 0, False)
        advance(two, one, coef_ref, 2, last - 2, 0, False)
        advance(one, two, coef_ref, 3, last - 3, 0, False)
        at = -HALO if side == 0 else ROWS - EDGE
        advance(two, field, coef_ref, HALO, EDGE, at, True)
    load.wait()
    stores = [
        pltpu.make_async_copy(
            field.at[:, first : first + count], rest_ref.at[:, to : to + count], out_sems.at[n]
        )
        for n, (first, count, to) in enumerate(
            ((0, CHUNK, 0), (2 * CHUNK, ROWS - 2 * CHUNK, CHUNK))
        )
    ]
    for store in stores:
        store.start()
    for g in range(GROUPS):
        for t in range(OBS // LANES):
            place = index_ref[g : g + 1, t * LANES : (t + 1) * LANES]
            row = jnp.broadcast_to(place >> 7, (OWN, LANES))
            col = jnp.broadcast_to(place & (LANES - 1), (OWN, LANES))
            total = jnp.zeros((OWN, LANES), jnp.float32)
            for i in range(ROWS):
                x = jnp.take_along_axis(field[g, i], col, axis=1, mode="promise_in_bounds")
                total = jnp.where(row == i, x, total)
            at = (g % 4) * OBS + t * LANES
            for x in range(N_MEM // 2):
                obs_ref[2 * x + g // 4, :, at : at + LANES] = total
    for store in stores:
        store.wait()


def gram_kernel(core_ref, obs_ref, value_ref, weight_ref, keep_ref, send_ref):
    obs = obs_ref[...]
    mean = jnp.sum(obs, axis=0, keepdims=True) * (1.0 / MEMBERS)
    anomalies = obs - mean
    weighted = split(anomalies * weight_ref[...])
    innovation = jnp.broadcast_to(value_ref[...] - mean, (8, HALF_OBS))
    nt = (((1,), (1,)), ((), ()))
    gram = dot3(split(anomalies), weighted, nt)
    drive = dot3(split(innovation), weighted, nt)
    core = core_ref[0]
    half = MEMBERS // 2
    for c in range(2):

        @pl.when(core == c)
        def _():
            keep_ref[:half] = gram[c * half : (c + 1) * half]
            send_ref[:half] = gram[(1 - c) * half : (2 - c) * half]

    keep_ref[half:] = drive
    send_ref[half:] = drive


def weights_kernel(mem_ref, mine_ref, other_ref, out_ref, gram_ref):
    mem = mem_ref[0]
    core = lax.rem(mem, 2)
    half = MEMBERS // 2
    for c in range(2):

        @pl.when(core == c)
        def _():
            gram_ref[c * half : (c + 1) * half] = mine_ref[:half]
            gram_ref[(1 - c) * half : (2 - c) * half] = other_ref[:half]

    drive = mine_ref[half:]
    rows = lax.broadcasted_iota(jnp.int32, (MEMBERS, MEMBERS), 0)
    cols = lax.broadcasted_iota(jnp.int32, (MEMBERS, MEMBERS), 1)
    identity = (rows == cols).astype(jnp.float32)
    gram = gram_ref[...] + (MEMBERS - 1.0) * identity
    squares = jnp.sum(jnp.sum(gram * gram, axis=0, keepdims=True), axis=1, keepdims=True)
    scale = jnp.sqrt(squares)
    upper = gram / scale
    lower = 1.5 * identity - 0.5 * upper
    middle = lower
    for number in range(1, NS_ITERS):
        upper = mul(upper, middle)
        middle = 1.5 * identity - 0.5 * mul(lower, upper)
        lower = mul(middle, lower)
    lower_parts = split(lower)
    nt = (((1,), (1,)), ((), ()))
    inner = dot3(split(drive), lower_parts, nt)
    wbar = dot3(split(inner), lower_parts, nt)[:1] / scale
    weights = (MEMBERS - 1.0) ** 0.5 * lower / jnp.sqrt(scale) + wbar
    rest = (1.0 - jnp.sum(weights, axis=1, keepdims=True)) * (1.0 / MEMBERS)
    gram_ref[...] = weights + rest
    for n, (a, b) in enumerate(PATHS):
        place = lax.rem(mem // 2 + a, 4) * 2 + lax.rem(core + b, 2)
        high, low = split(gram_ref[pl.ds(pl.multiple_of(place * OWN, OWN), OWN), :])
        out_ref[n * OWN : (n + 1) * OWN] = high
        out_ref[MEMBERS + n * OWN : MEMBERS + (n + 1) * OWN] = low


def product_kernel(mem_ref, weights_ref, early_ref, rest_ref, *out_refs):
    weights = (weights_ref[:MEMBERS], weights_ref[MEMBERS:])
    flat = [ref.reshape(OWN * CHUNK, LANES) for ref in out_refs]

    def rows(ref):
        for half in range(0, CHUNK, HALO):
            parts = [
                split(jnp.concatenate([ref[s, half + t] for s in range(N_MEM)], axis=0))
                for t in range(HALO)
            ]
            x = tuple(jnp.concatenate([p[n] for p in parts], axis=1) for n in range(2))
            y = dot3(weights, x)
            for t in range(HALO):
                for n in range(N_MEM):
                    flat[n][pl.ds(half + t, OWN, stride=CHUNK), :] = y[
                        n * OWN : (n + 1) * OWN, t * LANES : (t + 1) * LANES
                    ]

    step = pl.program_id(0)
    pl.when(step == 1)(lambda: rows(early_ref))
    pl.when(step != 1)(lambda: rows(rest_ref))


def place_kernel(group_ref, x_ref, before_ref, out_ref):
    out_ref[...] = x_ref[...]


def place(x, group, before):
    return pl.pallas_call(
        place_kernel,
        grid_spec=pltpu.PrefetchScalarGridSpec(
            num_scalar_prefetch=1,
            grid=(1,),
            in_specs=[
                pl.BlockSpec((OWN, ROWS, LANES), lambda n, g: (0, 0, 0)),
                pl.BlockSpec(memory_space=pl.ANY),
            ],
            out_specs=pl.BlockSpec((OWN, ROWS, LANES), lambda n, g: (0, 0, g[0])),
        ),
        out_shape=f32(OWN, ROWS, WIDTH),
        input_output_aliases={2: 0},
        compiler_params=params(8),
        cost_estimate=cost(1),
    )(group, x, before)


def f32(*shape):
    return jax.ShapeDtypeStruct(shape, jnp.float32)


def swap(x, axis, bit):
    count = lax.axis_size(axis)
    return lax.ppermute(x, axis, [(i, i ^ bit) for i in range(count)])


def local(
    prior_samples, horizontal_flow_ratio, vertical_flow_ratio, obs_index, obs_value, obs_weight
):
    h, v = horizontal_flow_ratio, vertical_flow_ratio
    anywhere = pl.BlockSpec(memory_space=pl.ANY)
    mem = lax.axis_index("mem").astype(jnp.int32)
    core = (mem % 2).reshape(1)
    parity = (lax.axis_index("reg").astype(jnp.int32) % 2).reshape(1)
    sources = [
        (((mem // 2 - a) % 4) * 2 + (mem % 2 + b) % 2).reshape(1) for a, b in PATHS
    ]
    mem = mem.reshape(1)

    halo_a, halo_b = pl.pallas_call(
        pack_kernel,
        out_shape=[f32(HALO, OWN + SUB, WIDTH)] * 2,
        in_specs=[SMEM, anywhere, VMEM, VMEM],
        out_specs=[VMEM, VMEM],
        scratch_shapes=[
            pltpu.VMEM((2, GROUPS, OWN, SUB, LANES), jnp.float32),
            pltpu.SemaphoreType.DMA((2, GROUPS)),
        ],
        compiler_params=params(56),
    )(parity, prior_samples, h, v)
    halo_a, halo_b, prior_samples, h, v = lax.optimization_barrier(
        (halo_a, halo_b, prior_samples, h, v)
    )
    halo_a = lax.ppermute(halo_a, "reg", [(i, i ^ 1) for i in range(N_REG)])
    halo_b = lax.ppermute(
        halo_b, "reg", [(i, (i - 1 if i % 2 == 0 else i + 1) % N_REG) for i in range(N_REG)]
    )

    facts = jnp.concatenate([obs_index.astype(jnp.float32), obs_value, obs_weight], axis=0)
    facts = lax.all_to_all(
        jnp.broadcast_to(facts[None], (N_MEM, 3, OBS)), "mem", 0, 0, tiled=True
    )
    index = facts[:, 0].astype(jnp.int32)
    half_facts = lax.dynamic_slice_in_dim(facts, core[0] * 4, 4, axis=0)
    value = half_facts[:, 1].reshape(1, HALF_OBS)
    weight = half_facts[:, 2].reshape(1, HALF_OBS)

    inner, early, rim = pl.pallas_call(
        interior_kernel,
        out_shape=[
            f32(GROUPS, ROWS - EDGE, OWN, LANES),
            f32(GROUPS, CHUNK, OWN, LANES),
            f32(2, EDGE, OWN, WIDTH),
        ],
        in_specs=[anywhere, VMEM, VMEM],
        out_specs=[anywhere] * 3,
        scratch_shapes=[
            pltpu.VMEM((GROUPS, OWN * ROWS, LANES), jnp.float32),
            pltpu.VMEM((ROWS, OWN, WIDTH), jnp.float32),
            pltpu.VMEM((ROWS, OWN, WIDTH), jnp.float32),
            pltpu.VMEM((GROUPS, ROWS - EDGE, OWN, LANES), jnp.float32),
            pltpu.VMEM((2, ROWS, SUB, WIDTH), jnp.float32),
            pltpu.SemaphoreType.DMA((GROUPS,)),
            pltpu.SemaphoreType.DMA((5,)),
        ],
        compiler_params=params(56),
        cost_estimate=cost(17),
    )(prior_samples.reshape(OWN * ROWS, WIDTH), h, v)
    early, halo_a, halo_b = lax.optimization_barrier((early, halo_a, halo_b))
    early = lax.all_to_all(early, "mem", 0, 0, tiled=True)
    obs, rest = pl.pallas_call(
        edge_kernel,
        out_shape=[
            f32(N_MEM, OWN, HALF_OBS),
            f32(GROUPS, ROWS - CHUNK, OWN, LANES),
        ],
        in_specs=[SMEM, anywhere] + [VMEM] * 6,
        out_specs=[VMEM, anywhere],
        scratch_shapes=[
            pltpu.VMEM((GROUPS, ROWS, OWN, LANES), jnp.float32),
            pltpu.VMEM((HALO + EDGE, OWN, WIDTH), jnp.float32),
            pltpu.VMEM((HALO + EDGE, OWN, WIDTH), jnp.float32),
            pltpu.VMEM((2, HALO + EDGE, SUB, WIDTH), jnp.float32),
            pltpu.SemaphoreType.DMA,
            pltpu.SemaphoreType.DMA((2,)),
        ],
        compiler_params=params(56),
        cost_estimate=cost(13),
    )(parity, inner, rim, halo_a, halo_b, h, v, index)
    early, obs = lax.optimization_barrier((early, obs))
    obs = lax.all_to_all(obs, "mem", 0, 0, tiled=True).reshape(MEMBERS, HALF_OBS)

    keep, send = pl.pallas_call(
        gram_kernel,
        out_shape=[f32(MEMBERS // 2 + 8, MEMBERS)] * 2,
        in_specs=[SMEM, VMEM, VMEM, VMEM],
        out_specs=[VMEM, VMEM],
        compiler_params=params(12),
        cost_estimate=cost(3),
    )(core, obs, value, weight)
    rest, send = lax.optimization_barrier((rest, send))
    rest = lax.all_to_all(rest, "mem", 0, 0, tiled=True)
    total = keep + swap(send, "mem", 1)
    for bit in (1, 2, 4, 8):
        total = total + swap(total, "reg", bit)
    other = swap(total, "mem", 1)

    weights = pl.pallas_call(
        weights_kernel,
        out_shape=jax.ShapeDtypeStruct((2 * MEMBERS, MEMBERS), jnp.bfloat16),
        in_specs=[SMEM, VMEM, VMEM],
        out_specs=VMEM,
        scratch_shapes=[pltpu.VMEM((MEMBERS, MEMBERS), jnp.float32)],
        compiler_params=params(16),
        cost_estimate=cost(6),
    )(mem, total, other)

    block = (N_MEM, CHUNK, OWN, LANES)
    result, *analysis = pl.pallas_call(
        product_kernel,
        grid_spec=pltpu.PrefetchScalarGridSpec(
            num_scalar_prefetch=1,
            grid=(ROWS // CHUNK,),
            in_specs=[
                pl.BlockSpec((2 * MEMBERS, MEMBERS), lambda n, g: (0, 0)),
                pl.BlockSpec(block, lambda n, g: (0, 0, 0, 0)),
                pl.BlockSpec(block, lambda n, g: (0, jnp.maximum(n - 1, 0), 0, 0)),
            ],
            out_specs=[pl.BlockSpec((OWN, CHUNK, LANES), lambda n, g: (0, n, g[0]))]
            + [pl.BlockSpec((OWN, CHUNK, LANES), lambda n, g: (0, n, 0))] * (N_MEM - 1),
        ),
        out_shape=[f32(OWN, ROWS, WIDTH)] + [f32(OWN, ROWS, LANES)] * (N_MEM - 1),
        compiler_params=params(20),
        cost_estimate=cost(6),
    )(mem, weights, early, rest)
    for x, (a, b), source in zip(analysis, PATHS[1:], sources[1:]):
        arrived = lax.ppermute(
            x, "mem", [(i, ((i // 2 + a) % 4) * 2 + (i + b) % 2) for i in range(N_MEM)]
        )
        result = place(arrived, source, result)
    return result


def solution(mesh):
    placed = (
        P("mem", "reg", None),
        P("reg", None),
        P("reg", None),
        P("reg", "mem"),
        P("reg", "mem"),
        P("reg", "mem"),
    )
    return jax.shard_map(
        local, mesh=mesh, in_specs=placed, out_specs=P("mem", "reg", None), check_vma=False
    )
```

time: 182 us -> 173 us (0.951)
  local copies, waits for them, and re-layouts: 11.9 us -> 3.07 us
  Pallas kernels: 53.3 us -> 45.7 us
  waiting for transfers between devices: 73.1 us -> 80.3 us
    pallas_call x1, Pallas kernels: 22.9 us -> 15.5 us  [local(): pl.pallas_call(interior_kernel, out_shape=[f32(GROUPS, ROWS - EDGE, OWN,...]
    unnamed x30 -> x18, local copies, waits for them, and re-layouts: 7.12 us -> 2.45 us
    slice x3 -> x0, local copies, waits for them, and re-layouts: 3.35 us -> none  [the longest x1 1.78 us: rows_out(): prior_samples[:, first:first + HALO]]
    pallas_call x1, Pallas kernels: 13.6 us -> 11.2 us  [local(): pl.pallas_call(edge_kernel, out_shape=[f32(N_MEM, OWN, HALF_OBS), f32(GRO...]
    all_to_all x1, waiting for transfers between devices: 0.84 us -> 3.31 us  [local(): early = lax.all_to_all(early, 'mem', 0, 0, tiled=True)]
    pallas_call x10, Pallas kernels: 15.7 us -> 18 us  [the longest x7 5.79 us: place(): pl.pallas_call(place_kernel, grid_spec=pltpu.PrefetchScalarGridSpec(num_s...]
    all_to_all x1, waiting for transfers between devices: 3.85 us -> 5.87 us  [local(): rest = lax.all_to_all(rest, 'mem', 0, 0, tiled=True)]
    ppermute x7, waiting for transfers between devices: 32 us -> 33.9 us  [local(): lax.ppermute(x, 'mem', [(i, (i // 2 + a) % 4 * 2 + (i + b) % 2) for i in...]
  transfers between devices with their start and end apart: 19 -> 19, of which waited for: 13 -> 13; matrix products, arithmetic and copies ran while one was open for 1% -> 1% of each run, Pallas kernels for 26% -> 21%
where the time goes in v4:
time: 173 us; the launch traced here: 172 us
  waiting for transfers between devices  80.3 us (46%)
  Pallas kernels  45.7 us (26%)
  starting transfers between devices  42.2 us (24%)
  local copies, waits for them, and re-layouts  3.07 us (2%)
    ppermute x7, waiting for transfers between devices, local(): lax.ppermute(x, 'mem', [(i, (i // 2 + a) % 4 * 2 + (i + b) % 2) for i in...  33.9 us
    ppermute x6, waiting for transfers between devices, swap(): return lax.ppermute(x, axis, [(i, i ^ bit) for i in range(count)])  22.1 us
    pallas_call x1, Pallas kernels, local(): pl.pallas_call(interior_kernel, out_shape=[f32(GROUPS, ROWS - EDGE, OWN,...  15.5 us
    all_to_all x1, waiting for transfers between devices, local(): lax.all_to_all(obs, 'mem', 0, 0, tiled=True).reshape(MEMBERS, HALF_OBS)  15.1 us
    pallas_call x1, Pallas kernels, local(): pl.pallas_call(edge_kernel, out_shape=[f32(N_MEM, OWN, HALF_OBS), f32(GRO...  11.2 us
    ppermute x7, starting transfers between devices, local(): lax.ppermute(x, 'mem', [(i, (i // 2 + a) % 4 * 2 + (i + b) % 2) for i in...  10.7 us
    all_to_all x1, waiting for transfers between devices, local(): rest = lax.all_to_all(rest, 'mem', 0, 0, tiled=True)  5.87 us
    pallas_call x7, Pallas kernels, place(): pl.pallas_call(place_kernel, grid_spec=pltpu.PrefetchScalarGridSpec(num_s...  5.79 us
  transfers between devices with their start and end apart: 19, of which 13 were waited for; matrix products, arithmetic and copies ran while one was open for 1% of the time, Pallas kernels for 21%

profile of v4, /device:TPU:1, one launch (start us, length us, event | category | flops | bytes accessed | tf_op | source)
XLA Modules:
  0.0 172.1 jit_solution(5092922398287756341)
XLA Ops:
  0.0 4.0 %shard_map.64 = (f32[4,40,1024]{2,1,0:T(8,128)}, f32[4,40,1024]{2,1,0:T(8,128)}) custom-call(s32[1]{0:T(128)} %bitcast.3.parity_ref, f32[32,32,1024]{2,1,0:T(8,128)} %prior_ref.1, f32[32,1024]{1,0:T(8,128)} %h_ref.3, f32[32,1024]{1,0:T(8,128)} %v_ref.3), custom_call_target="tpu_custom_call" | custom-call | tf_op jit(solution)/shard_map/pallas_call | solution.py:371
  6.6 4.7 %collective-permute-start.1 = (f32[4,40,1024]{2,1,0:T(8,128)}, f32[4,40,1024]{2,1,0:T(8,128)S(1)}, u32[]{:S(2)}, u32[]{:S(2)}) collective-permute-start(f32[4,40,1024]{2,1,0:T(8,128)} %get-tuple-element.41), channel_id=1, source_target_pairs={{0,15},{1,2},{2,1},{3,4},{4,3},{5,6},{6,5},{7,8},{8,7},{9,10},{10,... | collective-permute-start | bytes 1966088 | tf_op jit(solution)/shard_map/ppermute | solution.py:386
  11.9 5.5 %all-to-all-start.1 = ((f32[8,3,256]{2,1,0:T(4,128)}), f32[8,3,256]{2,1,0:T(4,128)S(1)}, u32[]{:S(2)}, u32[]{:S(2)}) async-start(f32[8,3,256]{2,1,0:T(4,128)} %broadcast_in_dim.2), calls=%async_computation.1 | async-start | bytes 65536 | tf_op jit(solution)/shard_map/all_to_all | solution.py:391
  17.5 15.5 %shard_map.65 = (f32[8,24,32,128]{3,2,1,0:T(8,128)}, f32[8,8,32,128]{3,2,1,0:T(8,128)}, f32[2,8,32,1024]{3,2,1,0:T(8,128)}) custom-call(f32[1024,1024]{1,0:T(8,128)} %bitcast.19, f32[32,1024]{1,0:T(8,128)} %h_ref.3, f32[32,1024]{1,0:T(8,128)} %v_ref.3), custom_call_target="tpu_custom_call" | custom-call | bytes 51000000 | tf_op jit(solution)/shard_map/pallas_call | solution.py:399
  33.0 4.8 %all-to-all-start = ((f32[8,8,32,128]{3,2,1,0:T(8,128)}), f32[8,8,32,128]{3,2,1,0:T(8,128)S(1)}, u32[]{:S(2)}, u32[]{:S(2)}) async-start(f32[8,8,32,128]{3,2,1,0:T(8,128)} %get-tuple-element.42), calls=%async_computation | async-start | bytes 2097152 | tf_op jit(solution)/shard_map/all_to_all | solution.py:421
  38.4 11.2 %shard_map.66 = (f32[8,32,1024]{2,1,0:T(8,128)}, f32[8,24,32,128]{3,2,1,0:T(8,128)}) custom-call(s32[1]{0:T(128)} %bitcast.3.parity_ref, f32[8,24,32,128]{3,2,1,0:T(8,128)} %get-tuple-element.43.inner_ref, f32[2,8,32,1024]{3,2,1,0:T(8,128)} %get-tuple-element.44.rim_ref, f32[4,40,1024]{2,1,0:T(8,128)} %copy-done.4, f32[4,40,1024]{2,1,0:T(8,128)} %copy-done.5, ...), custom_call_target="tpu_custom_call" | custom-call | bytes 39000000 | tf_op jit(solution)/shard_map/pallas_call | solution.py:422
  49.6 3.3 %all-to-all-done.early_ref = f32[8,8,32,128]{3,2,1,0:T(8,128)S(1)} async-done(((f32[8,8,32,128]{3,2,1,0:T(8,128)}), f32[8,8,32,128]{3,2,1,0:T(8,128)S(1)}, u32[]{:S(2)}, u32[]{:S(2)}) %all-to-all-start) | async-done | bytes 1048608 | tf_op jit(solution)/shard_map/all_to_all | solution.py:421
  52.9 4.3 %all-to-all-start.2 = ((f32[8,32,1024]{2,1,0:T(8,128)}), f32[8,32,1024]{2,1,0:T(8,128)S(1)}, u32[]{:S(2)}, u32[]{:S(2)}) async-start(f32[8,32,1024]{2,1,0:T(8,128)} %get-tuple-element.48), calls=%async_computation.2 | async-start | bytes 2097152 | tf_op jit(solution)/shard_map/all_to_all | solution.py:442
  57.2 15.1 %all-to-all-done.2 = f32[8,32,1024]{2,1,0:T(8,128)S(1)} async-done(((f32[8,32,1024]{2,1,0:T(8,128)}), f32[8,32,1024]{2,1,0:T(8,128)S(1)}, u32[]{:S(2)}, u32[]{:S(2)}) %all-to-all-start.2) | async-done | bytes 1048608 | tf_op jit(solution)/shard_map/all_to_all | solution.py:442
  73.4 4.4 %all-to-all-start.3 = ((f32[8,24,32,128]{3,2,1,0:T(8,128)}), f32[8,24,32,128]{3,2,1,0:T(8,128)S(1)}, u32[]{:S(2)}, u32[]{:S(2)}) async-start(f32[8,24,32,128]{3,2,1,0:T(8,128)} %get-tuple-element.54), calls=%async_computation.3 | async-start | bytes 6291456 | tf_op jit(solution)/shard_map/all_to_all | solution.py:453
  79.5 4.9 %collective-permute-done.3 = f32[136,256]{1,0:T(8,128)S(1)} collective-permute-done((f32[136,256]{1,0:T(8,128)S(1)}, f32[136,256]{1,0:T(8,128)S(1)}, u32[]{:S(2)}, u32[]{:S(2)}) %collective-permute-start.3) | collective-permute-done | bytes 139296 | tf_op jit(solution)/shard_map/ppermute | solution.py:355
  84.5 5.7 %collective-permute-done.4 = f32[136,256]{1,0:T(8,128)S(1)} collective-permute-done((f32[136,256]{1,0:T(8,128)S(1)}, f32[136,256]{1,0:T(8,128)S(1)}, u32[]{:S(2)}, u32[]{:S(2)}) %collective-permute-start.4) | collective-permute-done | bytes 139296 | tf_op jit(solution)/shard_map/ppermute | solution.py:355
  90.3 4.2 %collective-permute-done.5 = f32[136,256]{1,0:T(8,128)S(1)} collective-permute-done((f32[136,256]{1,0:T(8,128)S(1)}, f32[136,256]{1,0:T(8,128)S(1)}, u32[]{:S(2)}, u32[]{:S(2)}) %collective-permute-start.5) | collective-permute-done | bytes 139296 | tf_op jit(solution)/shard_map/ppermute | solution.py:355
  94.9 5.1 %collective-permute-done.6 = f32[136,256]{1,0:T(8,128)S(1)} collective-permute-done((f32[136,256]{1,0:T(8,128)S(1)}, f32[136,256]{1,0:T(8,128)S(1)}, u32[]{:S(2)}, u32[]{:S(2)}) %collective-permute-start.6) | collective-permute-done | bytes 139296 | tf_op jit(solution)/shard_map/ppermute | solution.py:355
  100.0 4.3 %collective-permute-start.7 = (f32[136,256]{1,0:T(8,128)S(1)}, f32[136,256]{1,0:T(8,128)S(1)}, u32[]{:S(2)}, u32[]{:S(2)}) collective-permute-start(f32[136,256]{1,0:T(8,128)S(1)} %add.100.mine_ref), channel_id=1, source_target_pairs={{0,16},{16,0},{32,48},{48,32},{64,80},{80,64},{96,112},{112,96},{1... | collective-permute-start | bytes 417800 | tf_op jit(solution)/shard_map/ppermute | solution.py:355
  105.3 4.3 %shard_map.68.weights_ref = bf16[512,256]{1,0:T(8,128)(2,1)S(1)} custom-call(s32[1]{0:T(128)} %bitcast.1.mem_ref, f32[136,256]{1,0:T(8,128)S(1)} %add.100.mine_ref, f32[136,256]{1,0:T(8,128)S(1)} %collective-permute-done.7.other_ref), custom_call_target="tpu_custom_call" | custom-call | bytes 18000000 | tf_op jit(solution)/shard_map/pallas_call | solution.py:459
  109.6 5.9 %all-to-all-done.3.rest_ref = f32[8,24,32,128]{3,2,1,0:T(8,128)S(1)} async-done(((f32[8,24,32,128]{3,2,1,0:T(8,128)}), f32[8,24,32,128]{3,2,1,0:T(8,128)S(1)}, u32[]{:S(2)}, u32[]{:S(2)}) %all-to-all-start.3) | async-done | bytes 3145760 | tf_op jit(solution)/shard_map/all_to_all | solution.py:453
  116.7 3.9 %shard_map.69 = (f32[32,32,1024]{2,1,0:T(8,128)}, f32[32,32,128]{2,1,0:T(8,128)S(1)}, f32[32,32,128]{2,1,0:T(8,128)S(1)}, f32[32,32,128]{2,1,0:T(8,128)}, f32[32...) custom-call(s32[1]{0:T(128)} %bitcast.1.mem_ref, ...), custom_call_target="tpu_custom_call" | custom-call | bytes 18000000 | tf_op jit(solution)/shard_map/pallas_call | solution.py:470
  123.6 3.1 %collective-permute-start.11 = (f32[32,32,128]{2,1,0:T(8,128)}, f32[32,32,128]{2,1,0:T(8,128)S(1)}, u32[]{:S(2)}, u32[]{:S(2)}) collective-permute-start(f32[32,32,128]{2,1,0:T(8,128)} %get-tuple-element.58), channel_id=1, source_target_pairs={{0,80},{16,64},{32,112},{48,96},{64,16},{80,0},{96,48},{112,32},{1... | collective-permute-start | bytes 1572872 | tf_op jit(solution)/shard_map/ppermute | solution.py:488
  126.6 8.1 %collective-permute-done.14.x_ref = f32[32,32,128]{2,1,0:T(8,128)S(1)} collective-permute-done((f32[32,32,128]{2,1,0:T(8,128)S(1)}, f32[32,32,128]{2,1,0:T(8,128)S(1)}, u32[]{:S(2)}, u32[]{:S(2)}) %collective-permute-start.14) | collective-permute-done | bytes 524320 | tf_op jit(solution)/shard_map/ppermute | solution.py:488
  134.8 3.9 %collective-permute-start.9 = (f32[32,32,128]{2,1,0:T(8,128)}, f32[32,32,128]{2,1,0:T(8,128)S(1)}, u32[]{:S(2)}, u32[]{:S(2)}) collective-permute-start(f32[32,32,128]{2,1,0:T(8,128)} %get-tuple-element.56), channel_id=1, source_target_pairs={{0,112},{16,96},{32,16},{48,0},{64,48},{80,32},{96,80},{112,64},{1... | collective-permute-start | bytes 1572872 | tf_op jit(solution)/shard_map/ppermute | solution.py:488
  138.6 9.7 %collective-permute-done.13.x_ref = f32[32,32,128]{2,1,0:T(8,128)S(1)} collective-permute-done((f32[32,32,128]{2,1,0:T(8,128)S(1)}, f32[32,32,128]{2,1,0:T(8,128)S(1)}, u32[]{:S(2)}, u32[]{:S(2)}) %collective-permute-start.13) | collective-permute-done | bytes 524320 | tf_op jit(solution)/shard_map/ppermute | solution.py:488
  152.8 6.8 %collective-permute-done.11.x_ref = f32[32,32,128]{2,1,0:T(8,128)S(1)} collective-permute-done((f32[32,32,128]{2,1,0:T(8,128)}, f32[32,32,128]{2,1,0:T(8,128)S(1)}, u32[]{:S(2)}, u32[]{:S(2)}) %collective-permute-start.11) | collective-permute-done | bytes 524320 | tf_op jit(solution)/shard_map/ppermute | solution.py:488
  160.5 9.2 %collective-permute-done.10.x_ref = f32[32,32,128]{2,1,0:T(8,128)S(1)} collective-permute-done((f32[32,32,128]{2,1,0:T(8,128)}, f32[32,32,128]{2,1,0:T(8,128)S(1)}, u32[]{:S(2)}, u32[]{:S(2)}) %collective-permute-start.10) | collective-permute-done | bytes 524320 | tf_op jit(solution)/shard_map/ppermute | solution.py:488
  (56 shorter events, 20.2 us)
Async XLA Ops:
  0.0 11.3 %copy-start.8 = (s32[1,256]{1,0:T(1,128)S(1)}, s32[1,256]{1,0:T(1,128)}, u32[]{:S(2)}) copy-start(s32[1,256]{1,0:T(1,128)} %param.9) | copy-start | bytes 3076
  0.0 11.3 %copy-start.7 = (f32[1,256]{1,0:T(1,128)S(1)}, f32[1,256]{1,0:T(1,128)}, u32[]{:S(2)}) copy-start(f32[1,256]{1,0:T(1,128)} %param.10) | copy-start | bytes 3076
  0.0 11.3 %copy-start.6 = (f32[1,256]{1,0:T(1,128)S(1)}, f32[1,256]{1,0:T(1,128)}, u32[]{:S(2)}) copy-start(f32[1,256]{1,0:T(1,128)} %param.11) | copy-start | bytes 3076
  4.1 28.9 %collective-permute-start = (f32[4,40,1024]{2,1,0:T(8,128)}, f32[4,40,1024]{2,1,0:T(8,128)S(1)}, u32[]{:S(2)}, u32[]{:S(2)}) collective-permute-start(f32[4,40,1024]{2,1,0:T(8,128)} %get-tuple-element.40), channel_id=1, source_target_pairs={{0,1},{1,0},{2,3},{3,2},{4,5},{5,4},{6,7},{7,6},{8,9},{9,8},{10,11... | collective-permute-start | bytes 1966088 | tf_op jit(solution)/shard_map/ppermute | solution.py:385
  6.6 26.4 %collective-permute-start.1 = (f32[4,40,1024]{2,1,0:T(8,128)}, f32[4,40,1024]{2,1,0:T(8,128)S(1)}, u32[]{:S(2)}, u32[]{:S(2)}) collective-permute-start(f32[4,40,1024]{2,1,0:T(8,128)} %get-tuple-element.41), channel_id=1, source_target_pairs={{0,15},{1,2},{2,1},{3,4},{4,3},{5,6},{6,5},{7,8},{8,7},{9,10},{10,... | collective-permute-start | bytes 1966088 | tf_op jit(solution)/shard_map/ppermute | solution.py:386
  11.9 21.0 %all-to-all-start.1 = ((f32[8,3,256]{2,1,0:T(4,128)}), f32[8,3,256]{2,1,0:T(4,128)S(1)}, u32[]{:S(2)}, u32[]{:S(2)}) async-start(f32[8,3,256]{2,1,0:T(4,128)} %broadcast_in_dim.2), calls=%async_computation.1 | async-start | bytes 65536 | tf_op jit(solution)/shard_map/all_to_all | solution.py:391
  32.9 5.5 %copy-start.4 = (f32[4,40,1024]{2,1,0:T(8,128)}, f32[4,40,1024]{2,1,0:T(8,128)S(1)}, u32[]{:S(2)}) copy-start(f32[4,40,1024]{2,1,0:T(8,128)S(1)} %collective-permute-done.a_ref) | copy-start | bytes 1966084
  33.0 19.9 %all-to-all-start = ((f32[8,8,32,128]{3,2,1,0:T(8,128)}), f32[8,8,32,128]{3,2,1,0:T(8,128)S(1)}, u32[]{:S(2)}, u32[]{:S(2)}) async-start(f32[8,8,32,128]{3,2,1,0:T(8,128)} %get-tuple-element.42), calls=%async_computation | async-start | bytes 2097152 | tf_op jit(solution)/shard_map/all_to_all | solution.py:421
  52.9 20.5 %copy-start = (f32[8,8,32,128]{3,2,1,0:T(8,128)}, f32[8,8,32,128]{3,2,1,0:T(8,128)S(1)}, u32[]{:S(2)}) copy-start(f32[8,8,32,128]{3,2,1,0:T(8,128)S(1)} %all-to-all-done.early_ref) | copy-start | bytes 3145732
  52.9 19.4 %all-to-all-start.2 = ((f32[8,32,1024]{2,1,0:T(8,128)}), f32[8,32,1024]{2,1,0:T(8,128)S(1)}, u32[]{:S(2)}, u32[]{:S(2)}) async-start(f32[8,32,1024]{2,1,0:T(8,128)} %get-tuple-element.48), calls=%async_computation.2 | async-start | bytes 2097152 | tf_op jit(solution)/shard_map/all_to_all | solution.py:442
  73.4 42.0 %all-to-all-start.3 = ((f32[8,24,32,128]{3,2,1,0:T(8,128)}), f32[8,24,32,128]{3,2,1,0:T(8,128)S(1)}, u32[]{:S(2)}, u32[]{:S(2)}) async-start(f32[8,24,32,128]{3,2,1,0:T(8,128)} %get-tuple-element.54), calls=%async_computation.3 | async-start | bytes 6291456 | tf_op jit(solution)/shard_map/all_to_all | solution.py:453
  77.8 1.5 collective-permute-start.2
  79.4 5.0 %collective-permute-start.3 = (f32[136,256]{1,0:T(8,128)S(1)}, f32[136,256]{1,0:T(8,128)S(1)}, u32[]{:S(2)}, u32[]{:S(2)}) collective-permute-start(f32[136,256]{1,0:T(8,128)S(1)} %add.96), channel_id=1, source_target_pairs={{0,1},{1,0},{2,3},{3,2},{4,5},{5,4},{6,7},{7,6},{8,9},{9,8},{10,11... | collective-permute-start | bytes 417800 | tf_op jit(solution)/shard_map/ppermute | solution.py:355
  84.4 5.8 %collective-permute-start.4 = (f32[136,256]{1,0:T(8,128)S(1)}, f32[136,256]{1,0:T(8,128)S(1)}, u32[]{:S(2)}, u32[]{:S(2)}) collective-permute-start(f32[136,256]{1,0:T(8,128)S(1)} %add.97), channel_id=1, source_target_pairs={{0,2},{1,3},{2,0},{3,1},{4,6},{5,7},{6,4},{7,5},{8,10},{9,11},{10,... | collective-permute-start | bytes 417800 | tf_op jit(solution)/shard_map/ppermute | solution.py:355
  90.2 4.3 %collective-permute-start.5 = (f32[136,256]{1,0:T(8,128)S(1)}, f32[136,256]{1,0:T(8,128)S(1)}, u32[]{:S(2)}, u32[]{:S(2)}) collective-permute-start(f32[136,256]{1,0:T(8,128)S(1)} %add.98), channel_id=1, source_target_pairs={{0,4},{1,5},{2,6},{3,7},{4,0},{5,1},{6,2},{7,3},{8,12},{9,13},{10,... | collective-permute-start | bytes 417800 | tf_op jit(solution)/shard_map/ppermute | solution.py:355
  94.5 5.5 %collective-permute-start.6 = (f32[136,256]{1,0:T(8,128)S(1)}, f32[136,256]{1,0:T(8,128)S(1)}, u32[]{:S(2)}, u32[]{:S(2)}) collective-permute-start(f32[136,256]{1,0:T(8,128)S(1)} %add.99), channel_id=1, source_target_pairs={{0,8},{1,9},{2,10},{3,11},{4,12},{5,13},{6,14},{7,15},{8,0},{9,1},... | collective-permute-start | bytes 417800 | tf_op jit(solution)/shard_map/ppermute | solution.py:355
  100.0 5.3 %collective-permute-start.7 = (f32[136,256]{1,0:T(8,128)S(1)}, f32[136,256]{1,0:T(8,128)S(1)}, u32[]{:S(2)}, u32[]{:S(2)}) collective-permute-start(f32[136,256]{1,0:T(8,128)S(1)} %add.100.mine_ref), channel_id=1, source_target_pairs={{0,16},{16,0},{32,48},{48,32},{64,80},{80,64},{96,112},{112,96},{1... | collective-permute-start | bytes 417800 | tf_op jit(solution)/shard_map/ppermute | solution.py:355
  120.6 14.2 %collective-permute-start.14 = (f32[32,32,128]{2,1,0:T(8,128)S(1)}, f32[32,32,128]{2,1,0:T(8,128)S(1)}, u32[]{:S(2)}, u32[]{:S(2)}) collective-permute-start(f32[32,32,128]{2,1,0:T(8,128)S(1)} %get-tuple-element.61), channel_id=1, source_target_pairs={{0,64},{16,80},{32,96},{48,112},{64,0},{80,16},{96,32},{112,48},{1... | collective-permute-start | bytes 1572872 | tf_op jit(solution)/shard_map/ppermute | solution.py:488
  120.9 27.4 %collective-permute-start.13 = (f32[32,32,128]{2,1,0:T(8,128)S(1)}, f32[32,32,128]{2,1,0:T(8,128)S(1)}, u32[]{:S(2)}, u32[]{:S(2)}) collective-permute-start(f32[32,32,128]{2,1,0:T(8,128)S(1)} %get-tuple-element.60), channel_id=1, source_target_pairs={{0,32},{16,48},{32,64},{48,80},{64,96},{80,112},{96,0},{112,16},{1... | collective-permute-start | bytes 1572872 | tf_op jit(solution)/shard_map/ppermute | solution.py:488
  122.1 29.9 %collective-permute-start.12 = (f32[32,32,128]{2,1,0:T(8,128)}, f32[32,32,128]{2,1,0:T(8,128)S(1)}, u32[]{:S(2)}, u32[]{:S(2)}) collective-permute-start(f32[32,32,128]{2,1,0:T(8,128)} %get-tuple-element.59), channel_id=1, source_target_pairs={{0,96},{16,112},{32,0},{48,16},{64,32},{80,48},{96,64},{112,80},{1... | collective-permute-start | bytes 1572872 | tf_op jit(solution)/shard_map/ppermute | solution.py:488
  123.6 36.1 %collective-permute-start.11 = (f32[32,32,128]{2,1,0:T(8,128)}, f32[32,32,128]{2,1,0:T(8,128)S(1)}, u32[]{:S(2)}, u32[]{:S(2)}) collective-permute-start(f32[32,32,128]{2,1,0:T(8,128)} %get-tuple-element.58), channel_id=1, source_target_pairs={{0,80},{16,64},{32,112},{48,96},{64,16},{80,0},{96,48},{112,32},{1... | collective-permute-start | bytes 1572872 | tf_op jit(solution)/shard_map/ppermute | solution.py:488
  126.6 43.0 %collective-permute-start.10 = (f32[32,32,128]{2,1,0:T(8,128)}, f32[32,32,128]{2,1,0:T(8,128)S(1)}, u32[]{:S(2)}, u32[]{:S(2)}) collective-permute-start(f32[32,32,128]{2,1,0:T(8,128)} %get-tuple-element.57), channel_id=1, source_target_pairs={{0,48},{16,32},{32,80},{48,64},{64,112},{80,96},{96,16},{112,0},{1... | collective-permute-start | bytes 1572872 | tf_op jit(solution)/shard_map/ppermute | solution.py:488
  134.8 35.7 %collective-permute-start.9 = (f32[32,32,128]{2,1,0:T(8,128)}, f32[32,32,128]{2,1,0:T(8,128)S(1)}, u32[]{:S(2)}, u32[]{:S(2)}) collective-permute-start(f32[32,32,128]{2,1,0:T(8,128)} %get-tuple-element.56), channel_id=1, source_target_pairs={{0,112},{16,96},{32,16},{48,0},{64,48},{80,32},{96,80},{112,64},{1... | collective-permute-start | bytes 1572872 | tf_op jit(solution)/shard_map/ppermute | solution.py:488
  149.1 22.2 %collective-permute-start.8 = (f32[32,32,128]{2,1,0:T(8,128)}, f32[32,32,128]{2,1,0:T(8,128)S(1)}, u32[]{:S(2)}, u32[]{:S(2)}) collective-permute-start(f32[32,32,128]{2,1,0:T(8,128)} %get-tuple-element.55), channel_id=1, source_target_pairs={{0,16},{16,0},{32,48},{48,32},{64,80},{80,64},{96,112},{112,96},{1... | collective-permute-start | bytes 1572872 | tf_op jit(solution)/shard_map/ppermute | solution.py:488
  (4 other events, 8.7 us)

commit v5 on v4

--- a/solution.py
+++ b/solution.py
@@ -185,8 +185,8 @@
 
 
 def edge_kernel(
-    parity_ref, inner_ref, rim_ref, a_ref, b_ref, h_ref, v_ref, index_ref,
-    obs_ref, rest_ref, field, one, two, coef_ref, in_sem, out_sems,
+    parity_ref, core_ref, inner_ref, rim_ref, a_ref, b_ref, h_ref, v_ref, index_ref,
+    same_ref, flip_ref, rest_ref, obs_ref, field, one, two, coef_ref, in_sem, out_sems,
 ):
     load = pltpu.make_async_copy(inner_ref, field.at[:, HALO : ROWS - HALO], in_sem)
     load.start()
@@ -233,13 +233,20 @@
                 x = jnp.take_along_axis(field[g, i], col, axis=1, mode="promise_in_bounds")
                 total = jnp.where(row == i, x, total)
             at = (g % 4) * OBS + t * LANES
-            for x in range(N_MEM // 2):
-                obs_ref[2 * x + g // 4, :, at : at + LANES] = total
+            obs_ref[lax.rem(core_ref[0] + g // 4, 2), :, at : at + LANES] = total
+    same_ref[...] = obs_ref[0]
+    flip_ref[...] = obs_ref[1]
     for store in stores:
         store.wait()
 
 
-def gram_kernel(core_ref, obs_ref, value_ref, weight_ref, keep_ref, send_ref):
+def gram_kernel(mem_ref, *refs):
+    *from_refs, value_ref, weight_ref, keep_ref, send_ref, obs_ref = refs
+    mem = mem_ref[0]
+    core = lax.rem(mem, 2)
+    for (a, b), ref in zip(PATHS, from_refs):
+        source = lax.rem(mem // 2 + 4 - a, 4) * 2 + lax.rem(core + b, 2)
+        obs_ref[pl.ds(pl.multiple_of(source * OWN, OWN), OWN), :] = ref[...]
     obs = obs_ref[...]
     mean = jnp.sum(obs, axis=0, keepdims=True) * (1.0 / MEMBERS)
     anomalies = obs - mean
@@ -248,7 +255,6 @@
     nt = (((1,), (1,)), ((), ()))
     gram = dot3(split(anomalies), weighted, nt)
     drive = dot3(split(innovation), weighted, nt)
-    core = core_ref[0]
     half = MEMBERS // 2
     for c in range(2):
 
@@ -300,27 +306,65 @@
         out_ref[MEMBERS + n * OWN : MEMBERS + (n + 1) * OWN] = low
 
 
-def product_kernel(mem_ref, weights_ref, early_ref, rest_ref, *out_refs):
-    weights = (weights_ref[:MEMBERS], weights_ref[MEMBERS:])
-    flat = [ref.reshape(OWN * CHUNK, LANES) for ref in out_refs]
-
-    def rows(ref):
+def product_kernel(mem_ref, weights_ref, x_ref, *refs):
+    members = refs[-1].shape[0]
+
+    def compute(out_refs):
+        weights = (weights_ref[:MEMBERS], weights_ref[MEMBERS:])
+        flat = [ref.reshape(members * CHUNK, LANES) for ref in out_refs]
         for half in range(0, CHUNK, HALO):
             parts = [
-                split(jnp.concatenate([ref[s, half + t] for s in range(N_MEM)], axis=0))
+                split(jnp.concatenate([x_ref[s, half + t] for s in range(N_MEM)], axis=0))
                 for t in range(HALO)
             ]
             x = tuple(jnp.concatenate([p[n] for p in parts], axis=1) for n in range(2))
             y = dot3(weights, x)
             for t in range(HALO):
-                for n in range(N_MEM):
-                    flat[n][pl.ds(half + t, OWN, stride=CHUNK), :] = y[
-                        n * OWN : (n + 1) * OWN, t * LANES : (t + 1) * LANES
+                for n, ref in enumerate(flat):
+                    ref[pl.ds(half + t, members, stride=CHUNK), :] = y[
+                        n * members : (n + 1) * members, t * LANES : (t + 1) * LANES
                     ]
 
-    step = pl.program_id(0)
-    pl.when(step == 1)(lambda: rows(early_ref))
-    pl.when(step != 1)(lambda: rows(rest_ref))
+    if len(refs) == 1:
+        compute(refs)
+    else:
+        step = pl.program_id(0)
+
+        @pl.when(step == 1)
+        def _():
+            for n, ref in enumerate(refs[1:]):
+                ref[...] = refs[0][n * OWN : (n + 1) * OWN]
+
+        pl.when(step != 1)(lambda: compute(refs[1:]))
+
+
+def product(mem, weights, x, done):
+    early = pl.BlockSpec((MEMBERS, CHUNK, LANES), lambda n, g: (0, 0, 0))
+    outs = [pl.BlockSpec((OWN, CHUNK, LANES), lambda n, g: (0, n, 0))] * (N_MEM - 1)
+    if done:
+        own = pl.BlockSpec((OWN, CHUNK, LANES), lambda n, g: (0, n, g[0]))
+        shapes = [f32(OWN, ROWS, WIDTH)] + [f32(OWN, ROWS, LANES)] * (N_MEM - 1)
+        grid = (ROWS // CHUNK,)
+    else:
+        own, outs, shapes, grid = early, [], [f32(MEMBERS, CHUNK, LANES)], (1,)
+    return pl.pallas_call(
+        product_kernel,
+        grid_spec=pltpu.PrefetchScalarGridSpec(
+            num_scalar_prefetch=1,
+            grid=grid,
+            in_specs=[
+                pl.BlockSpec((2 * MEMBERS, MEMBERS), lambda n, g: (0, 0)),
+                pl.BlockSpec(
+                    (N_MEM, CHUNK, OWN, LANES), lambda n, g: (0, jnp.maximum(n - 1, 0), 0, 0)
+                ),
+            ]
+            + [early] * len(done),
+            out_specs=[own] + outs,
+        ),
+        out_shape=shapes,
+        compiler_params=params(20),
+        cost_estimate=cost(4 if done else 2),
+    )(mem, weights, x, *done)
 
 
 def place_kernel(group_ref, x_ref, before_ref, out_ref):
@@ -350,6 +394,12 @@
     return jax.ShapeDtypeStruct(shape, jnp.float32)
 
 
+def send_on(x, a, b):
+    return lax.ppermute(
+        x, "mem", [(i, ((i // 2 + a) % 4) * 2 + (i + b) % 2) for i in range(N_MEM)]
+    )
+
+
 def swap(x, axis, bit):
     count = lax.axis_size(axis)
     return lax.ppermute(x, axis, [(i, i ^ bit) for i in range(count)])
@@ -382,10 +432,10 @@
     halo_a, halo_b, prior_samples, h, v = lax.optimization_barrier(
         (halo_a, halo_b, prior_samples, h, v)
     )
-    halo_a = lax.ppermute(halo_a, "reg", [(i, i ^ 1) for i in range(N_REG)])
     halo_b = lax.ppermute(
         halo_b, "reg", [(i, (i - 1 if i % 2 == 0 else i + 1) % N_REG) for i in range(N_REG)]
     )
+    halo_a = lax.ppermute(halo_a, "reg", [(i, i ^ 1) for i in range(N_REG)])
 
     facts = jnp.concatenate([obs_index.astype(jnp.float32), obs_value, obs_weight], axis=0)
     facts = lax.all_to_all(
@@ -419,15 +469,17 @@
     )(prior_samples.reshape(OWN * ROWS, WIDTH), h, v)
     early, halo_a, halo_b = lax.optimization_barrier((early, halo_a, halo_b))
     early = lax.all_to_all(early, "mem", 0, 0, tiled=True)
-    obs, rest = pl.pallas_call(
+    same, flip, rest = pl.pallas_call(
         edge_kernel,
         out_shape=[
-            f32(N_MEM, OWN, HALF_OBS),
+            f32(OWN, HALF_OBS),
+            f32(OWN, HALF_OBS),
             f32(GROUPS, ROWS - CHUNK, OWN, LANES),
         ],
-        in_specs=[SMEM, anywhere] + [VMEM] * 6,
-        out_specs=[VMEM, anywhere],
+        in_specs=[SMEM, SMEM, anywhere] + [VMEM] * 6,
+        out_specs=[VMEM, VMEM, anywhere],
         scratch_shapes=[
+            pltpu.VMEM((2, OWN, HALF_OBS), jnp.float32),
             pltpu.VMEM((GROUPS, ROWS, OWN, LANES), jnp.float32),
             pltpu.VMEM((HALO + EDGE, OWN, WIDTH), jnp.float32),
             pltpu.VMEM((HALO + EDGE, OWN, WIDTH), jnp.float32),
@@ -437,18 +489,19 @@
         ],
         compiler_params=params(56),
         cost_estimate=cost(13),
-    )(parity, inner, rim, halo_a, halo_b, h, v, index)
-    early, obs = lax.optimization_barrier((early, obs))
-    obs = lax.all_to_all(obs, "mem", 0, 0, tiled=True).reshape(MEMBERS, HALF_OBS)
+    )(parity, core, inner, rim, halo_a, halo_b, h, v, index)
+    obs = [same] + [send_on(flip if b else same, a, b) for a, b in PATHS[1:]]
+    early, *obs = lax.optimization_barrier((early, *obs))
 
     keep, send = pl.pallas_call(
         gram_kernel,
         out_shape=[f32(MEMBERS // 2 + 8, MEMBERS)] * 2,
-        in_specs=[SMEM, VMEM, VMEM, VMEM],
+        in_specs=[SMEM] + [VMEM] * (N_MEM + 2),
         out_specs=[VMEM, VMEM],
+        scratch_shapes=[pltpu.VMEM((MEMBERS, HALF_OBS), jnp.float32)],
         compiler_params=params(12),
         cost_estimate=cost(3),
-    )(core, obs, value, weight)
+    )(mem, *obs, value, weight)
     rest, send = lax.optimization_barrier((rest, send))
     rest = lax.all_to_all(rest, "mem", 0, 0, tiled=True)
     total = keep + swap(send, "mem", 1)
@@ -466,28 +519,10 @@
         cost_estimate=cost(6),
     )(mem, total, other)
 
-    block = (N_MEM, CHUNK, OWN, LANES)
-    result, *analysis = pl.pallas_call(
-        product_kernel,
-        grid_spec=pltpu.PrefetchScalarGridSpec(
-            num_scalar_prefetch=1,
-            grid=(ROWS // CHUNK,),
-            in_specs=[
-                pl.BlockSpec((2 * MEMBERS, MEMBERS), lambda n, g: (0, 0)),
-                pl.BlockSpec(block, lambda n, g: (0, 0, 0, 0)),
-                pl.BlockSpec(block, lambda n, g: (0, jnp.maximum(n - 1, 0), 0, 0)),
-            ],
-            out_specs=[pl.BlockSpec((OWN, CHUNK, LANES), lambda n, g: (0, n, g[0]))]
-            + [pl.BlockSpec((OWN, CHUNK, LANES), lambda n, g: (0, n, 0))] * (N_MEM - 1),
-        ),
-        out_shape=[f32(OWN, ROWS, WIDTH)] + [f32(OWN, ROWS, LANES)] * (N_MEM - 1),
-        compiler_params=params(20),
-        cost_estimate=cost(6),
-    )(mem, weights, early, rest)
+    analysis = product(mem, weights, early, [])
+    result, *analysis = product(mem, weights, rest, analysis)
     for x, (a, b), source in zip(analysis, PATHS[1:], sources[1:]):
-        arrived = lax.ppermute(
-            x, "mem", [(i, ((i // 2 + a) % 4) * 2 + (i + b) % 2) for i in range(N_MEM)]
-        )
+        arrived = send_on(x, a, b)
         result = place(arrived, source, result)
     return result
 

time: 173 us -> 168 us (0.971)
  waiting for transfers between devices: 80.3 us -> 64.8 us
  starting transfers between devices: 42.2 us -> 48.1 us
  local copies, waits for them, and re-layouts: 3.07 us -> 6.32 us
    all_to_all x1 -> x0, waiting for transfers between devices: 15.1 us -> none  [local(): lax.all_to_all(obs, 'mem', 0, 0, tiled=True).reshape(MEMBERS, HALF_OBS)]
    ppermute x7 -> x14, starting transfers between devices: 10.7 us -> 21.3 us  [send_on(): lax.ppermute(x, 'mem', [(i, (i // 2 + a) % 4 * 2 + (i + b) % 2) for i in...]
    ppermute x7 -> x14, waiting for transfers between devices: 33.9 us -> 39.2 us  [send_on(): lax.ppermute(x, 'mem', [(i, (i // 2 + a) % 4 * 2 + (i + b) % 2) for i in...]
    all_to_all x1 -> x0, starting transfers between devices: 4.33 us -> none  [local(): lax.all_to_all(obs, 'mem', 0, 0, tiled=True).reshape(MEMBERS, HALF_OBS)]
    all_to_all x1, waiting for transfers between devices: 3.31 us -> 0.01 us  [local(): early = lax.all_to_all(early, 'mem', 0, 0, tiled=True)]
    unnamed x18 -> x24, local copies, waits for them, and re-layouts: 2.45 us -> 5.69 us
    all_to_all x1, waiting for transfers between devices: 5.87 us -> 3.28 us  [local(): rest = lax.all_to_all(rest, 'mem', 0, 0, tiled=True)]
    pallas_call x2 -> x3, Pallas kernels: 15.1 us -> 16.4 us  [the longest x1 11.8 us: local(): pl.pallas_call(edge_kernel, out_shape=[f32(OWN, HALF_OBS), f32(OWN, HALF_...]
  transfers between devices with their start and end apart: 19 -> 25, of which waited for: 13 -> 14; matrix products, arithmetic and copies ran while one was open for 1% -> 1% of each run, Pallas kernels for 21% -> 22%
where the time goes in v5:
time: 168 us; the launch traced here: 167 us
  waiting for transfers between devices  64.8 us (39%)
  starting transfers between devices  48.1 us (29%)
  Pallas kernels  47.1 us (28%)
  local copies, waits for them, and re-layouts  6.32 us (4%)
    ppermute x14, waiting for transfers between devices, send_on(): lax.ppermute(x, 'mem', [(i, (i // 2 + a) % 4 * 2 + (i + b) % 2) for i in...  39.2 us
    ppermute x6, waiting for transfers between devices, swap(): return lax.ppermute(x, axis, [(i, i ^ bit) for i in range(count)])  22.3 us
    ppermute x14, starting transfers between devices, send_on(): lax.ppermute(x, 'mem', [(i, (i // 2 + a) % 4 * 2 + (i + b) % 2) for i in...  21.3 us
    pallas_call x1, Pallas kernels, local(): pl.pallas_call(interior_kernel, out_shape=[f32(GROUPS, ROWS - EDGE, OWN,...  15.5 us
    pallas_call x1, Pallas kernels, local(): pl.pallas_call(edge_kernel, out_shape=[f32(OWN, HALF_OBS), f32(OWN, HALF_...  11.8 us
    pallas_call x7, Pallas kernels, place(): pl.pallas_call(place_kernel, grid_spec=pltpu.PrefetchScalarGridSpec(num_s...  5.79 us
    unnamed x24, local copies, waits for them, and re-layouts  5.69 us
    all_to_all x1, starting transfers between devices, local(): lax.all_to_all(jnp.broadcast_to(facts[None], (N_MEM, 3, OBS)), 'mem', 0,...  5.53 us
  transfers between devices with their start and end apart: 25, of which 14 were waited for; matrix products, arithmetic and copies ran while one was open for 1% of the time, Pallas kernels for 22%

profile of v5, /device:TPU:1, one launch (start us, length us, event | category | flops | bytes accessed | tf_op | source)
XLA Modules:
  0.0 167.3 jit_solution(16446049886415298879)
XLA Ops:
  0.0 4.0 %shard_map.64 = (f32[4,40,1024]{2,1,0:T(8,128)}, f32[4,40,1024]{2,1,0:T(8,128)}) custom-call(s32[1]{0:T(128)} %bitcast.2.parity_ref, f32[32,32,1024]{2,1,0:T(8,128)} %prior_ref.1, f32[32,1024]{1,0:T(8,128)} %h_ref.3, f32[32,1024]{1,0:T(8,128)} %v_ref.3), custom_call_target="tpu_custom_call" | custom-call | tf_op jit(solution)/shard_map/pallas_call | solution.py:421
  6.6 4.7 %collective-permute-start.1 = (f32[4,40,1024]{2,1,0:T(8,128)}, f32[4,40,1024]{2,1,0:T(8,128)S(1)}, u32[]{:S(2)}, u32[]{:S(2)}) collective-permute-start(f32[4,40,1024]{2,1,0:T(8,128)} %get-tuple-element.49), channel_id=1, source_target_pairs={{0,15},{1,2},{2,1},{3,4},{4,3},{5,6},{6,5},{7,8},{8,7},{9,10},{10,... | collective-permute-start | bytes 1966088 | tf_op jit(solution)/shard_map/ppermute | solution.py:435
  11.9 5.5 %all-to-all-start.1 = ((f32[8,3,256]{2,1,0:T(4,128)}), f32[8,3,256]{2,1,0:T(4,128)S(1)}, u32[]{:S(2)}, u32[]{:S(2)}) async-start(f32[8,3,256]{2,1,0:T(4,128)} %broadcast_in_dim.2), calls=%async_computation.1 | async-start | bytes 65536 | tf_op jit(solution)/shard_map/all_to_all | solution.py:441
  17.5 15.5 %shard_map.65 = (f32[8,24,32,128]{3,2,1,0:T(8,128)}, f32[8,8,32,128]{3,2,1,0:T(8,128)}, f32[2,8,32,1024]{3,2,1,0:T(8,128)}) custom-call(f32[1024,1024]{1,0:T(8,128)} %bitcast.17, f32[32,1024]{1,0:T(8,128)} %h_ref.3, f32[32,1024]{1,0:T(8,128)} %v_ref.3), custom_call_target="tpu_custom_call" | custom-call | bytes 51000000 | tf_op jit(solution)/shard_map/pallas_call | solution.py:449
  33.0 4.8 %all-to-all-start = ((f32[8,8,32,128]{3,2,1,0:T(8,128)}), f32[8,8,32,128]{3,2,1,0:T(8,128)S(1)}, u32[]{:S(2)}, u32[]{:S(2)}) async-start(f32[8,8,32,128]{3,2,1,0:T(8,128)} %get-tuple-element.50), calls=%async_computation | async-start | bytes 2097152 | tf_op jit(solution)/shard_map/all_to_all | solution.py:471
  38.4 11.8 %shard_map.66 = (f32[32,1024]{1,0:T(8,128)}, f32[32,1024]{1,0:T(8,128)}, f32[8,24,32,128]{3,2,1,0:T(8,128)}) custom-call(s32[1]{0:T(128)} %bitcast.2.parity_ref, s32[1]{0:T(128)} %bitcast.4.core_ref, f32[8,24,32,128]{3,2,1,0:T(8,128)} %get-tuple-element.51.inner_ref, f32[2,8,32,1024]{3,2,1,0:T(8,128)} %get-tuple-element.52.rim_ref, ...), custom_call_target="tpu_custom_call" | custom-call | bytes 39000000 | tf_op jit(solution)/shard_map/pallas_call | solution.py:472
  50.3 3.0 %collective-permute-start.2 = (f32[32,1024]{1,0:T(8,128)}, f32[32,1024]{1,0:T(8,128)S(1)}, u32[]{:S(2)}, u32[]{:S(2)}) collective-permute-start(f32[32,1024]{1,0:T(8,128)} %get-tuple-element.57.refs_0_), channel_id=1, source_target_pairs={{0,64},{16,80},{32,96},{48,112},{64,0},{80,16},{96,32},{112,48},{1... | collective-permute-start | bytes 393224 | tf_op jit(solution)/shard_map/ppermute | solution.py:398
  57.2 4.1 %collective-permute-start.7 = (f32[32,1024]{1,0:T(8,128)}, f32[32,1024]{1,0:T(8,128)S(1)}, u32[]{:S(2)}, u32[]{:S(2)}) collective-permute-start(f32[32,1024]{1,0:T(8,128)} %get-tuple-element.56), channel_id=1, source_target_pairs={{0,112},{16,96},{32,16},{48,0},{64,48},{80,32},{96,80},{112,64},{1... | collective-permute-start | bytes 393224 | tf_op jit(solution)/shard_map/ppermute | solution.py:398
  63.3 2.9 %collective-permute-done.6.refs_5_ = f32[32,1024]{1,0:T(8,128)S(1)} collective-permute-done((f32[32,1024]{1,0:T(8,128)}, f32[32,1024]{1,0:T(8,128)S(1)}, u32[]{:S(2)}, u32[]{:S(2)}) %collective-permute-start.6) | collective-permute-done | bytes 131104 | tf_op jit(solution)/shard_map/ppermute | solution.py:398
  68.5 4.5 %all-to-all-start.2 = ((f32[8,24,32,128]{3,2,1,0:T(8,128)}), f32[8,24,32,128]{3,2,1,0:T(8,128)S(1)}, u32[]{:S(2)}, u32[]{:S(2)}) async-start(f32[8,24,32,128]{3,2,1,0:T(8,128)} %get-tuple-element.69), calls=%async_computation.2 | async-start | bytes 6291456 | tf_op jit(solution)/shard_map/all_to_all | solution.py:506
  74.5 5.0 %collective-permute-done.10 = f32[136,256]{1,0:T(8,128)S(1)} collective-permute-done((f32[136,256]{1,0:T(8,128)S(1)}, f32[136,256]{1,0:T(8,128)S(1)}, u32[]{:S(2)}, u32[]{:S(2)}) %collective-permute-start.10) | collective-permute-done | bytes 139296 | tf_op jit(solution)/shard_map/ppermute | solution.py:405
  79.7 5.6 %collective-permute-done.11 = f32[136,256]{1,0:T(8,128)S(1)} collective-permute-done((f32[136,256]{1,0:T(8,128)S(1)}, f32[136,256]{1,0:T(8,128)S(1)}, u32[]{:S(2)}, u32[]{:S(2)}) %collective-permute-start.11) | collective-permute-done | bytes 139296 | tf_op jit(solution)/shard_map/ppermute | solution.py:405
  85.4 4.2 %collective-permute-done.12 = f32[136,256]{1,0:T(8,128)S(1)} collective-permute-done((f32[136,256]{1,0:T(8,128)S(1)}, f32[136,256]{1,0:T(8,128)S(1)}, u32[]{:S(2)}, u32[]{:S(2)}) %collective-permute-start.12) | collective-permute-done | bytes 139296 | tf_op jit(solution)/shard_map/ppermute | solution.py:405
  90.0 5.1 %collective-permute-done.13 = f32[136,256]{1,0:T(8,128)S(1)} collective-permute-done((f32[136,256]{1,0:T(8,128)S(1)}, f32[136,256]{1,0:T(8,128)S(1)}, u32[]{:S(2)}, u32[]{:S(2)}) %collective-permute-start.13) | collective-permute-done | bytes 139296 | tf_op jit(solution)/shard_map/ppermute | solution.py:405
  95.1 4.1 %collective-permute-start.14 = (f32[136,256]{1,0:T(8,128)S(1)}, f32[136,256]{1,0:T(8,128)S(1)}, u32[]{:S(2)}, u32[]{:S(2)}) collective-permute-start(f32[136,256]{1,0:T(8,128)S(1)} %add.100.mine_ref), channel_id=1, source_target_pairs={{0,16},{16,0},{32,48},{48,32},{64,80},{80,64},{96,112},{112,96},{1... | collective-permute-start | bytes 417800 | tf_op jit(solution)/shard_map/ppermute | solution.py:405
  100.2 4.3 %shard_map.68.weights_ref = bf16[512,256]{1,0:T(8,128)(2,1)S(1)} custom-call(s32[1]{0:T(128)} %bitcast.1.mem_ref, f32[136,256]{1,0:T(8,128)S(1)} %add.100.mine_ref, f32[136,256]{1,0:T(8,128)S(1)} %collective-permute-done.14.other_ref), custom_call_target="tpu_custom_call" | custom-call | bytes 18000000 | tf_op jit(solution)/shard_map/pallas_call | solution.py:512
  107.3 3.3 %all-to-all-done.2.x_ref = f32[8,24,32,128]{3,2,1,0:T(8,128)S(1)} async-done(((f32[8,24,32,128]{3,2,1,0:T(8,128)}), f32[8,24,32,128]{3,2,1,0:T(8,128)S(1)}, u32[]{:S(2)}, u32[]{:S(2)}) %all-to-all-start.2) | async-done | bytes 3145760 | tf_op jit(solution)/shard_map/all_to_all | solution.py:506
  111.8 3.9 %shard_map.70 = (f32[32,32,1024]{2,1,0:T(8,128)}, f32[32,32,128]{2,1,0:T(8,128)S(1)}, f32[32,32,128]{2,1,0:T(8,128)S(1)}, f32[32,32,128]{2,1,0:T(8,128)}, f32[32...) custom-call(s32[1]{0:T(128)} %bitcast.1.mem_ref, ...), custom_call_target="tpu_custom_call" | custom-call | bytes 12000000 | tf_op jit(solution)/shard_map/pallas_call | solution.py:350
  118.8 3.0 %collective-permute-start.18 = (f32[32,32,128]{2,1,0:T(8,128)}, f32[32,32,128]{2,1,0:T(8,128)S(1)}, u32[]{:S(2)}, u32[]{:S(2)}) collective-permute-start(f32[32,32,128]{2,1,0:T(8,128)} %get-tuple-element.74), channel_id=1, source_target_pairs={{0,80},{16,64},{32,112},{48,96},{64,16},{80,0},{96,48},{112,32},{1... | collective-permute-start | bytes 1572872 | tf_op jit(solution)/shard_map/ppermute | solution.py:398
  121.8 8.1 %collective-permute-done.21.x_ref = f32[32,32,128]{2,1,0:T(8,128)S(1)} collective-permute-done((f32[32,32,128]{2,1,0:T(8,128)S(1)}, f32[32,32,128]{2,1,0:T(8,128)S(1)}, u32[]{:S(2)}, u32[]{:S(2)}) %collective-permute-start.21) | collective-permute-done | bytes 524320 | tf_op jit(solution)/shard_map/ppermute | solution.py:398
  129.9 3.9 %collective-permute-start.16 = (f32[32,32,128]{2,1,0:T(8,128)}, f32[32,32,128]{2,1,0:T(8,128)S(1)}, u32[]{:S(2)}, u32[]{:S(2)}) collective-permute-start(f32[32,32,128]{2,1,0:T(8,128)} %get-tuple-element.72), channel_id=1, source_target_pairs={{0,112},{16,96},{32,16},{48,0},{64,48},{80,32},{96,80},{112,64},{1... | collective-permute-start | bytes 1572872 | tf_op jit(solution)/shard_map/ppermute | solution.py:398
  133.8 9.8 %collective-permute-done.20.x_ref = f32[32,32,128]{2,1,0:T(8,128)S(1)} collective-permute-done((f32[32,32,128]{2,1,0:T(8,128)S(1)}, f32[32,32,128]{2,1,0:T(8,128)S(1)}, u32[]{:S(2)}, u32[]{:S(2)}) %collective-permute-start.20) | collective-permute-done | bytes 524320 | tf_op jit(solution)/shard_map/ppermute | solution.py:398
  148.0 6.8 %collective-permute-done.18.x_ref = f32[32,32,128]{2,1,0:T(8,128)S(1)} collective-permute-done((f32[32,32,128]{2,1,0:T(8,128)}, f32[32,32,128]{2,1,0:T(8,128)S(1)}, u32[]{:S(2)}, u32[]{:S(2)}) %collective-permute-start.18) | collective-permute-done | bytes 524320 | tf_op jit(solution)/shard_map/ppermute | solution.py:398
  155.6 9.1 %collective-permute-done.17.x_ref = f32[32,32,128]{2,1,0:T(8,128)S(1)} collective-permute-done((f32[32,32,128]{2,1,0:T(8,128)}, f32[32,32,128]{2,1,0:T(8,128)S(1)}, u32[]{:S(2)}, u32[]{:S(2)}) %collective-permute-start.17) | collective-permute-done | bytes 524320 | tf_op jit(solution)/shard_map/ppermute | solution.py:398
  (75 shorter events, 30.0 us)
Async XLA Ops:
  4.1 28.9 %collective-permute-start = (f32[4,40,1024]{2,1,0:T(8,128)}, f32[4,40,1024]{2,1,0:T(8,128)S(1)}, u32[]{:S(2)}, u32[]{:S(2)}) collective-permute-start(f32[4,40,1024]{2,1,0:T(8,128)} %get-tuple-element.48), channel_id=1, source_target_pairs={{0,1},{1,0},{2,3},{3,2},{4,5},{5,4},{6,7},{7,6},{8,9},{9,8},{10,11... | collective-permute-start | bytes 1966088 | tf_op jit(solution)/shard_map/ppermute | solution.py:438
  6.6 26.4 %collective-permute-start.1 = (f32[4,40,1024]{2,1,0:T(8,128)}, f32[4,40,1024]{2,1,0:T(8,128)S(1)}, u32[]{:S(2)}, u32[]{:S(2)}) collective-permute-start(f32[4,40,1024]{2,1,0:T(8,128)} %get-tuple-element.49), channel_id=1, source_target_pairs={{0,15},{1,2},{2,1},{3,4},{4,3},{5,6},{6,5},{7,8},{8,7},{9,10},{10,... | collective-permute-start | bytes 1966088 | tf_op jit(solution)/shard_map/ppermute | solution.py:435
  11.9 21.0 %all-to-all-start.1 = ((f32[8,3,256]{2,1,0:T(4,128)}), f32[8,3,256]{2,1,0:T(4,128)S(1)}, u32[]{:S(2)}, u32[]{:S(2)}) async-start(f32[8,3,256]{2,1,0:T(4,128)} %broadcast_in_dim.2), calls=%async_computation.1 | async-start | bytes 65536 | tf_op jit(solution)/shard_map/all_to_all | solution.py:441
  33.0 33.3 %all-to-all-start = ((f32[8,8,32,128]{3,2,1,0:T(8,128)}), f32[8,8,32,128]{3,2,1,0:T(8,128)S(1)}, u32[]{:S(2)}, u32[]{:S(2)}) async-start(f32[8,8,32,128]{3,2,1,0:T(8,128)} %get-tuple-element.50), calls=%async_computation | async-start | bytes 2097152 | tf_op jit(solution)/shard_map/all_to_all | solution.py:471
  50.3 6.9 %collective-permute-start.2 = (f32[32,1024]{1,0:T(8,128)}, f32[32,1024]{1,0:T(8,128)S(1)}, u32[]{:S(2)}, u32[]{:S(2)}) collective-permute-start(f32[32,1024]{1,0:T(8,128)} %get-tuple-element.57.refs_0_), channel_id=1, source_target_pairs={{0,64},{16,80},{32,96},{48,112},{64,0},{80,16},{96,32},{112,48},{1... | collective-permute-start | bytes 393224 | tf_op jit(solution)/shard_map/ppermute | solution.py:398
  53.2 8.0 %collective-permute-start.3 = (f32[32,1024]{1,0:T(8,128)}, f32[32,1024]{1,0:T(8,128)S(1)}, u32[]{:S(2)}, u32[]{:S(2)}) collective-permute-start(f32[32,1024]{1,0:T(8,128)} %get-tuple-element.57.refs_0_), channel_id=1, source_target_pairs={{0,32},{16,48},{32,64},{48,80},{64,96},{80,112},{96,0},{112,16},{1... | collective-permute-start | bytes 393224 | tf_op jit(solution)/shard_map/ppermute | solution.py:398
  53.5 7.8 %collective-permute-start.4 = (f32[32,1024]{1,0:T(8,128)}, f32[32,1024]{1,0:T(8,128)S(1)}, u32[]{:S(2)}, u32[]{:S(2)}) collective-permute-start(f32[32,1024]{1,0:T(8,128)} %get-tuple-element.57.refs_0_), channel_id=1, source_target_pairs={{0,96},{16,112},{32,0},{48,16},{64,32},{80,48},{96,64},{112,80},{1... | collective-permute-start | bytes 393224 | tf_op jit(solution)/shard_map/ppermute | solution.py:398
  55.9 7.4 %collective-permute-start.5 = (f32[32,1024]{1,0:T(8,128)}, f32[32,1024]{1,0:T(8,128)S(1)}, u32[]{:S(2)}, u32[]{:S(2)}) collective-permute-start(f32[32,1024]{1,0:T(8,128)} %get-tuple-element.56), channel_id=1, source_target_pairs={{0,80},{16,64},{32,112},{48,96},{64,16},{80,0},{96,48},{112,32},{1... | collective-permute-start | bytes 393224 | tf_op jit(solution)/shard_map/ppermute | solution.py:398
  56.1 10.1 %collective-permute-start.6 = (f32[32,1024]{1,0:T(8,128)}, f32[32,1024]{1,0:T(8,128)S(1)}, u32[]{:S(2)}, u32[]{:S(2)}) collective-permute-start(f32[32,1024]{1,0:T(8,128)} %get-tuple-element.56), channel_id=1, source_target_pairs={{0,48},{16,32},{32,80},{48,64},{64,112},{80,96},{96,16},{112,0},{1... | collective-permute-start | bytes 393224 | tf_op jit(solution)/shard_map/ppermute | solution.py:398
  57.2 9.1 %collective-permute-start.7 = (f32[32,1024]{1,0:T(8,128)}, f32[32,1024]{1,0:T(8,128)S(1)}, u32[]{:S(2)}, u32[]{:S(2)}) collective-permute-start(f32[32,1024]{1,0:T(8,128)} %get-tuple-element.56), channel_id=1, source_target_pairs={{0,112},{16,96},{32,16},{48,0},{64,48},{80,32},{96,80},{112,64},{1... | collective-permute-start | bytes 393224 | tf_op jit(solution)/shard_map/ppermute | solution.py:398
  61.2 5.0 %collective-permute-start.8 = (f32[32,1024]{1,0:T(8,128)}, f32[32,1024]{1,0:T(8,128)S(1)}, u32[]{:S(2)}, u32[]{:S(2)}) collective-permute-start(f32[32,1024]{1,0:T(8,128)} %get-tuple-element.56), channel_id=1, source_target_pairs={{0,16},{16,0},{32,48},{48,32},{64,80},{80,64},{96,112},{112,96},{1... | collective-permute-start | bytes 393224 | tf_op jit(solution)/shard_map/ppermute | solution.py:398
  68.5 42.1 %all-to-all-start.2 = ((f32[8,24,32,128]{3,2,1,0:T(8,128)}), f32[8,24,32,128]{3,2,1,0:T(8,128)S(1)}, u32[]{:S(2)}, u32[]{:S(2)}) async-start(f32[8,24,32,128]{3,2,1,0:T(8,128)} %get-tuple-element.69), calls=%async_computation.2 | async-start | bytes 6291456 | tf_op jit(solution)/shard_map/all_to_all | solution.py:506
  74.4 5.1 %collective-permute-start.10 = (f32[136,256]{1,0:T(8,128)S(1)}, f32[136,256]{1,0:T(8,128)S(1)}, u32[]{:S(2)}, u32[]{:S(2)}) collective-permute-start(f32[136,256]{1,0:T(8,128)S(1)} %add.96), channel_id=1, source_target_pairs={{0,1},{1,0},{2,3},{3,2},{4,5},{5,4},{6,7},{7,6},{8,9},{9,8},{10,11... | collective-permute-start | bytes 417800 | tf_op jit(solution)/shard_map/ppermute | solution.py:405
  79.6 5.7 %collective-permute-start.11 = (f32[136,256]{1,0:T(8,128)S(1)}, f32[136,256]{1,0:T(8,128)S(1)}, u32[]{:S(2)}, u32[]{:S(2)}) collective-permute-start(f32[136,256]{1,0:T(8,128)S(1)} %add.97), channel_id=1, source_target_pairs={{0,2},{1,3},{2,0},{3,1},{4,6},{5,7},{6,4},{7,5},{8,10},{9,11},{10,... | collective-permute-start | bytes 417800 | tf_op jit(solution)/shard_map/ppermute | solution.py:405
  85.3 4.3 %collective-permute-start.12 = (f32[136,256]{1,0:T(8,128)S(1)}, f32[136,256]{1,0:T(8,128)S(1)}, u32[]{:S(2)}, u32[]{:S(2)}) collective-permute-start(f32[136,256]{1,0:T(8,128)S(1)} %add.98), channel_id=1, source_target_pairs={{0,4},{1,5},{2,6},{3,7},{4,0},{5,1},{6,2},{7,3},{8,12},{9,13},{10,... | collective-permute-start | bytes 417800 | tf_op jit(solution)/shard_map/ppermute | solution.py:405
  89.6 5.5 %collective-permute-start.13 = (f32[136,256]{1,0:T(8,128)S(1)}, f32[136,256]{1,0:T(8,128)S(1)}, u32[]{:S(2)}, u32[]{:S(2)}) collective-permute-start(f32[136,256]{1,0:T(8,128)S(1)} %add.99), channel_id=1, source_target_pairs={{0,8},{1,9},{2,10},{3,11},{4,12},{5,13},{6,14},{7,15},{8,0},{9,1},... | collective-permute-start | bytes 417800 | tf_op jit(solution)/shard_map/ppermute | solution.py:405
  95.1 5.1 %collective-permute-start.14 = (f32[136,256]{1,0:T(8,128)S(1)}, f32[136,256]{1,0:T(8,128)S(1)}, u32[]{:S(2)}, u32[]{:S(2)}) collective-permute-start(f32[136,256]{1,0:T(8,128)S(1)} %add.100.mine_ref), channel_id=1, source_target_pairs={{0,16},{16,0},{32,48},{48,32},{64,80},{80,64},{96,112},{112,96},{1... | collective-permute-start | bytes 417800 | tf_op jit(solution)/shard_map/ppermute | solution.py:405
  115.7 14.1 %collective-permute-start.21 = (f32[32,32,128]{2,1,0:T(8,128)S(1)}, f32[32,32,128]{2,1,0:T(8,128)S(1)}, u32[]{:S(2)}, u32[]{:S(2)}) collective-permute-start(f32[32,32,128]{2,1,0:T(8,128)S(1)} %get-tuple-element.77), channel_id=1, source_target_pairs={{0,64},{16,80},{32,96},{48,112},{64,0},{80,16},{96,32},{112,48},{1... | collective-permute-start | bytes 1572872 | tf_op jit(solution)/shard_map/ppermute | solution.py:398
  116.1 27.4 %collective-permute-start.20 = (f32[32,32,128]{2,1,0:T(8,128)S(1)}, f32[32,32,128]{2,1,0:T(8,128)S(1)}, u32[]{:S(2)}, u32[]{:S(2)}) collective-permute-start(f32[32,32,128]{2,1,0:T(8,128)S(1)} %get-tuple-element.76), channel_id=1, source_target_pairs={{0,32},{16,48},{32,64},{48,80},{64,96},{80,112},{96,0},{112,16},{1... | collective-permute-start | bytes 1572872 | tf_op jit(solution)/shard_map/ppermute | solution.py:398
  117.2 30.0 %collective-permute-start.19 = (f32[32,32,128]{2,1,0:T(8,128)}, f32[32,32,128]{2,1,0:T(8,128)S(1)}, u32[]{:S(2)}, u32[]{:S(2)}) collective-permute-start(f32[32,32,128]{2,1,0:T(8,128)} %get-tuple-element.75), channel_id=1, source_target_pairs={{0,96},{16,112},{32,0},{48,16},{64,32},{80,48},{96,64},{112,80},{1... | collective-permute-start | bytes 1572872 | tf_op jit(solution)/shard_map/ppermute | solution.py:398
  118.8 36.0 %collective-permute-start.18 = (f32[32,32,128]{2,1,0:T(8,128)}, f32[32,32,128]{2,1,0:T(8,128)S(1)}, u32[]{:S(2)}, u32[]{:S(2)}) collective-permute-start(f32[32,32,128]{2,1,0:T(8,128)} %get-tuple-element.74), channel_id=1, source_target_pairs={{0,80},{16,64},{32,112},{48,96},{64,16},{80,0},{96,48},{112,32},{1... | collective-permute-start | bytes 1572872 | tf_op jit(solution)/shard_map/ppermute | solution.py:398
  121.8 43.0 %collective-permute-start.17 = (f32[32,32,128]{2,1,0:T(8,128)}, f32[32,32,128]{2,1,0:T(8,128)S(1)}, u32[]{:S(2)}, u32[]{:S(2)}) collective-permute-start(f32[32,32,128]{2,1,0:T(8,128)} %get-tuple-element.73), channel_id=1, source_target_pairs={{0,48},{16,32},{32,80},{48,64},{64,112},{80,96},{96,16},{112,0},{1... | collective-permute-start | bytes 1572872 | tf_op jit(solution)/shard_map/ppermute | solution.py:398
  129.9 35.8 %collective-permute-start.16 = (f32[32,32,128]{2,1,0:T(8,128)}, f32[32,32,128]{2,1,0:T(8,128)S(1)}, u32[]{:S(2)}, u32[]{:S(2)}) collective-permute-start(f32[32,32,128]{2,1,0:T(8,128)} %get-tuple-element.72), channel_id=1, source_target_pairs={{0,112},{16,96},{32,16},{48,0},{64,48},{80,32},{96,80},{112,64},{1... | collective-permute-start | bytes 1572872 | tf_op jit(solution)/shard_map/ppermute | solution.py:398
  144.4 22.1 %collective-permute-start.15 = (f32[32,32,128]{2,1,0:T(8,128)}, f32[32,32,128]{2,1,0:T(8,128)S(1)}, u32[]{:S(2)}, u32[]{:S(2)}) collective-permute-start(f32[32,32,128]{2,1,0:T(8,128)} %get-tuple-element.71), channel_id=1, source_target_pairs={{0,16},{16,0},{32,48},{48,32},{64,80},{80,64},{96,112},{112,96},{1... | collective-permute-start | bytes 1572872 | tf_op jit(solution)/shard_map/ppermute | solution.py:398
  (13 other events, 55.0 us)

commit v6 on v5

--- a/solution.py
+++ b/solution.py
@@ -185,7 +185,7 @@
 
 
 def edge_kernel(
-    parity_ref, core_ref, inner_ref, rim_ref, a_ref, b_ref, h_ref, v_ref, index_ref,
+    parity_ref, core_ref, inner_ref, rim_ref, a_ref, b_ref, h_ref, v_ref, facts_ref,
     same_ref, flip_ref, rest_ref, obs_ref, field, one, two, coef_ref, in_sem, out_sems,
 ):
     load = pltpu.make_async_copy(inner_ref, field.at[:, HALO : ROWS - HALO], in_sem)
@@ -225,7 +225,7 @@
         store.start()
     for g in range(GROUPS):
         for t in range(OBS // LANES):
-            place = index_ref[g : g + 1, t * LANES : (t + 1) * LANES]
+            place = facts_ref[g, :1, t * LANES : (t + 1) * LANES].astype(jnp.int32)
             row = jnp.broadcast_to(place >> 7, (OWN, LANES))
             col = jnp.broadcast_to(place & (LANES - 1), (OWN, LANES))
             total = jnp.zeros((OWN, LANES), jnp.float32)
@@ -241,17 +241,18 @@
 
 
 def gram_kernel(mem_ref, *refs):
-    *from_refs, value_ref, weight_ref, keep_ref, send_ref, obs_ref = refs
+    *from_refs, facts_ref, keep_ref, send_ref, obs_ref = refs
     mem = mem_ref[0]
     core = lax.rem(mem, 2)
     for (a, b), ref in zip(PATHS, from_refs):
         source = lax.rem(mem // 2 + 4 - a, 4) * 2 + lax.rem(core + b, 2)
         obs_ref[pl.ds(pl.multiple_of(source * OWN, OWN), OWN), :] = ref[...]
     obs = obs_ref[...]
+    facts = jnp.concatenate([facts_ref[4 * core + q] for q in range(4)], axis=1)
     mean = jnp.sum(obs, axis=0, keepdims=True) * (1.0 / MEMBERS)
     anomalies = obs - mean
-    weighted = split(anomalies * weight_ref[...])
-    innovation = jnp.broadcast_to(value_ref[...] - mean, (8, HALF_OBS))
+    weighted = split(anomalies * facts[2:3])
+    innovation = jnp.broadcast_to(facts[1:2] - mean, (8, HALF_OBS))
     nt = (((1,), (1,)), ((), ()))
     gram = dot3(split(anomalies), weighted, nt)
     drive = dot3(split(innovation), weighted, nt)
@@ -302,16 +303,15 @@
     for n, (a, b) in enumerate(PATHS):
         place = lax.rem(mem // 2 + a, 4) * 2 + lax.rem(core + b, 2)
         high, low = split(gram_ref[pl.ds(pl.multiple_of(place * OWN, OWN), OWN), :])
-        out_ref[n * OWN : (n + 1) * OWN] = high
-        out_ref[MEMBERS + n * OWN : MEMBERS + (n + 1) * OWN] = low
-
-
-def product_kernel(mem_ref, weights_ref, x_ref, *refs):
-    members = refs[-1].shape[0]
-
-    def compute(out_refs):
-        weights = (weights_ref[:MEMBERS], weights_ref[MEMBERS:])
-        flat = [ref.reshape(members * CHUNK, LANES) for ref in out_refs]
+        out_ref[0, n * OWN : (n + 1) * OWN] = high
+        out_ref[1, n * OWN : (n + 1) * OWN] = low
+
+
+def product_kernel(mem_ref, weights_ref, early_ref, rest_ref, *out_refs):
+    flat = [ref.reshape(OWN * CHUNK, LANES) for ref in out_refs]
+
+    def compute(x_ref):
+        weights = (weights_ref[0], weights_ref[1])
         for half in range(0, CHUNK, HALO):
             parts = [
                 split(jnp.concatenate([x_ref[s, half + t] for s in range(N_MEM)], axis=0))
@@ -321,50 +321,38 @@
             y = dot3(weights, x)
             for t in range(HALO):
                 for n, ref in enumerate(flat):
-                    ref[pl.ds(half + t, members, stride=CHUNK), :] = y[
-                        n * members : (n + 1) * members, t * LANES : (t + 1) * LANES
+                    ref[pl.ds(half + t, OWN, stride=CHUNK), :] = y[
+                        n * OWN : (n + 1) * OWN, t * LANES : (t + 1) * LANES
                     ]
 
-    if len(refs) == 1:
-        compute(refs)
-    else:
-        step = pl.program_id(0)
-
-        @pl.when(step == 1)
-        def _():
-            for n, ref in enumerate(refs[1:]):
-                ref[...] = refs[0][n * OWN : (n + 1) * OWN]
-
-        pl.when(step != 1)(lambda: compute(refs[1:]))
-
-
-def product(mem, weights, x, done):
-    early = pl.BlockSpec((MEMBERS, CHUNK, LANES), lambda n, g: (0, 0, 0))
-    outs = [pl.BlockSpec((OWN, CHUNK, LANES), lambda n, g: (0, n, 0))] * (N_MEM - 1)
-    if done:
-        own = pl.BlockSpec((OWN, CHUNK, LANES), lambda n, g: (0, n, g[0]))
-        shapes = [f32(OWN, ROWS, WIDTH)] + [f32(OWN, ROWS, LANES)] * (N_MEM - 1)
-        grid = (ROWS // CHUNK,)
-    else:
-        own, outs, shapes, grid = early, [], [f32(MEMBERS, CHUNK, LANES)], (1,)
+    step = pl.program_id(0)
+    pl.when(step == 1)(lambda: compute(early_ref))
+    pl.when(step != 1)(lambda: compute(rest_ref))
+
+
+def product(mem, weights, early, rest, part):
+    outs = [pl.BlockSpec((OWN, CHUNK, LANES), lambda n, g: (0, n, 0))] * (N_MEM // 2)
+    shapes = [f32(OWN, ROWS, LANES)] * (N_MEM // 2)
+    if part == 0:
+        outs[0] = pl.BlockSpec((OWN, CHUNK, LANES), lambda n, g: (0, n, g[0]))
+        shapes[0] = f32(OWN, ROWS, WIDTH)
+    block = (N_MEM, CHUNK, OWN, LANES)
     return pl.pallas_call(
         product_kernel,
         grid_spec=pltpu.PrefetchScalarGridSpec(
             num_scalar_prefetch=1,
-            grid=grid,
+            grid=(ROWS // CHUNK,),
             in_specs=[
-                pl.BlockSpec((2 * MEMBERS, MEMBERS), lambda n, g: (0, 0)),
-                pl.BlockSpec(
-                    (N_MEM, CHUNK, OWN, LANES), lambda n, g: (0, jnp.maximum(n - 1, 0), 0, 0)
-                ),
-            ]
-            + [early] * len(done),
-            out_specs=[own] + outs,
+                pl.BlockSpec((2, MEMBERS // 2, MEMBERS), lambda n, g: (0, part, 0)),
+                pl.BlockSpec(block, lambda n, g: (0, 0, 0, 0)),
+                pl.BlockSpec(block, lambda n, g: (0, jnp.maximum(n - 1, 0), 0, 0)),
+            ],
+            out_specs=outs,
         ),
         out_shape=shapes,
-        compiler_params=params(20),
-        cost_estimate=cost(4 if done else 2),
-    )(mem, weights, x, *done)
+        compiler_params=params(16),
+        cost_estimate=cost(3),
+    )(mem, weights, early, rest)
 
 
 def place_kernel(group_ref, x_ref, before_ref, out_ref):
@@ -437,14 +425,12 @@
     )
     halo_a = lax.ppermute(halo_a, "reg", [(i, i ^ 1) for i in range(N_REG)])
 
-    facts = jnp.concatenate([obs_index.astype(jnp.float32), obs_value, obs_weight], axis=0)
+    facts = jnp.concatenate(
+        [obs_index.astype(jnp.float32), obs_value, obs_weight, jnp.zeros((SUB - 3, OBS))], axis=0
+    )
     facts = lax.all_to_all(
-        jnp.broadcast_to(facts[None], (N_MEM, 3, OBS)), "mem", 0, 0, tiled=True
-    )
-    index = facts[:, 0].astype(jnp.int32)
-    half_facts = lax.dynamic_slice_in_dim(facts, core[0] * 4, 4, axis=0)
-    value = half_facts[:, 1].reshape(1, HALF_OBS)
-    weight = half_facts[:, 2].reshape(1, HALF_OBS)
+        jnp.broadcast_to(facts[None], (N_MEM, SUB, OBS)), "mem", 0, 0, tiled=True
+    )
 
     inner, early, rim = pl.pallas_call(
         interior_kernel,
@@ -489,21 +475,20 @@
         ],
         compiler_params=params(56),
         cost_estimate=cost(13),
-    )(parity, core, inner, rim, halo_a, halo_b, h, v, index)
+    )(parity, core, inner, rim, halo_a, halo_b, h, v, facts)
     obs = [same] + [send_on(flip if b else same, a, b) for a, b in PATHS[1:]]
-    early, *obs = lax.optimization_barrier((early, *obs))
+    early, rest, *obs = lax.optimization_barrier((early, rest, *obs))
+    rest = lax.all_to_all(rest, "mem", 0, 0, tiled=True)
 
     keep, send = pl.pallas_call(
         gram_kernel,
         out_shape=[f32(MEMBERS // 2 + 8, MEMBERS)] * 2,
-        in_specs=[SMEM] + [VMEM] * (N_MEM + 2),
+        in_specs=[SMEM] + [VMEM] * (N_MEM + 1),
         out_specs=[VMEM, VMEM],
         scratch_shapes=[pltpu.VMEM((MEMBERS, HALF_OBS), jnp.float32)],
         compiler_params=params(12),
         cost_estimate=cost(3),
-    )(mem, *obs, value, weight)
-    rest, send = lax.optimization_barrier((rest, send))
-    rest = lax.all_to_all(rest, "mem", 0, 0, tiled=True)
+    )(mem, *obs, facts)
     total = keep + swap(send, "mem", 1)
     for bit in (1, 2, 4, 8):
         total = total + swap(total, "reg", bit)
@@ -511,7 +496,7 @@
 
     weights = pl.pallas_call(
         weights_kernel,
-        out_shape=jax.ShapeDtypeStruct((2 * MEMBERS, MEMBERS), jnp.bfloat16),
+        out_shape=jax.ShapeDtypeStruct((2, MEMBERS, MEMBERS), jnp.bfloat16),
         in_specs=[SMEM, VMEM, VMEM],
         out_specs=VMEM,
         scratch_shapes=[pltpu.VMEM((MEMBERS, MEMBERS), jnp.float32)],
@@ -519,8 +504,8 @@
         cost_estimate=cost(6),
     )(mem, total, other)
 
-    analysis = product(mem, weights, early, [])
-    result, *analysis = product(mem, weights, rest, analysis)
+    result, *analysis = product(mem, weights, early, rest, 0)
+    analysis = analysis + list(product(mem, weights, early, rest, 1))
     for x, (a, b), source in zip(analysis, PATHS[1:], sources[1:]):
         arrived = send_on(x, a, b)
         result = place(arrived, source, result)

time: 168 us -> 170 us (1.012)
  waiting for transfers between devices: 64.8 us -> 53.4 us
  local copies, waits for them, and re-layouts: 6.32 us -> 15.3 us
  starting transfers between devices: 48.1 us -> 50.1 us
  Pallas kernels: 47.1 us -> 49 us
    unnamed x24 -> x52, local copies, waits for them, and re-layouts: 5.69 us -> 14.6 us
    ppermute x14, waiting for transfers between devices: 39.2 us -> 31.1 us  [send_on(): lax.ppermute(x, 'mem', [(i, (i // 2 + a) % 4 * 2 + (i + b) % 2) for i in...]
    all_to_all x1, waiting for transfers between devices: 3.28 us -> 0.01 us  [local(): rest = lax.all_to_all(rest, 'mem', 0, 0, tiled=True)]
    all_to_all x1, starting transfers between devices: 4.52 us -> 7.39 us  [local(): rest = lax.all_to_all(rest, 'mem', 0, 0, tiled=True)]
  transfers between devices with their start and end apart: 25 -> 25, of which waited for: 14 -> 14; matrix products, arithmetic and copies ran while one was open for 1% -> 1% of each run, Pallas kernels for 22% -> 24%
where the time goes in v6:
time: 170 us; the launch traced here: 168 us
  waiting for transfers between devices  53.4 us (31%)
  starting transfers between devices  50.1 us (29%)
  Pallas kernels  49 us (29%)
  local copies, waits for them, and re-layouts  15.3 us (9%)
    ppermute x14, waiting for transfers between devices, send_on(): lax.ppermute(x, 'mem', [(i, (i // 2 + a) % 4 * 2 + (i + b) % 2) for i in...  31.1 us
    ppermute x6, waiting for transfers between devices, swap(): return lax.ppermute(x, axis, [(i, i ^ bit) for i in range(count)])  22.3 us
    ppermute x14, starting transfers between devices, send_on(): lax.ppermute(x, 'mem', [(i, (i // 2 + a) % 4 * 2 + (i + b) % 2) for i in...  20.4 us
    pallas_call x1, Pallas kernels, local(): pl.pallas_call(interior_kernel, out_shape=[f32(GROUPS, ROWS - EDGE, OWN,...  15.5 us
    unnamed x52, local copies, waits for them, and re-layouts  14.6 us
    pallas_call x1, Pallas kernels, local(): pl.pallas_call(edge_kernel, out_shape=[f32(OWN, HALF_OBS), f32(OWN, HALF_...  11 us
    all_to_all x1, starting transfers between devices, local(): rest = lax.all_to_all(rest, 'mem', 0, 0, tiled=True)  7.39 us
    pallas_call x7, Pallas kernels, place(): pl.pallas_call(place_kernel, grid_spec=pltpu.PrefetchScalarGridSpec(num_s...  6.83 us
  transfers between devices with their start and end apart: 25, of which 14 were waited for; matrix products, arithmetic and copies ran while one was open for 1% of the time, Pallas kernels for 24%

profile of v6, /device:TPU:1, one launch (start us, length us, event | category | flops | bytes accessed | tf_op | source)
XLA Modules:
  0.0 168.2 jit_solution(2607341536318600719)
XLA Ops:
  0.0 4.0 %shard_map.64 = (f32[4,40,1024]{2,1,0:T(8,128)}, f32[4,40,1024]{2,1,0:T(8,128)}) custom-call(s32[1]{0:T(128)} %bitcast.2.parity_ref, f32[32,32,1024]{2,1,0:T(8,128)} %prior_ref.1, f32[32,1024]{1,0:T(8,128)} %h_ref.3, f32[32,1024]{1,0:T(8,128)} %v_ref.3), custom_call_target="tpu_custom_call" | custom-call | tf_op jit(solution)/shard_map/pallas_call | solution.py:409
  4.1 2.5 %collective-permute-start = (f32[4,40,1024]{2,1,0:T(8,128)}, f32[4,40,1024]{2,1,0:T(8,128)S(1)}, u32[]{:S(2)}, u32[]{:S(2)}) collective-permute-start(f32[4,40,1024]{2,1,0:T(8,128)} %get-tuple-element.47), channel_id=1, source_target_pairs={{0,1},{1,0},{2,3},{3,2},{4,5},{5,4},{6,7},{7,6},{8,9},{9,8},{10,11... | collective-permute-start | bytes 1966088 | tf_op jit(solution)/shard_map/ppermute | solution.py:426
  6.6 4.7 %collective-permute-start.1 = (f32[4,40,1024]{2,1,0:T(8,128)}, f32[4,40,1024]{2,1,0:T(8,128)S(1)}, u32[]{:S(2)}, u32[]{:S(2)}) collective-permute-start(f32[4,40,1024]{2,1,0:T(8,128)} %get-tuple-element.48), channel_id=1, source_target_pairs={{0,15},{1,2},{2,1},{3,4},{4,3},{5,6},{6,5},{7,8},{8,7},{9,10},{10,... | collective-permute-start | bytes 1966088 | tf_op jit(solution)/shard_map/ppermute | solution.py:423
  12.1 5.5 %all-to-all-start.1 = ((f32[8,8,256]{2,1,0:T(8,128)}), f32[8,8,256]{2,1,0:T(8,128)S(1)}, u32[]{:S(2)}, u32[]{:S(2)}) async-start(f32[8,8,256]{2,1,0:T(8,128)} %broadcast_in_dim.10), calls=%async_computation.1 | async-start | bytes 131072 | tf_op jit(solution)/shard_map/all_to_all | solution.py:431
  17.6 15.5 %shard_map.65 = (f32[8,24,32,128]{3,2,1,0:T(8,128)}, f32[8,8,32,128]{3,2,1,0:T(8,128)}, f32[2,8,32,1024]{3,2,1,0:T(8,128)}) custom-call(f32[1024,1024]{1,0:T(8,128)} %bitcast.11, f32[32,1024]{1,0:T(8,128)} %h_ref.3, f32[32,1024]{1,0:T(8,128)} %v_ref.3), custom_call_target="tpu_custom_call" | custom-call | bytes 51000000 | tf_op jit(solution)/shard_map/pallas_call | solution.py:435
  33.2 4.8 %all-to-all-start = ((f32[8,8,32,128]{3,2,1,0:T(8,128)}), f32[8,8,32,128]{3,2,1,0:T(8,128)S(1)}, u32[]{:S(2)}, u32[]{:S(2)}) async-start(f32[8,8,32,128]{3,2,1,0:T(8,128)} %get-tuple-element.49), calls=%async_computation | async-start | bytes 2097152 | tf_op jit(solution)/shard_map/all_to_all | solution.py:457
  38.0 11.0 %shard_map.66 = (f32[32,1024]{1,0:T(8,128)}, f32[32,1024]{1,0:T(8,128)}, f32[8,24,32,128]{3,2,1,0:T(8,128)}) custom-call(s32[1]{0:T(128)} %bitcast.2.parity_ref, s32[1]{0:T(128)} %bitcast.4.core_ref, f32[8,24,32,128]{3,2,1,0:T(8,128)} %get-tuple-element.50.inner_ref, f32[2,8,32,1024]{3,2,1,0:T(8,128)} %get-tuple-element.51.rim_ref, ...), custom_call_target="tpu_custom_call" | custom-call | bytes 39000000 | tf_op jit(solution)/shard_map/pallas_call | solution.py:458
  49.0 2.7 %collective-permute-start.4 = (f32[32,1024]{1,0:T(8,128)}, f32[32,1024]{1,0:T(8,128)S(1)}, u32[]{:S(2)}, u32[]{:S(2)}) collective-permute-start(f32[32,1024]{1,0:T(8,128)} %get-tuple-element.57.refs_0_), channel_id=1, source_target_pairs={{0,96},{16,112},{32,0},{48,16},{64,32},{80,48},{96,64},{112,80},{1... | collective-permute-start | bytes 393224 | tf_op jit(solution)/shard_map/ppermute | solution.py:386
  67.1 7.4 %all-to-all-start.2 = ((f32[8,24,32,128]{3,2,1,0:T(8,128)}), f32[8,24,32,128]{3,2,1,0:T(8,128)S(1)}, u32[]{:S(2)}, u32[]{:S(2)}) async-start(f32[8,24,32,128]{3,2,1,0:T(8,128)} %get-tuple-element.68), calls=%async_computation.2 | async-start | bytes 6291456 | tf_op jit(solution)/shard_map/all_to_all | solution.py:481
  82.7 5.1 %collective-permute-done.10 = f32[136,256]{1,0:T(8,128)S(1)} collective-permute-done((f32[136,256]{1,0:T(8,128)S(1)}, f32[136,256]{1,0:T(8,128)S(1)}, u32[]{:S(2)}, u32[]{:S(2)}) %collective-permute-start.10) | collective-permute-done | bytes 139296 | tf_op jit(solution)/shard_map/ppermute | solution.py:393
  87.9 5.7 %collective-permute-done.11 = f32[136,256]{1,0:T(8,128)S(1)} collective-permute-done((f32[136,256]{1,0:T(8,128)S(1)}, f32[136,256]{1,0:T(8,128)S(1)}, u32[]{:S(2)}, u32[]{:S(2)}) %collective-permute-start.11) | collective-permute-done | bytes 139296 | tf_op jit(solution)/shard_map/ppermute | solution.py:393
  93.7 4.2 %collective-permute-done.12 = f32[136,256]{1,0:T(8,128)S(1)} collective-permute-done((f32[136,256]{1,0:T(8,128)S(1)}, f32[136,256]{1,0:T(8,128)S(1)}, u32[]{:S(2)}, u32[]{:S(2)}) %collective-permute-start.12) | collective-permute-done | bytes 139296 | tf_op jit(solution)/shard_map/ppermute | solution.py:393
  98.3 5.1 %collective-permute-done.13 = f32[136,256]{1,0:T(8,128)S(1)} collective-permute-done((f32[136,256]{1,0:T(8,128)S(1)}, f32[136,256]{1,0:T(8,128)S(1)}, u32[]{:S(2)}, u32[]{:S(2)}) %collective-permute-start.13) | collective-permute-done | bytes 139296 | tf_op jit(solution)/shard_map/ppermute | solution.py:393
  103.4 4.0 %collective-permute-start.14 = (f32[136,256]{1,0:T(8,128)S(1)}, f32[136,256]{1,0:T(8,128)S(1)}, u32[]{:S(2)}, u32[]{:S(2)}) collective-permute-start(f32[136,256]{1,0:T(8,128)S(1)} %add.96.mine_ref), channel_id=1, source_target_pairs={{0,16},{16,0},{32,48},{48,32},{64,80},{80,64},{96,112},{112,96},{1... | collective-permute-start | bytes 417800 | tf_op jit(solution)/shard_map/ppermute | solution.py:393
  108.4 4.3 %shard_map.68.weights_ref = bf16[2,256,256]{2,1,0:T(8,128)(2,1)S(1)} custom-call(s32[1]{0:T(128)} %bitcast.1.mem_ref, f32[136,256]{1,0:T(8,128)S(1)} %add.96.mine_ref, f32[136,256]{1,0:T(8,128)S(1)} %collective-permute-done.14.other_ref), custom_call_target="tpu_custom_call" | custom-call | bytes 18000000 | tf_op jit(solution)/shard_map/pallas_call | solution.py:497
  113.9 3.0 %shard_map.70 = (f32[32,32,1024]{2,1,0:T(8,128)}, f32[32,32,128]{2,1,0:T(8,128)S(1)}, f32[32,32,128]{2,1,0:T(8,128)S(1)}, f32[32,32,128]{2,1,0:T(8,128)}) custom-call(s32[1]{0:T(128)} %bitcast.1.mem_ref, bf16[2,256,256]{2,1,0:T(8,128)(2,1)S(1)} %shard_map.68.weights_ref, f32[8,8,32,128]{3,2,1,0:T(8,128)S(1)} %copy-done.1, ...), custom_call_target="tpu_custom_call" | custom-call | bytes 9000000 | tf_op jit(solution)/shard_map/pallas_call | solution.py:340
  118.6 2.4 %collective-permute-start.21 = (f32[32,32,128]{2,1,0:T(8,128)S(1)}, f32[32,32,128]{2,1,0:T(8,128)S(1)}, u32[]{:S(2)}, u32[]{:S(2)}) collective-permute-start(f32[32,32,128]{2,1,0:T(8,128)S(1)} %get-tuple-element.75), channel_id=1, source_target_pairs={{0,64},{16,80},{32,96},{48,112},{64,0},{80,16},{96,32},{112,48},{1... | collective-permute-start | bytes 1572872 | tf_op jit(solution)/shard_map/ppermute | solution.py:386
  122.2 3.2 %shard_map.69 = (f32[32,32,128]{2,1,0:T(8,128)}, f32[32,32,128]{2,1,0:T(8,128)}, f32[32,32,128]{2,1,0:T(8,128)}, f32[32,32,128]{2,1,0:T(8,128)}) custom-call(s32[1]{0:T(128)} %bitcast.1.mem_ref, bf16[2,256,256]{2,1,0:T(8,128)(2,1)S(1)} %shard_map.68.weights_ref, f32[8,8,32,128]{3,2,1,0:T(8,128)S(1)} %copy-done.1, f32[8,24,32,128]{3,2,1,0:T(8,128)S(1)} %all-to-all-done.2.rest_ref), custom_call_target="tpu_custom_call" | custom-call | bytes 9000000 | tf_op jit(solution)/shard_map/pallas_call | solution.py:340
  126.8 5.0 %collective-permute-done.20.x_ref = f32[32,32,128]{2,1,0:T(8,128)S(1)} collective-permute-done((f32[32,32,128]{2,1,0:T(8,128)S(1)}, f32[32,32,128]{2,1,0:T(8,128)S(1)}, u32[]{:S(2)}, u32[]{:S(2)}) %collective-permute-start.20) | collective-permute-done | bytes 524320 | tf_op jit(solution)/shard_map/ppermute | solution.py:386
  132.7 3.0 %collective-permute-start.16 = (f32[32,32,128]{2,1,0:T(8,128)}, f32[32,32,128]{2,1,0:T(8,128)S(1)}, u32[]{:S(2)}, u32[]{:S(2)}) collective-permute-start(f32[32,32,128]{2,1,0:T(8,128)} %get-tuple-element.70), channel_id=1, source_target_pairs={{0,112},{16,96},{32,16},{48,0},{64,48},{80,32},{96,80},{112,64},{1... | collective-permute-start | bytes 1572872 | tf_op jit(solution)/shard_map/ppermute | solution.py:386
  135.7 8.3 %collective-permute-done.21.x_ref = f32[32,32,128]{2,1,0:T(8,128)S(1)} collective-permute-done((f32[32,32,128]{2,1,0:T(8,128)S(1)}, f32[32,32,128]{2,1,0:T(8,128)S(1)}, u32[]{:S(2)}, u32[]{:S(2)}) %collective-permute-start.21) | collective-permute-done | bytes 524320 | tf_op jit(solution)/shard_map/ppermute | solution.py:386
  144.8 2.0 %collective-permute-start.15 = (f32[32,32,128]{2,1,0:T(8,128)}, f32[32,32,128]{2,1,0:T(8,128)S(1)}, u32[]{:S(2)}, u32[]{:S(2)}) collective-permute-start(f32[32,32,128]{2,1,0:T(8,128)} %get-tuple-element.69), channel_id=1, source_target_pairs={{0,16},{16,0},{32,48},{48,32},{64,80},{80,64},{96,112},{112,96},{1... | collective-permute-start | bytes 1572872 | tf_op jit(solution)/shard_map/ppermute | solution.py:386
  151.8 4.7 %collective-permute-done.18.x_ref = f32[32,32,128]{2,1,0:T(8,128)S(1)} collective-permute-done((f32[32,32,128]{2,1,0:T(8,128)}, f32[32,32,128]{2,1,0:T(8,128)S(1)}, u32[]{:S(2)}, u32[]{:S(2)}) %collective-permute-start.18) | collective-permute-done | bytes 524320 | tf_op jit(solution)/shard_map/ppermute | solution.py:386
  157.4 8.4 %collective-permute-done.17.x_ref = f32[32,32,128]{2,1,0:T(8,128)S(1)} collective-permute-done((f32[32,32,128]{2,1,0:T(8,128)}, f32[32,32,128]{2,1,0:T(8,128)S(1)}, u32[]{:S(2)}, u32[]{:S(2)}) %collective-permute-start.17) | collective-permute-done | bytes 524320 | tf_op jit(solution)/shard_map/ppermute | solution.py:386
  (102 shorter events, 41.4 us)
Async XLA Ops:
  4.1 29.0 %collective-permute-start = (f32[4,40,1024]{2,1,0:T(8,128)}, f32[4,40,1024]{2,1,0:T(8,128)S(1)}, u32[]{:S(2)}, u32[]{:S(2)}) collective-permute-start(f32[4,40,1024]{2,1,0:T(8,128)} %get-tuple-element.47), channel_id=1, source_target_pairs={{0,1},{1,0},{2,3},{3,2},{4,5},{5,4},{6,7},{7,6},{8,9},{9,8},{10,11... | collective-permute-start | bytes 1966088 | tf_op jit(solution)/shard_map/ppermute | solution.py:426
  6.6 26.5 %collective-permute-start.1 = (f32[4,40,1024]{2,1,0:T(8,128)}, f32[4,40,1024]{2,1,0:T(8,128)S(1)}, u32[]{:S(2)}, u32[]{:S(2)}) collective-permute-start(f32[4,40,1024]{2,1,0:T(8,128)} %get-tuple-element.48), channel_id=1, source_target_pairs={{0,15},{1,2},{2,1},{3,4},{4,3},{5,6},{6,5},{7,8},{8,7},{9,10},{10,... | collective-permute-start | bytes 1966088 | tf_op jit(solution)/shard_map/ppermute | solution.py:423
  12.1 21.0 %all-to-all-start.1 = ((f32[8,8,256]{2,1,0:T(8,128)}), f32[8,8,256]{2,1,0:T(8,128)S(1)}, u32[]{:S(2)}, u32[]{:S(2)}) async-start(f32[8,8,256]{2,1,0:T(8,128)} %broadcast_in_dim.10), calls=%async_computation.1 | async-start | bytes 131072 | tf_op jit(solution)/shard_map/all_to_all | solution.py:431
  33.2 33.0 %all-to-all-start = ((f32[8,8,32,128]{3,2,1,0:T(8,128)}), f32[8,8,32,128]{3,2,1,0:T(8,128)S(1)}, u32[]{:S(2)}, u32[]{:S(2)}) async-start(f32[8,8,32,128]{3,2,1,0:T(8,128)} %get-tuple-element.49), calls=%async_computation | async-start | bytes 2097152 | tf_op jit(solution)/shard_map/all_to_all | solution.py:457
  49.0 6.4 %collective-permute-start.4 = (f32[32,1024]{1,0:T(8,128)}, f32[32,1024]{1,0:T(8,128)S(1)}, u32[]{:S(2)}, u32[]{:S(2)}) collective-permute-start(f32[32,1024]{1,0:T(8,128)} %get-tuple-element.57.refs_0_), channel_id=1, source_target_pairs={{0,96},{16,112},{32,0},{48,16},{64,32},{80,48},{96,64},{112,80},{1... | collective-permute-start | bytes 393224 | tf_op jit(solution)/shard_map/ppermute | solution.py:386
  51.7 7.1 %collective-permute-start.3 = (f32[32,1024]{1,0:T(8,128)}, f32[32,1024]{1,0:T(8,128)S(1)}, u32[]{:S(2)}, u32[]{:S(2)}) collective-permute-start(f32[32,1024]{1,0:T(8,128)} %get-tuple-element.57.refs_0_), channel_id=1, source_target_pairs={{0,32},{16,48},{32,64},{48,80},{64,96},{80,112},{96,0},{112,16},{1... | collective-permute-start | bytes 393224 | tf_op jit(solution)/shard_map/ppermute | solution.py:386
  51.7 8.3 %collective-permute-start.2 = (f32[32,1024]{1,0:T(8,128)}, f32[32,1024]{1,0:T(8,128)S(1)}, u32[]{:S(2)}, u32[]{:S(2)}) collective-permute-start(f32[32,1024]{1,0:T(8,128)} %get-tuple-element.57.refs_0_), channel_id=1, source_target_pairs={{0,64},{16,80},{32,96},{48,112},{64,0},{80,16},{96,32},{112,48},{1... | collective-permute-start | bytes 393224 | tf_op jit(solution)/shard_map/ppermute | solution.py:386
  53.4 7.2 %collective-permute-start.8 = (f32[32,1024]{1,0:T(8,128)}, f32[32,1024]{1,0:T(8,128)S(1)}, u32[]{:S(2)}, u32[]{:S(2)}) collective-permute-start(f32[32,1024]{1,0:T(8,128)} %get-tuple-element.56), channel_id=1, source_target_pairs={{0,16},{16,0},{32,48},{48,32},{64,80},{80,64},{96,112},{112,96},{1... | collective-permute-start | bytes 393224 | tf_op jit(solution)/shard_map/ppermute | solution.py:386
  54.6 7.4 %collective-permute-start.7 = (f32[32,1024]{1,0:T(8,128)}, f32[32,1024]{1,0:T(8,128)S(1)}, u32[]{:S(2)}, u32[]{:S(2)}) collective-permute-start(f32[32,1024]{1,0:T(8,128)} %get-tuple-element.56), channel_id=1, source_target_pairs={{0,112},{16,96},{32,16},{48,0},{64,48},{80,32},{96,80},{112,64},{1... | collective-permute-start | bytes 393224 | tf_op jit(solution)/shard_map/ppermute | solution.py:386
  55.4 8.5 %collective-permute-start.6 = (f32[32,1024]{1,0:T(8,128)}, f32[32,1024]{1,0:T(8,128)S(1)}, u32[]{:S(2)}, u32[]{:S(2)}) collective-permute-start(f32[32,1024]{1,0:T(8,128)} %get-tuple-element.56), channel_id=1, source_target_pairs={{0,48},{16,32},{32,80},{48,64},{64,112},{80,96},{96,16},{112,0},{1... | collective-permute-start | bytes 393224 | tf_op jit(solution)/shard_map/ppermute | solution.py:386
  59.4 6.1 %collective-permute-start.5 = (f32[32,1024]{1,0:T(8,128)}, f32[32,1024]{1,0:T(8,128)S(1)}, u32[]{:S(2)}, u32[]{:S(2)}) collective-permute-start(f32[32,1024]{1,0:T(8,128)} %get-tuple-element.56), channel_id=1, source_target_pairs={{0,80},{16,64},{32,112},{48,96},{64,16},{80,0},{96,48},{112,32},{1... | collective-permute-start | bytes 393224 | tf_op jit(solution)/shard_map/ppermute | solution.py:386
  67.1 45.5 %all-to-all-start.2 = ((f32[8,24,32,128]{3,2,1,0:T(8,128)}), f32[8,24,32,128]{3,2,1,0:T(8,128)S(1)}, u32[]{:S(2)}, u32[]{:S(2)}) async-start(f32[8,24,32,128]{3,2,1,0:T(8,128)} %get-tuple-element.68), calls=%async_computation.2 | async-start | bytes 6291456 | tf_op jit(solution)/shard_map/all_to_all | solution.py:481
  82.6 5.2 %collective-permute-start.10 = (f32[136,256]{1,0:T(8,128)S(1)}, f32[136,256]{1,0:T(8,128)S(1)}, u32[]{:S(2)}, u32[]{:S(2)}) collective-permute-start(f32[136,256]{1,0:T(8,128)S(1)} %add.92), channel_id=1, source_target_pairs={{0,1},{1,0},{2,3},{3,2},{4,5},{5,4},{6,7},{7,6},{8,9},{9,8},{10,11... | collective-permute-start | bytes 417800 | tf_op jit(solution)/shard_map/ppermute | solution.py:393
  87.8 5.8 %collective-permute-start.11 = (f32[136,256]{1,0:T(8,128)S(1)}, f32[136,256]{1,0:T(8,128)S(1)}, u32[]{:S(2)}, u32[]{:S(2)}) collective-permute-start(f32[136,256]{1,0:T(8,128)S(1)} %add.93), channel_id=1, source_target_pairs={{0,2},{1,3},{2,0},{3,1},{4,6},{5,7},{6,4},{7,5},{8,10},{9,11},{10,... | collective-permute-start | bytes 417800 | tf_op jit(solution)/shard_map/ppermute | solution.py:393
  93.6 4.3 %collective-permute-start.12 = (f32[136,256]{1,0:T(8,128)S(1)}, f32[136,256]{1,0:T(8,128)S(1)}, u32[]{:S(2)}, u32[]{:S(2)}) collective-permute-start(f32[136,256]{1,0:T(8,128)S(1)} %add.94), channel_id=1, source_target_pairs={{0,4},{1,5},{2,6},{3,7},{4,0},{5,1},{6,2},{7,3},{8,12},{9,13},{10,... | collective-permute-start | bytes 417800 | tf_op jit(solution)/shard_map/ppermute | solution.py:393
  97.9 5.5 %collective-permute-start.13 = (f32[136,256]{1,0:T(8,128)S(1)}, f32[136,256]{1,0:T(8,128)S(1)}, u32[]{:S(2)}, u32[]{:S(2)}) collective-permute-start(f32[136,256]{1,0:T(8,128)S(1)} %add.95), channel_id=1, source_target_pairs={{0,8},{1,9},{2,10},{3,11},{4,12},{5,13},{6,14},{7,15},{8,0},{9,1},... | collective-permute-start | bytes 417800 | tf_op jit(solution)/shard_map/ppermute | solution.py:393
  103.4 5.0 %collective-permute-start.14 = (f32[136,256]{1,0:T(8,128)S(1)}, f32[136,256]{1,0:T(8,128)S(1)}, u32[]{:S(2)}, u32[]{:S(2)}) collective-permute-start(f32[136,256]{1,0:T(8,128)S(1)} %add.96.mine_ref), channel_id=1, source_target_pairs={{0,16},{16,0},{32,48},{48,32},{64,80},{80,64},{96,112},{112,96},{1... | collective-permute-start | bytes 417800 | tf_op jit(solution)/shard_map/ppermute | solution.py:393
  116.9 15.0 %collective-permute-start.20 = (f32[32,32,128]{2,1,0:T(8,128)S(1)}, f32[32,32,128]{2,1,0:T(8,128)S(1)}, u32[]{:S(2)}, u32[]{:S(2)}) collective-permute-start(f32[32,32,128]{2,1,0:T(8,128)S(1)} %get-tuple-element.74), channel_id=1, source_target_pairs={{0,32},{16,48},{32,64},{48,80},{64,96},{80,112},{96,0},{112,16},{1... | collective-permute-start | bytes 1572872 | tf_op jit(solution)/shard_map/ppermute | solution.py:386
  118.6 25.4 %collective-permute-start.21 = (f32[32,32,128]{2,1,0:T(8,128)S(1)}, f32[32,32,128]{2,1,0:T(8,128)S(1)}, u32[]{:S(2)}, u32[]{:S(2)}) collective-permute-start(f32[32,32,128]{2,1,0:T(8,128)S(1)} %get-tuple-element.75), channel_id=1, source_target_pairs={{0,64},{16,80},{32,96},{48,112},{64,0},{80,16},{96,32},{112,48},{1... | collective-permute-start | bytes 1572872 | tf_op jit(solution)/shard_map/ppermute | solution.py:386
  121.0 28.9 %collective-permute-start.19 = (f32[32,32,128]{2,1,0:T(8,128)}, f32[32,32,128]{2,1,0:T(8,128)}, u32[]{:S(2)}, u32[]{:S(2)}) collective-permute-start(f32[32,32,128]{2,1,0:T(8,128)} %get-tuple-element.73), channel_id=1, source_target_pairs={{0,96},{16,112},{32,0},{48,16},{64,32},{80,48},{96,64},{112,80},{1... | collective-permute-start | bytes 1572872 | tf_op jit(solution)/shard_map/ppermute | solution.py:386
  125.5 31.1 %collective-permute-start.18 = (f32[32,32,128]{2,1,0:T(8,128)}, f32[32,32,128]{2,1,0:T(8,128)S(1)}, u32[]{:S(2)}, u32[]{:S(2)}) collective-permute-start(f32[32,32,128]{2,1,0:T(8,128)} %get-tuple-element.72), channel_id=1, source_target_pairs={{0,80},{16,64},{32,112},{48,96},{64,16},{80,0},{96,48},{112,32},{1... | collective-permute-start | bytes 1572872 | tf_op jit(solution)/shard_map/ppermute | solution.py:386
  126.3 39.5 %collective-permute-start.17 = (f32[32,32,128]{2,1,0:T(8,128)}, f32[32,32,128]{2,1,0:T(8,128)S(1)}, u32[]{:S(2)}, u32[]{:S(2)}) collective-permute-start(f32[32,32,128]{2,1,0:T(8,128)} %get-tuple-element.71), channel_id=1, source_target_pairs={{0,48},{16,32},{32,80},{48,64},{64,112},{80,96},{96,16},{112,0},{1... | collective-permute-start | bytes 1572872 | tf_op jit(solution)/shard_map/ppermute | solution.py:386
  132.7 33.9 %collective-permute-start.16 = (f32[32,32,128]{2,1,0:T(8,128)}, f32[32,32,128]{2,1,0:T(8,128)S(1)}, u32[]{:S(2)}, u32[]{:S(2)}) collective-permute-start(f32[32,32,128]{2,1,0:T(8,128)} %get-tuple-element.70), channel_id=1, source_target_pairs={{0,112},{16,96},{32,16},{48,0},{64,48},{80,32},{96,80},{112,64},{1... | collective-permute-start | bytes 1572872 | tf_op jit(solution)/shard_map/ppermute | solution.py:386
  144.8 22.6 %collective-permute-start.15 = (f32[32,32,128]{2,1,0:T(8,128)}, f32[32,32,128]{2,1,0:T(8,128)S(1)}, u32[]{:S(2)}, u32[]{:S(2)}) collective-permute-start(f32[32,32,128]{2,1,0:T(8,128)} %get-tuple-element.69), channel_id=1, source_target_pairs={{0,16},{16,0},{32,48},{48,32},{64,80},{80,64},{96,112},{112,96},{1... | collective-permute-start | bytes 1572872 | tf_op jit(solution)/shard_map/ppermute | solution.py:386
  (27 other events, 116.5 us)

commit v7 on v6

--- a/solution.py
+++ b/solution.py
@@ -477,8 +477,7 @@
         cost_estimate=cost(13),
     )(parity, core, inner, rim, halo_a, halo_b, h, v, facts)
     obs = [same] + [send_on(flip if b else same, a, b) for a, b in PATHS[1:]]
-    early, rest, *obs = lax.optimization_barrier((early, rest, *obs))
-    rest = lax.all_to_all(rest, "mem", 0, 0, tiled=True)
+    early, *obs = lax.optimization_barrier((early, *obs))
 
     keep, send = pl.pallas_call(
         gram_kernel,
@@ -489,6 +488,8 @@
         compiler_params=params(12),
         cost_estimate=cost(3),
     )(mem, *obs, facts)
+    rest, send = lax.optimization_barrier((rest, send))
+    rest = lax.all_to_all(rest, "mem", 0, 0, tiled=True)
     total = keep + swap(send, "mem", 1)
     for bit in (1, 2, 4, 8):
         total = total + swap(total, "reg", bit)

time: 170 us -> 170 us (level)
  starting transfers between devices: 50.1 us -> 69.9 us
  waiting for transfers between devices: 53.4 us -> 42.6 us
  local copies, waits for them, and re-layouts: 15.3 us -> 6.78 us
    ppermute x14, starting transfers between devices: 20.4 us -> 40.3 us  [send_on(): lax.ppermute(x, 'mem', [(i, (i // 2 + a) % 4 * 2 + (i + b) % 2) for i in...]
    ppermute x14, waiting for transfers between devices: 31.1 us -> 14.6 us  [send_on(): lax.ppermute(x, 'mem', [(i, (i // 2 + a) % 4 * 2 + (i + b) % 2) for i in...]
    unnamed x52 -> x28, local copies, waits for them, and re-layouts: 14.6 us -> 6.07 us
    all_to_all x1, waiting for transfers between devices: 0.01 us -> 5.87 us  [local(): rest = lax.all_to_all(rest, 'mem', 0, 0, tiled=True)]
where the time goes in v7:
time: 170 us; the launch traced here: 169 us
  starting transfers between devices  69.9 us (41%)
  Pallas kernels  49 us (29%)
  waiting for transfers between devices  42.6 us (25%)
  local copies, waits for them, and re-layouts  6.78 us (4%)
    ppermute x14, starting transfers between devices, send_on(): lax.ppermute(x, 'mem', [(i, (i // 2 + a) % 4 * 2 + (i + b) % 2) for i in...  40.3 us
    ppermute x6, waiting for transfers between devices, swap(): return lax.ppermute(x, axis, [(i, i ^ bit) for i in range(count)])  22.1 us
    pallas_call x1, Pallas kernels, local(): pl.pallas_call(interior_kernel, out_shape=[f32(GROUPS, ROWS - EDGE, OWN,...  15.5 us
    ppermute x14, waiting for transfers between devices, send_on(): lax.ppermute(x, 'mem', [(i, (i // 2 + a) % 4 * 2 + (i + b) % 2) for i in...  14.6 us
    pallas_call x1, Pallas kernels, local(): pl.pallas_call(edge_kernel, out_shape=[f32(OWN, HALF_OBS), f32(OWN, HALF_...  11 us
    all_to_all x1, starting transfers between devices, local(): rest = lax.all_to_all(rest, 'mem', 0, 0, tiled=True)  6.88 us
    pallas_call x7, Pallas kernels, place(): pl.pallas_call(place_kernel, grid_spec=pltpu.PrefetchScalarGridSpec(num_s...  6.83 us
    pallas_call x2, Pallas kernels, product(): pl.pallas_call(product_kernel, grid_spec=pltpu.PrefetchScalarGridSpec(num...  6.24 us
  transfers between devices with their start and end apart: 25, of which 14 were waited for; matrix products, arithmetic and copies ran while one was open for 1% of the time, Pallas kernels for 24%

profile of v7, /device:TPU:1, one launch (start us, length us, event | category | flops | bytes accessed | tf_op | source)
XLA Modules:
  0.0 168.7 jit_solution(9628897151620431222)
XLA Ops:
  0.0 4.1 %shard_map.64 = (f32[4,40,1024]{2,1,0:T(8,128)}, f32[4,40,1024]{2,1,0:T(8,128)}) custom-call(s32[1]{0:T(128)} %bitcast.2.parity_ref, f32[32,32,1024]{2,1,0:T(8,128)} %prior_ref.1, f32[32,1024]{1,0:T(8,128)} %h_ref.3, f32[32,1024]{1,0:T(8,128)} %v_ref.3), custom_call_target="tpu_custom_call" | custom-call | tf_op jit(solution)/shard_map/pallas_call | solution.py:409
  4.1 2.5 %collective-permute-start = (f32[4,40,1024]{2,1,0:T(8,128)}, f32[4,40,1024]{2,1,0:T(8,128)S(1)}, u32[]{:S(2)}, u32[]{:S(2)}) collective-permute-start(f32[4,40,1024]{2,1,0:T(8,128)} %get-tuple-element.48), channel_id=1, source_target_pairs={{0,1},{1,0},{2,3},{3,2},{4,5},{5,4},{6,7},{7,6},{8,9},{9,8},{10,11... | collective-permute-start | bytes 1966088 | tf_op jit(solution)/shard_map/ppermute | solution.py:426
  6.6 4.7 %collective-permute-start.1 = (f32[4,40,1024]{2,1,0:T(8,128)}, f32[4,40,1024]{2,1,0:T(8,128)S(1)}, u32[]{:S(2)}, u32[]{:S(2)}) collective-permute-start(f32[4,40,1024]{2,1,0:T(8,128)} %get-tuple-element.49), channel_id=1, source_target_pairs={{0,15},{1,2},{2,1},{3,4},{4,3},{5,6},{6,5},{7,8},{8,7},{9,10},{10,... | collective-permute-start | bytes 1966088 | tf_op jit(solution)/shard_map/ppermute | solution.py:423
  12.1 5.5 %all-to-all-start.1 = ((f32[8,8,256]{2,1,0:T(8,128)}), f32[8,8,256]{2,1,0:T(8,128)S(1)}, u32[]{:S(2)}, u32[]{:S(2)}) async-start(f32[8,8,256]{2,1,0:T(8,128)} %broadcast_in_dim.10), calls=%async_computation.1 | async-start | bytes 131072 | tf_op jit(solution)/shard_map/all_to_all | solution.py:431
  17.6 15.5 %shard_map.65 = (f32[8,24,32,128]{3,2,1,0:T(8,128)}, f32[8,8,32,128]{3,2,1,0:T(8,128)}, f32[2,8,32,1024]{3,2,1,0:T(8,128)}) custom-call(f32[1024,1024]{1,0:T(8,128)} %bitcast.11, f32[32,1024]{1,0:T(8,128)} %h_ref.3, f32[32,1024]{1,0:T(8,128)} %v_ref.3), custom_call_target="tpu_custom_call" | custom-call | bytes 51000000 | tf_op jit(solution)/shard_map/pallas_call | solution.py:435
  33.2 4.8 %all-to-all-start = ((f32[8,8,32,128]{3,2,1,0:T(8,128)}), f32[8,8,32,128]{3,2,1,0:T(8,128)S(1)}, u32[]{:S(2)}, u32[]{:S(2)}) async-start(f32[8,8,32,128]{3,2,1,0:T(8,128)} %get-tuple-element.50), calls=%async_computation | async-start | bytes 2097152 | tf_op jit(solution)/shard_map/all_to_all | solution.py:457
  38.0 11.0 %shard_map.66 = (f32[32,1024]{1,0:T(8,128)}, f32[32,1024]{1,0:T(8,128)}, f32[8,24,32,128]{3,2,1,0:T(8,128)}) custom-call(s32[1]{0:T(128)} %bitcast.2.parity_ref, s32[1]{0:T(128)} %bitcast.4.core_ref, f32[8,24,32,128]{3,2,1,0:T(8,128)} %get-tuple-element.51.inner_ref, f32[2,8,32,1024]{3,2,1,0:T(8,128)} %get-tuple-element.52.rim_ref, ...), custom_call_target="tpu_custom_call" | custom-call | bytes 39000000 | tf_op jit(solution)/shard_map/pallas_call | solution.py:458
  49.0 2.7 %collective-permute-start.4 = (f32[32,1024]{1,0:T(8,128)}, f32[32,1024]{1,0:T(8,128)S(1)}, u32[]{:S(2)}, u32[]{:S(2)}) collective-permute-start(f32[32,1024]{1,0:T(8,128)} %get-tuple-element.57.refs_0_), channel_id=1, source_target_pairs={{0,96},{16,112},{32,0},{48,16},{64,32},{80,48},{96,64},{112,80},{1... | collective-permute-start | bytes 393224 | tf_op jit(solution)/shard_map/ppermute | solution.py:386
  59.4 2.6 %collective-permute-done.7.refs_6_ = f32[32,1024]{1,0:T(8,128)S(1)} collective-permute-done((f32[32,1024]{1,0:T(8,128)}, f32[32,1024]{1,0:T(8,128)S(1)}, u32[]{:S(2)}, u32[]{:S(2)}) %collective-permute-start.7) | collective-permute-done | bytes 131104 | tf_op jit(solution)/shard_map/ppermute | solution.py:386
  62.0 3.3 %collective-permute-done.6.refs_5_ = f32[32,1024]{1,0:T(8,128)S(1)} collective-permute-done((f32[32,1024]{1,0:T(8,128)}, f32[32,1024]{1,0:T(8,128)S(1)}, u32[]{:S(2)}, u32[]{:S(2)}) %collective-permute-start.6) | collective-permute-done | bytes 131104 | tf_op jit(solution)/shard_map/ppermute | solution.py:386
  68.3 6.9 %all-to-all-start.2 = ((f32[8,24,32,128]{3,2,1,0:T(8,128)}), f32[8,24,32,128]{3,2,1,0:T(8,128)S(1)}, u32[]{:S(2)}, u32[]{:S(2)}) async-start(f32[8,24,32,128]{3,2,1,0:T(8,128)} %get-tuple-element.70), calls=%async_computation.2 | async-start | bytes 6291456 | tf_op jit(solution)/shard_map/all_to_all | solution.py:492
  76.8 4.9 %collective-permute-done.10 = f32[136,256]{1,0:T(8,128)S(1)} collective-permute-done((f32[136,256]{1,0:T(8,128)S(1)}, f32[136,256]{1,0:T(8,128)S(1)}, u32[]{:S(2)}, u32[]{:S(2)}) %collective-permute-start.10) | collective-permute-done | bytes 139296 | tf_op jit(solution)/shard_map/ppermute | solution.py:393
  81.8 5.7 %collective-permute-done.11 = f32[136,256]{1,0:T(8,128)S(1)} collective-permute-done((f32[136,256]{1,0:T(8,128)S(1)}, f32[136,256]{1,0:T(8,128)S(1)}, u32[]{:S(2)}, u32[]{:S(2)}) %collective-permute-start.11) | collective-permute-done | bytes 139296 | tf_op jit(solution)/shard_map/ppermute | solution.py:393
  87.6 4.2 %collective-permute-done.12 = f32[136,256]{1,0:T(8,128)S(1)} collective-permute-done((f32[136,256]{1,0:T(8,128)S(1)}, f32[136,256]{1,0:T(8,128)S(1)}, u32[]{:S(2)}, u32[]{:S(2)}) %collective-permute-start.12) | collective-permute-done | bytes 139296 | tf_op jit(solution)/shard_map/ppermute | solution.py:393
  92.2 5.1 %collective-permute-done.13 = f32[136,256]{1,0:T(8,128)S(1)} collective-permute-done((f32[136,256]{1,0:T(8,128)S(1)}, f32[136,256]{1,0:T(8,128)S(1)}, u32[]{:S(2)}, u32[]{:S(2)}) %collective-permute-start.13) | collective-permute-done | bytes 139296 | tf_op jit(solution)/shard_map/ppermute | solution.py:393
  97.3 4.3 %collective-permute-start.14 = (f32[136,256]{1,0:T(8,128)S(1)}, f32[136,256]{1,0:T(8,128)S(1)}, u32[]{:S(2)}, u32[]{:S(2)}) collective-permute-start(f32[136,256]{1,0:T(8,128)S(1)} %add.96.mine_ref), channel_id=1, source_target_pairs={{0,16},{16,0},{32,48},{48,32},{64,80},{80,64},{96,112},{112,96},{1... | collective-permute-start | bytes 417800 | tf_op jit(solution)/shard_map/ppermute | solution.py:393
  102.6 4.3 %shard_map.68.weights_ref = bf16[2,256,256]{2,1,0:T(8,128)(2,1)S(1)} custom-call(s32[1]{0:T(128)} %bitcast.1.mem_ref, f32[136,256]{1,0:T(8,128)S(1)} %add.96.mine_ref, f32[136,256]{1,0:T(8,128)S(1)} %collective-permute-done.14.other_ref), custom_call_target="tpu_custom_call" | custom-call | bytes 18000000 | tf_op jit(solution)/shard_map/pallas_call | solution.py:498
  106.9 5.9 %all-to-all-done.2.rest_ref = f32[8,24,32,128]{3,2,1,0:T(8,128)S(1)} async-done(((f32[8,24,32,128]{3,2,1,0:T(8,128)}), f32[8,24,32,128]{3,2,1,0:T(8,128)S(1)}, u32[]{:S(2)}, u32[]{:S(2)}) %all-to-all-start.2) | async-done | bytes 3145760 | tf_op jit(solution)/shard_map/all_to_all | solution.py:492
  114.0 3.0 %shard_map.70 = (f32[32,32,1024]{2,1,0:T(8,128)}, f32[32,32,128]{2,1,0:T(8,128)S(1)}, f32[32,32,128]{2,1,0:T(8,128)S(1)}, f32[32,32,128]{2,1,0:T(8,128)}) custom-call(s32[1]{0:T(128)} %bitcast.1.mem_ref, bf16[2,256,256]{2,1,0:T(8,128)(2,1)S(1)} %shard_map.68.weights_ref, f32[8,8,32,128]{3,2,1,0:T(8,128)S(1)} %copy-done.1, ...), custom_call_target="tpu_custom_call" | custom-call | bytes 9000000 | tf_op jit(solution)/shard_map/pallas_call | solution.py:340
  119.7 3.2 %shard_map.69 = (f32[32,32,128]{2,1,0:T(8,128)}, f32[32,32,128]{2,1,0:T(8,128)}, f32[32,32,128]{2,1,0:T(8,128)}, f32[32,32,128]{2,1,0:T(8,128)}) custom-call(s32[1]{0:T(128)} %bitcast.1.mem_ref, bf16[2,256,256]{2,1,0:T(8,128)(2,1)S(1)} %shard_map.68.weights_ref, f32[8,8,32,128]{3,2,1,0:T(8,128)S(1)} %copy-done.1, f32[8,24,32,128]{3,2,1,0:T(8,128)S(1)} %all-to-all-done.2.rest_ref), custom_call_target="tpu_custom_call" | custom-call | bytes 9000000 | tf_op jit(solution)/shard_map/pallas_call | solution.py:340
  122.9 3.9 %collective-permute-start.18 = (f32[32,32,128]{2,1,0:T(8,128)}, f32[32,32,128]{2,1,0:T(8,128)S(1)}, u32[]{:S(2)}, u32[]{:S(2)}) collective-permute-start(f32[32,32,128]{2,1,0:T(8,128)} %get-tuple-element.74), channel_id=1, source_target_pairs={{0,80},{16,64},{32,112},{48,96},{64,16},{80,0},{96,48},{112,32},{1... | collective-permute-start | bytes 1572872 | tf_op jit(solution)/shard_map/ppermute | solution.py:386
  126.9 4.5 %collective-permute-done.20.x_ref = f32[32,32,128]{2,1,0:T(8,128)S(1)} collective-permute-done((f32[32,32,128]{2,1,0:T(8,128)S(1)}, f32[32,32,128]{2,1,0:T(8,128)S(1)}, u32[]{:S(2)}, u32[]{:S(2)}) %collective-permute-start.20) | collective-permute-done | bytes 524320 | tf_op jit(solution)/shard_map/ppermute | solution.py:386
  132.2 24.0 %collective-permute-start.16 = (f32[32,32,128]{2,1,0:T(8,128)}, f32[32,32,128]{2,1,0:T(8,128)S(1)}, u32[]{:S(2)}, u32[]{:S(2)}) collective-permute-start(f32[32,32,128]{2,1,0:T(8,128)} %get-tuple-element.72), channel_id=1, source_target_pairs={{0,112},{16,96},{32,16},{48,0},{64,48},{80,32},{96,80},{112,64},{1... | collective-permute-start | bytes 1572872 | tf_op jit(solution)/shard_map/ppermute | solution.py:386
  161.1 1.9 %shard_map.73.before_ref = f32[32,32,1024]{2,1,0:T(8,128)} custom-call(s32[1]{0:T(128)} %bitcast.8.group_ref, f32[32,32,128]{2,1,0:T(8,128)} %collective-permute-done.19.x_ref, f32[32,32,1024]{2,1,0:T(8,128)} %shard_map.72.before_ref), custom_call_target="tpu_custom_call", output_to_operand_aliasing={{}: (2, {})} | custom-call | bytes 3000000 | tf_op jit(solution)/shard_map/pallas_call | solution.py:363
  (78 shorter events, 30.1 us)
Async XLA Ops:
  4.1 29.0 %collective-permute-start = (f32[4,40,1024]{2,1,0:T(8,128)}, f32[4,40,1024]{2,1,0:T(8,128)S(1)}, u32[]{:S(2)}, u32[]{:S(2)}) collective-permute-start(f32[4,40,1024]{2,1,0:T(8,128)} %get-tuple-element.48), channel_id=1, source_target_pairs={{0,1},{1,0},{2,3},{3,2},{4,5},{5,4},{6,7},{7,6},{8,9},{9,8},{10,11... | collective-permute-start | bytes 1966088 | tf_op jit(solution)/shard_map/ppermute | solution.py:426
  6.6 26.5 %collective-permute-start.1 = (f32[4,40,1024]{2,1,0:T(8,128)}, f32[4,40,1024]{2,1,0:T(8,128)S(1)}, u32[]{:S(2)}, u32[]{:S(2)}) collective-permute-start(f32[4,40,1024]{2,1,0:T(8,128)} %get-tuple-element.49), channel_id=1, source_target_pairs={{0,15},{1,2},{2,1},{3,4},{4,3},{5,6},{6,5},{7,8},{8,7},{9,10},{10,... | collective-permute-start | bytes 1966088 | tf_op jit(solution)/shard_map/ppermute | solution.py:423
  12.1 21.0 %all-to-all-start.1 = ((f32[8,8,256]{2,1,0:T(8,128)}), f32[8,8,256]{2,1,0:T(8,128)S(1)}, u32[]{:S(2)}, u32[]{:S(2)}) async-start(f32[8,8,256]{2,1,0:T(8,128)} %broadcast_in_dim.10), calls=%async_computation.1 | async-start | bytes 131072 | tf_op jit(solution)/shard_map/all_to_all | solution.py:431
  33.2 32.2 %all-to-all-start = ((f32[8,8,32,128]{3,2,1,0:T(8,128)}), f32[8,8,32,128]{3,2,1,0:T(8,128)S(1)}, u32[]{:S(2)}, u32[]{:S(2)}) async-start(f32[8,8,32,128]{3,2,1,0:T(8,128)} %get-tuple-element.50), calls=%async_computation | async-start | bytes 2097152 | tf_op jit(solution)/shard_map/all_to_all | solution.py:457
  49.0 6.4 %collective-permute-start.4 = (f32[32,1024]{1,0:T(8,128)}, f32[32,1024]{1,0:T(8,128)S(1)}, u32[]{:S(2)}, u32[]{:S(2)}) collective-permute-start(f32[32,1024]{1,0:T(8,128)} %get-tuple-element.57.refs_0_), channel_id=1, source_target_pairs={{0,96},{16,112},{32,0},{48,16},{64,32},{80,48},{96,64},{112,80},{1... | collective-permute-start | bytes 393224 | tf_op jit(solution)/shard_map/ppermute | solution.py:386
  51.7 7.1 %collective-permute-start.3 = (f32[32,1024]{1,0:T(8,128)}, f32[32,1024]{1,0:T(8,128)S(1)}, u32[]{:S(2)}, u32[]{:S(2)}) collective-permute-start(f32[32,1024]{1,0:T(8,128)} %get-tuple-element.57.refs_0_), channel_id=1, source_target_pairs={{0,32},{16,48},{32,64},{48,80},{64,96},{80,112},{96,0},{112,16},{1... | collective-permute-start | bytes 393224 | tf_op jit(solution)/shard_map/ppermute | solution.py:386
  51.7 7.7 %collective-permute-start.2 = (f32[32,1024]{1,0:T(8,128)}, f32[32,1024]{1,0:T(8,128)S(1)}, u32[]{:S(2)}, u32[]{:S(2)}) collective-permute-start(f32[32,1024]{1,0:T(8,128)} %get-tuple-element.57.refs_0_), channel_id=1, source_target_pairs={{0,64},{16,80},{32,96},{48,112},{64,0},{80,16},{96,32},{112,48},{1... | collective-permute-start | bytes 393224 | tf_op jit(solution)/shard_map/ppermute | solution.py:386
  53.4 6.0 %collective-permute-start.8 = (f32[32,1024]{1,0:T(8,128)}, f32[32,1024]{1,0:T(8,128)S(1)}, u32[]{:S(2)}, u32[]{:S(2)}) collective-permute-start(f32[32,1024]{1,0:T(8,128)} %get-tuple-element.56), channel_id=1, source_target_pairs={{0,16},{16,0},{32,48},{48,32},{64,80},{80,64},{96,112},{112,96},{1... | collective-permute-start | bytes 393224 | tf_op jit(solution)/shard_map/ppermute | solution.py:386
  54.6 7.4 %collective-permute-start.7 = (f32[32,1024]{1,0:T(8,128)}, f32[32,1024]{1,0:T(8,128)S(1)}, u32[]{:S(2)}, u32[]{:S(2)}) collective-permute-start(f32[32,1024]{1,0:T(8,128)} %get-tuple-element.56), channel_id=1, source_target_pairs={{0,112},{16,96},{32,16},{48,0},{64,48},{80,32},{96,80},{112,64},{1... | collective-permute-start | bytes 393224 | tf_op jit(solution)/shard_map/ppermute | solution.py:386
  55.4 9.9 %collective-permute-start.6 = (f32[32,1024]{1,0:T(8,128)}, f32[32,1024]{1,0:T(8,128)S(1)}, u32[]{:S(2)}, u32[]{:S(2)}) collective-permute-start(f32[32,1024]{1,0:T(8,128)} %get-tuple-element.56), channel_id=1, source_target_pairs={{0,48},{16,32},{32,80},{48,64},{64,112},{80,96},{96,16},{112,0},{1... | collective-permute-start | bytes 393224 | tf_op jit(solution)/shard_map/ppermute | solution.py:386
  58.7 6.6 %collective-permute-start.5 = (f32[32,1024]{1,0:T(8,128)}, f32[32,1024]{1,0:T(8,128)S(1)}, u32[]{:S(2)}, u32[]{:S(2)}) collective-permute-start(f32[32,1024]{1,0:T(8,128)} %get-tuple-element.56), channel_id=1, source_target_pairs={{0,80},{16,64},{32,112},{48,96},{64,16},{80,0},{96,48},{112,32},{1... | collective-permute-start | bytes 393224 | tf_op jit(solution)/shard_map/ppermute | solution.py:386
  68.3 44.5 %all-to-all-start.2 = ((f32[8,24,32,128]{3,2,1,0:T(8,128)}), f32[8,24,32,128]{3,2,1,0:T(8,128)S(1)}, u32[]{:S(2)}, u32[]{:S(2)}) async-start(f32[8,24,32,128]{3,2,1,0:T(8,128)} %get-tuple-element.70), calls=%async_computation.2 | async-start | bytes 6291456 | tf_op jit(solution)/shard_map/all_to_all | solution.py:492
  76.7 5.0 %collective-permute-start.10 = (f32[136,256]{1,0:T(8,128)S(1)}, f32[136,256]{1,0:T(8,128)S(1)}, u32[]{:S(2)}, u32[]{:S(2)}) collective-permute-start(f32[136,256]{1,0:T(8,128)S(1)} %add.92), channel_id=1, source_target_pairs={{0,1},{1,0},{2,3},{3,2},{4,5},{5,4},{6,7},{7,6},{8,9},{9,8},{10,11... | collective-permute-start | bytes 417800 | tf_op jit(solution)/shard_map/ppermute | solution.py:393
  81.7 5.8 %collective-permute-start.11 = (f32[136,256]{1,0:T(8,128)S(1)}, f32[136,256]{1,0:T(8,128)S(1)}, u32[]{:S(2)}, u32[]{:S(2)}) collective-permute-start(f32[136,256]{1,0:T(8,128)S(1)} %add.93), channel_id=1, source_target_pairs={{0,2},{1,3},{2,0},{3,1},{4,6},{5,7},{6,4},{7,5},{8,10},{9,11},{10,... | collective-permute-start | bytes 417800 | tf_op jit(solution)/shard_map/ppermute | solution.py:393
  87.5 4.3 %collective-permute-start.12 = (f32[136,256]{1,0:T(8,128)S(1)}, f32[136,256]{1,0:T(8,128)S(1)}, u32[]{:S(2)}, u32[]{:S(2)}) collective-permute-start(f32[136,256]{1,0:T(8,128)S(1)} %add.94), channel_id=1, source_target_pairs={{0,4},{1,5},{2,6},{3,7},{4,0},{5,1},{6,2},{7,3},{8,12},{9,13},{10,... | collective-permute-start | bytes 417800 | tf_op jit(solution)/shard_map/ppermute | solution.py:393
  91.8 5.5 %collective-permute-start.13 = (f32[136,256]{1,0:T(8,128)S(1)}, f32[136,256]{1,0:T(8,128)S(1)}, u32[]{:S(2)}, u32[]{:S(2)}) collective-permute-start(f32[136,256]{1,0:T(8,128)S(1)} %add.95), channel_id=1, source_target_pairs={{0,8},{1,9},{2,10},{3,11},{4,12},{5,13},{6,14},{7,15},{8,0},{9,1},... | collective-permute-start | bytes 417800 | tf_op jit(solution)/shard_map/ppermute | solution.py:393
  97.3 5.3 %collective-permute-start.14 = (f32[136,256]{1,0:T(8,128)S(1)}, f32[136,256]{1,0:T(8,128)S(1)}, u32[]{:S(2)}, u32[]{:S(2)}) collective-permute-start(f32[136,256]{1,0:T(8,128)S(1)} %add.96.mine_ref), channel_id=1, source_target_pairs={{0,16},{16,0},{32,48},{48,32},{64,80},{80,64},{96,112},{112,96},{1... | collective-permute-start | bytes 417800 | tf_op jit(solution)/shard_map/ppermute | solution.py:393
  117.0 14.4 %collective-permute-start.20 = (f32[32,32,128]{2,1,0:T(8,128)S(1)}, f32[32,32,128]{2,1,0:T(8,128)S(1)}, u32[]{:S(2)}, u32[]{:S(2)}) collective-permute-start(f32[32,32,128]{2,1,0:T(8,128)S(1)} %get-tuple-element.76), channel_id=1, source_target_pairs={{0,32},{16,48},{32,64},{48,80},{64,96},{80,112},{96,0},{112,16},{1... | collective-permute-start | bytes 1572872 | tf_op jit(solution)/shard_map/ppermute | solution.py:386
  117.3 38.9 %collective-permute-start.21 = (f32[32,32,128]{2,1,0:T(8,128)S(1)}, f32[32,32,128]{2,1,0:T(8,128)S(1)}, u32[]{:S(2)}, u32[]{:S(2)}) collective-permute-start(f32[32,32,128]{2,1,0:T(8,128)S(1)} %get-tuple-element.77), channel_id=1, source_target_pairs={{0,64},{16,80},{32,96},{48,112},{64,0},{80,16},{96,32},{112,48},{1... | collective-permute-start | bytes 1572872 | tf_op jit(solution)/shard_map/ppermute | solution.py:386
  119.0 42.0 %collective-permute-start.19 = (f32[32,32,128]{2,1,0:T(8,128)}, f32[32,32,128]{2,1,0:T(8,128)}, u32[]{:S(2)}, u32[]{:S(2)}) collective-permute-start(f32[32,32,128]{2,1,0:T(8,128)} %get-tuple-element.75), channel_id=1, source_target_pairs={{0,96},{16,112},{32,0},{48,16},{64,32},{80,48},{96,64},{112,80},{1... | collective-permute-start | bytes 1572872 | tf_op jit(solution)/shard_map/ppermute | solution.py:386
  122.9 40.0 %collective-permute-start.18 = (f32[32,32,128]{2,1,0:T(8,128)}, f32[32,32,128]{2,1,0:T(8,128)S(1)}, u32[]{:S(2)}, u32[]{:S(2)}) collective-permute-start(f32[32,32,128]{2,1,0:T(8,128)} %get-tuple-element.74), channel_id=1, source_target_pairs={{0,80},{16,64},{32,112},{48,96},{64,16},{80,0},{96,48},{112,32},{1... | collective-permute-start | bytes 1572872 | tf_op jit(solution)/shard_map/ppermute | solution.py:386
  126.9 38.7 %collective-permute-start.17 = (f32[32,32,128]{2,1,0:T(8,128)}, f32[32,32,128]{2,1,0:T(8,128)S(1)}, u32[]{:S(2)}, u32[]{:S(2)}) collective-permute-start(f32[32,32,128]{2,1,0:T(8,128)} %get-tuple-element.73), channel_id=1, source_target_pairs={{0,48},{16,32},{32,80},{48,64},{64,112},{80,96},{96,16},{112,0},{1... | collective-permute-start | bytes 1572872 | tf_op jit(solution)/shard_map/ppermute | solution.py:386
  132.2 34.9 %collective-permute-start.16 = (f32[32,32,128]{2,1,0:T(8,128)}, f32[32,32,128]{2,1,0:T(8,128)S(1)}, u32[]{:S(2)}, u32[]{:S(2)}) collective-permute-start(f32[32,32,128]{2,1,0:T(8,128)} %get-tuple-element.72), channel_id=1, source_target_pairs={{0,112},{16,96},{32,16},{48,0},{64,48},{80,32},{96,80},{112,64},{1... | collective-permute-start | bytes 1572872 | tf_op jit(solution)/shard_map/ppermute | solution.py:386
  157.0 10.9 %collective-permute-start.15 = (f32[32,32,128]{2,1,0:T(8,128)}, f32[32,32,128]{2,1,0:T(8,128)S(1)}, u32[]{:S(2)}, u32[]{:S(2)}) collective-permute-start(f32[32,32,128]{2,1,0:T(8,128)} %get-tuple-element.71), channel_id=1, source_target_pairs={{0,16},{16,0},{32,48},{48,32},{64,80},{80,64},{96,112},{112,96},{1... | collective-permute-start | bytes 1572872 | tf_op jit(solution)/shard_map/ppermute | solution.py:386
  (15 other events, 60.1 us)

commit v8 on v7

--- a/solution.py
+++ b/solution.py
@@ -95,89 +95,76 @@
     lax.fori_loop(0, -(-(last - first) // HALO), body, 0)
 
 
-def pack_kernel(parity_ref, prior_ref, h_ref, v_ref, a_ref, b_ref, given, sems):
-    copies = []
-    for side in range(2):
-        rows = slice(side * (ROWS - SUB), side * (ROWS - SUB) + SUB)
-        copies.append(
-            [
-                pltpu.make_async_copy(
-                    prior_ref.at[:, rows, j * LANES : (j + 1) * LANES],
-                    given.at[side, j],
-                    sems.at[side, j],
-                )
-                for j in range(GROUPS)
-            ]
-        )
-    for j in range(GROUPS):
-        for side in range(2):
-            copies[side][j].start()
-    for side in range(2):
-        for copy in copies[side]:
-            copy.wait()
-    parity = parity_ref[0]
-    for even in range(2):
-
-        @pl.when(parity == 1 - even)
-        def _():
-            for side in range(2):
-                out_ref = a_ref if side == even else b_ref
-                first = side * (ROWS - HALO)
-                for i in range(HALO):
-                    for j in range(GROUPS):
-                        x = given.at[side, j].reshape(OWN * SUB, LANES)[
-                            pl.ds(side * (SUB - HALO) + i, OWN, stride=SUB), :
-                        ]
-                        out_ref[i, :OWN, j * LANES : (j + 1) * LANES] = x
-                    out_ref[i, OWN : OWN + 1] = h_ref[first + i : first + i + 1]
-                    out_ref[i, OWN + 1 : OWN + 2] = v_ref[first + i : first + i + 1]
-
-
-def interior_kernel(
-    prior_ref, h_ref, v_ref,
-    inner_ref, early_ref, rim_ref, given, one, two, field, coef_ref, sems, out_sems,
+def turn_kernel(
+    parity_ref, prior_ref, h_ref, v_ref, a_ref, b_ref, turned_ref, given, one, sems, out_sems
 ):
-    copies = [
+    loads = [
         pltpu.make_async_copy(
             prior_ref.at[:, j * LANES : (j + 1) * LANES], given.at[j], sems.at[j]
         )
         for j in range(GROUPS)
     ]
-    for copy in copies:
-        copy.start()
+    for load in loads:
+        load.start()
+    stores = []
+    for j in range(GROUPS):
+        at = slice(j * LANES, (j + 1) * LANES)
+        loads[j].wait()
+        for i in range(ROWS):
+            one[i, :, at] = given[j, pl.ds(i, OWN, stride=ROWS), :]
+        stores.append(
+            pltpu.make_async_copy(one.at[:, :, at], turned_ref.at[:, :, at], out_sems.at[j])
+        )
+        stores[j].start()
+    parity = parity_ref[0]
+    for even in range(2):
+
+        @pl.when(parity == 1 - even)
+        def _():
+            for side in range(2):
+                out_ref = a_ref if side == even else b_ref
+                for i in range(HALO):
+                    row = side * (ROWS - HALO) + i
+                    out_ref[i, :OWN] = one[row]
+                    out_ref[i, OWN : OWN + 1] = h_ref[row : row + 1]
+                    out_ref[i, OWN + 1 : OWN + 2] = v_ref[row : row + 1]
+
+    for store in stores:
+        store.wait()
+
+
+def interior_kernel(
+    turned_ref, h_ref, v_ref,
+    inner_ref, early_ref, one, two, field, coef_ref, sems, out_sems,
+):
+    loads = [
+        pltpu.make_async_copy(
+            turned_ref.at[n * CHUNK : (n + 1) * CHUNK],
+            one.at[n * CHUNK : (n + 1) * CHUNK],
+            sems.at[n],
+        )
+        for n in range(ROWS // CHUNK)
+    ]
+    for load in loads:
+        load.start()
     for i in range(ROWS):
         coefficients(h_ref[i : i + 1], v_ref[i : i + 1], coef_ref, i)
-    for j in range(GROUPS):
-        at = slice(j * LANES, (j + 1) * LANES)
-        copies[j].wait()
-        for i in range(ROWS):
-            one[i, :, at] = given[j, pl.ds(i, OWN, stride=ROWS), :]
-    rims = [
-        pltpu.make_async_copy(
-            one.at[side * (ROWS - EDGE) : side * (ROWS - EDGE) + EDGE],
-            rim_ref.at[side],
-            out_sems.at[side],
-        )
-        for side in range(2)
-    ]
-    for copy in rims:
-        copy.start()
-    advance(one, two, coef_ref, 1, ROWS - 1, 0, False)
-    for copy in rims:
-        copy.wait()
+    for n, load in enumerate(loads):
+        load.wait()
+        advance(one, two, coef_ref, max(n * CHUNK - 1, 1), (n + 1) * CHUNK - 1, 0, False)
     advance(two, one, coef_ref, 2, ROWS - 2, 0, False)
     advance(one, two, coef_ref, 3, ROWS - 3, 0, False)
     advance(two, field, coef_ref, CHUNK, 2 * CHUNK, -HALO, True)
     early = pltpu.make_async_copy(
-        field.at[:, CHUNK - HALO : 2 * CHUNK - HALO], early_ref, out_sems.at[2]
+        field.at[:, CHUNK - HALO : 2 * CHUNK - HALO], early_ref, out_sems.at[0]
     )
     early.start()
     advance(two, field, coef_ref, HALO, CHUNK, -HALO, True)
     middle = 2 * CHUNK - HALO
-    upper = pltpu.make_async_copy(field.at[:, :middle], inner_ref.at[:, :middle], out_sems.at[3])
+    upper = pltpu.make_async_copy(field.at[:, :middle], inner_ref.at[:, :middle], out_sems.at[1])
     upper.start()
     advance(two, field, coef_ref, 2 * CHUNK, ROWS - HALO, -HALO, True)
-    lower = pltpu.make_async_copy(field.at[:, middle:], inner_ref.at[:, middle:], out_sems.at[4])
+    lower = pltpu.make_async_copy(field.at[:, middle:], inner_ref.at[:, middle:], out_sems.at[2])
     lower.start()
     early.wait()
     upper.wait()
@@ -185,21 +172,30 @@
 
 
 def edge_kernel(
-    parity_ref, core_ref, inner_ref, rim_ref, a_ref, b_ref, h_ref, v_ref, facts_ref,
-    same_ref, flip_ref, rest_ref, obs_ref, field, one, two, coef_ref, in_sem, out_sems,
+    parity_ref, core_ref, inner_ref, turned_ref, a_ref, b_ref, h_ref, v_ref, facts_ref,
+    same_ref, flip_ref, rest_ref, obs_ref, field, ones, two, coef_ref, in_sem, out_sems, own_sems,
 ):
     load = pltpu.make_async_copy(inner_ref, field.at[:, HALO : ROWS - HALO], in_sem)
     load.start()
+    owns = [
+        pltpu.make_async_copy(
+            turned_ref.at[side * (ROWS - EDGE) : side * (ROWS - EDGE) + EDGE],
+            ones.at[side, (1 - side) * HALO : (1 - side) * HALO + EDGE],
+            own_sems.at[side],
+        )
+        for side in range(2)
+    ]
+    for own in owns:
+        own.start()
     odd = parity_ref[0] == 1
     for side, (near_ref, far_ref, halo_at, own_at, own_first) in enumerate(
         ((a_ref, b_ref, 0, HALO, 0), (b_ref, a_ref, EDGE, 0, ROWS - EDGE))
     ):
         for i in range(HALO):
             halo = jnp.where(odd, near_ref[i], far_ref[i])
-            one[halo_at + i] = halo[:OWN]
+            ones[side, halo_at + i] = halo[:OWN]
             coefficients(halo[OWN : OWN + 1], halo[OWN + 1 : OWN + 2], coef_ref, halo_at + i)
         for i in range(EDGE):
-            one[own_at + i] = rim_ref[side, i]
             coefficients(
                 h_ref[own_first + i : own_first + i + 1],
                 v_ref[own_first + i : own_first + i + 1],
@@ -207,6 +203,8 @@
                 own_at + i,
             )
         last = HALO + EDGE
+        one = ones.at[side]
+        owns[side].wait()
         advance(one, two, coef_ref, 1, last - 1, 0, False)
         advance(two, one, coef_ref, 2, last - 2, 0, False)
         advance(one, two, coef_ref, 3, last - 3, 0, False)
@@ -330,12 +328,9 @@
     pl.when(step != 1)(lambda: compute(rest_ref))
 
 
-def product(mem, weights, early, rest, part):
-    outs = [pl.BlockSpec((OWN, CHUNK, LANES), lambda n, g: (0, n, 0))] * (N_MEM // 2)
-    shapes = [f32(OWN, ROWS, LANES)] * (N_MEM // 2)
-    if part == 0:
-        outs[0] = pl.BlockSpec((OWN, CHUNK, LANES), lambda n, g: (0, n, g[0]))
-        shapes[0] = f32(OWN, ROWS, WIDTH)
+def product(mem, weights, early, rest):
+    outs = [pl.BlockSpec((OWN, CHUNK, LANES), lambda n, g: (0, n, g[0]))]
+    outs += [pl.BlockSpec((OWN, CHUNK, LANES), lambda n, g: (0, n, 0))] * (N_MEM - 1)
     block = (N_MEM, CHUNK, OWN, LANES)
     return pl.pallas_call(
         product_kernel,
@@ -343,15 +338,15 @@
             num_scalar_prefetch=1,
             grid=(ROWS // CHUNK,),
             in_specs=[
-                pl.BlockSpec((2, MEMBERS // 2, MEMBERS), lambda n, g: (0, part, 0)),
+                pl.BlockSpec((2, MEMBERS, MEMBERS), lambda n, g: (0, 0, 0)),
                 pl.BlockSpec(block, lambda n, g: (0, 0, 0, 0)),
                 pl.BlockSpec(block, lambda n, g: (0, jnp.maximum(n - 1, 0), 0, 0)),
             ],
             out_specs=outs,
         ),
-        out_shape=shapes,
-        compiler_params=params(16),
-        cost_estimate=cost(3),
+        out_shape=[f32(OWN, ROWS, WIDTH)] + [f32(OWN, ROWS, LANES)] * (N_MEM - 1),
+        compiler_params=params(20),
+        cost_estimate=cost(6),
     )(mem, weights, early, rest)
 
 
@@ -406,20 +401,20 @@
     ]
     mem = mem.reshape(1)
 
-    halo_a, halo_b = pl.pallas_call(
-        pack_kernel,
-        out_shape=[f32(HALO, OWN + SUB, WIDTH)] * 2,
+    halo_a, halo_b, turned = pl.pallas_call(
+        turn_kernel,
+        out_shape=[f32(HALO, OWN + SUB, WIDTH)] * 2 + [f32(ROWS, OWN, WIDTH)],
         in_specs=[SMEM, anywhere, VMEM, VMEM],
-        out_specs=[VMEM, VMEM],
+        out_specs=[VMEM, VMEM, anywhere],
         scratch_shapes=[
-            pltpu.VMEM((2, GROUPS, OWN, SUB, LANES), jnp.float32),
-            pltpu.SemaphoreType.DMA((2, GROUPS)),
+            pltpu.VMEM((GROUPS, OWN * ROWS, LANES), jnp.float32),
+            pltpu.VMEM((ROWS, OWN, WIDTH), jnp.float32),
+            pltpu.SemaphoreType.DMA((GROUPS,)),
+            pltpu.SemaphoreType.DMA((GROUPS,)),
         ],
         compiler_params=params(56),
-    )(parity, prior_samples, h, v)
-    halo_a, halo_b, prior_samples, h, v = lax.optimization_barrier(
-        (halo_a, halo_b, prior_samples, h, v)
-    )
+    )(parity, prior_samples.reshape(OWN * ROWS, WIDTH), h, v)
+    halo_a, halo_b, turned, h, v = lax.optimization_barrier((halo_a, halo_b, turned, h, v))
     halo_b = lax.ppermute(
         halo_b, "reg", [(i, (i - 1 if i % 2 == 0 else i + 1) % N_REG) for i in range(N_REG)]
     )
@@ -432,27 +427,25 @@
         jnp.broadcast_to(facts[None], (N_MEM, SUB, OBS)), "mem", 0, 0, tiled=True
     )
 
-    inner, early, rim = pl.pallas_call(
+    inner, early = pl.pallas_call(
         interior_kernel,
         out_shape=[
             f32(GROUPS, ROWS - EDGE, OWN, LANES),
             f32(GROUPS, CHUNK, OWN, LANES),
-            f32(2, EDGE, OWN, WIDTH),
         ],
         in_specs=[anywhere, VMEM, VMEM],
-        out_specs=[anywhere] * 3,
+        out_specs=[anywhere] * 2,
         scratch_shapes=[
-            pltpu.VMEM((GROUPS, OWN * ROWS, LANES), jnp.float32),
             pltpu.VMEM((ROWS, OWN, WIDTH), jnp.float32),
             pltpu.VMEM((ROWS, OWN, WIDTH), jnp.float32),
             pltpu.VMEM((GROUPS, ROWS - EDGE, OWN, LANES), jnp.float32),
             pltpu.VMEM((2, ROWS, SUB, WIDTH), jnp.float32),
-            pltpu.SemaphoreType.DMA((GROUPS,)),
-            pltpu.SemaphoreType.DMA((5,)),
+            pltpu.SemaphoreType.DMA((ROWS // CHUNK,)),
+            pltpu.SemaphoreType.DMA((3,)),
         ],
         compiler_params=params(56),
-        cost_estimate=cost(17),
-    )(prior_samples.reshape(OWN * ROWS, WIDTH), h, v)
+        cost_estimate=cost(13),
+    )(turned, h, v)
     early, halo_a, halo_b = lax.optimization_barrier((early, halo_a, halo_b))
     early = lax.all_to_all(early, "mem", 0, 0, tiled=True)
     same, flip, rest = pl.pallas_call(
@@ -462,20 +455,21 @@
             f32(OWN, HALF_OBS),
             f32(GROUPS, ROWS - CHUNK, OWN, LANES),
         ],
-        in_specs=[SMEM, SMEM, anywhere] + [VMEM] * 6,
+        in_specs=[SMEM, SMEM, anywhere, anywhere] + [VMEM] * 5,
         out_specs=[VMEM, VMEM, anywhere],
         scratch_shapes=[
             pltpu.VMEM((2, OWN, HALF_OBS), jnp.float32),
             pltpu.VMEM((GROUPS, ROWS, OWN, LANES), jnp.float32),
-            pltpu.VMEM((HALO + EDGE, OWN, WIDTH), jnp.float32),
+            pltpu.VMEM((2, HALO + EDGE, OWN, WIDTH), jnp.float32),
             pltpu.VMEM((HALO + EDGE, OWN, WIDTH), jnp.float32),
             pltpu.VMEM((2, HALO + EDGE, SUB, WIDTH), jnp.float32),
             pltpu.SemaphoreType.DMA,
             pltpu.SemaphoreType.DMA((2,)),
+            pltpu.SemaphoreType.DMA((2,)),
         ],
         compiler_params=params(56),
         cost_estimate=cost(13),
-    )(parity, core, inner, rim, halo_a, halo_b, h, v, facts)
+    )(parity, core, inner, turned, halo_a, halo_b, h, v, facts)
     obs = [same] + [send_on(flip if b else same, a, b) for a, b in PATHS[1:]]
     early, *obs = lax.optimization_barrier((early, *obs))
 
@@ -505,8 +499,7 @@
         cost_estimate=cost(6),
     )(mem, total, other)
 
-    result, *analysis = product(mem, weights, early, rest, 0)
-    analysis = analysis + list(product(mem, weights, early, rest, 1))
+    result, *analysis = product(mem, weights, early, rest)
     for x, (a, b), source in zip(analysis, PATHS[1:], sources[1:]):
         arrived = send_on(x, a, b)
         result = place(arrived, source, result)

time: 170 us -> 168 us (0.988)
  waiting for transfers between devices: 42.6 us -> 45.5 us
  Pallas kernels: 49 us -> 46.2 us
    ppermute x14, waiting for transfers between devices: 14.6 us -> 17.1 us  [send_on(): lax.ppermute(x, 'mem', [(i, (i // 2 + a) % 4 * 2 + (i + b) % 2) for i in...]
    pallas_call x1, Pallas kernels: 4.05 us -> 6.51 us  [local(): pl.pallas_call(turn_kernel, out_shape=[f32(HALO, OWN + SUB, WIDTH)] * 2 +...]
    all_to_all x1, starting transfers between devices: 6.88 us -> 4.53 us  [local(): rest = lax.all_to_all(rest, 'mem', 0, 0, tiled=True)]
    pallas_call x1, Pallas kernels: 15.5 us -> 13.2 us  [local(): pl.pallas_call(interior_kernel, out_shape=[f32(GROUPS, ROWS - EDGE, OWN,...]
    pallas_call x2 -> x1, Pallas kernels: 6.24 us -> 3.96 us  [product(): pl.pallas_call(product_kernel, grid_spec=pltpu.PrefetchScalarGridSpec(num...]
    ppermute x14, starting transfers between devices: 40.3 us -> 42.2 us  [send_on(): lax.ppermute(x, 'mem', [(i, (i // 2 + a) % 4 * 2 + (i + b) % 2) for i in...]
    unnamed x28 -> x24, local copies, waits for them, and re-layouts: 6.07 us -> 4.92 us
  transfers between devices with their start and end apart: 25 -> 25, of which waited for: 14 -> 12; matrix products, arithmetic and copies ran while one was open for 1% -> 1% of each run, Pallas kernels for 24% -> 20%
where the time goes in v8:
time: 168 us; the launch traced here: 167 us
  starting transfers between devices  69.1 us (41%)
  Pallas kernels  46.2 us (28%)
  waiting for transfers between devices  45.5 us (27%)
  local copies, waits for them, and re-layouts  5.63 us (3%)
    ppermute x14, starting transfers between devices, send_on(): lax.ppermute(x, 'mem', [(i, (i // 2 + a) % 4 * 2 + (i + b) % 2) for i in...  42.2 us
    ppermute x6, waiting for transfers between devices, swap(): return lax.ppermute(x, axis, [(i, i ^ bit) for i in range(count)])  22.3 us
    ppermute x14, waiting for transfers between devices, send_on(): lax.ppermute(x, 'mem', [(i, (i // 2 + a) % 4 * 2 + (i + b) % 2) for i in...  17.1 us
    pallas_call x1, Pallas kernels, local(): pl.pallas_call(interior_kernel, out_shape=[f32(GROUPS, ROWS - EDGE, OWN,...  13.2 us
    pallas_call x1, Pallas kernels, local(): pl.pallas_call(edge_kernel, out_shape=[f32(OWN, HALF_OBS), f32(OWN, HALF_...  11.4 us
    pallas_call x1, Pallas kernels, local(): pl.pallas_call(turn_kernel, out_shape=[f32(HALO, OWN + SUB, WIDTH)] * 2 +...  6.51 us
    all_to_all x1, waiting for transfers between devices, local(): rest = lax.all_to_all(rest, 'mem', 0, 0, tiled=True)  6.1 us
    pallas_call x7, Pallas kernels, place(): pl.pallas_call(place_kernel, grid_spec=pltpu.PrefetchScalarGridSpec(num_s...  5.79 us
  transfers between devices with their start and end apart: 25, of which 12 were waited for; matrix products, arithmetic and copies ran while one was open for 1% of the time, Pallas kernels for 20%

profile of v8, /device:TPU:1, one launch (start us, length us, event | category | flops | bytes accessed | tf_op | source)
XLA Modules:
  0.0 166.9 jit_solution(13143254297672218540)
XLA Ops:
  0.0 6.5 %shard_map.64 = (f32[4,40,1024]{2,1,0:T(8,128)}, f32[4,40,1024]{2,1,0:T(8,128)}, f32[32,32,1024]{2,1,0:T(8,128)}) custom-call(s32[1]{0:T(128)} %bitcast.2.parity_ref, f32[1024,1024]{1,0:T(8,128)} %bitcast.11, f32[32,1024]{1,0:T(8,128)} %h_ref.3, f32[32,1024]{1,0:T(8,128)} %v_ref.3), custom_call_target="tpu_custom_call" | custom-call | tf_op jit(solution)/shard_map/pallas_call | solution.py:404
  6.5 2.5 %collective-permute-start = (f32[4,40,1024]{2,1,0:T(8,128)}, f32[4,40,1024]{2,1,0:T(8,128)S(1)}, u32[]{:S(2)}, u32[]{:S(2)}) collective-permute-start(f32[4,40,1024]{2,1,0:T(8,128)} %get-tuple-element.49), channel_id=1, source_target_pairs={{0,1},{1,0},{2,3},{3,2},{4,5},{5,4},{6,7},{7,6},{8,9},{9,8},{10,11... | collective-permute-start | bytes 1966088 | tf_op jit(solution)/shard_map/ppermute | solution.py:421
  9.1 4.7 %collective-permute-start.1 = (f32[4,40,1024]{2,1,0:T(8,128)}, f32[4,40,1024]{2,1,0:T(8,128)S(1)}, u32[]{:S(2)}, u32[]{:S(2)}) collective-permute-start(f32[4,40,1024]{2,1,0:T(8,128)} %get-tuple-element.50), channel_id=1, source_target_pairs={{0,15},{1,2},{2,1},{3,4},{4,3},{5,6},{6,5},{7,8},{8,7},{9,10},{10,... | collective-permute-start | bytes 1966088 | tf_op jit(solution)/shard_map/ppermute | solution.py:418
  14.6 5.5 %all-to-all-start.1 = ((f32[8,8,256]{2,1,0:T(8,128)}), f32[8,8,256]{2,1,0:T(8,128)S(1)}, u32[]{:S(2)}, u32[]{:S(2)}) async-start(f32[8,8,256]{2,1,0:T(8,128)} %broadcast_in_dim.10), calls=%async_computation.1 | async-start | bytes 131072 | tf_op jit(solution)/shard_map/all_to_all | solution.py:426
  20.1 13.2 %shard_map.65 = (f32[8,24,32,128]{3,2,1,0:T(8,128)}, f32[8,8,32,128]{3,2,1,0:T(8,128)}) custom-call(f32[32,32,1024]{2,1,0:T(8,128)} %get-tuple-element.45.turned_ref, f32[32,1024]{1,0:T(8,128)} %h_ref.3, f32[32,1024]{1,0:T(8,128)} %v_ref.3), custom_call_target="tpu_custom_call" | custom-call | bytes 39000000 | tf_op jit(solution)/shard_map/pallas_call | solution.py:430
  33.3 4.8 %all-to-all-start = ((f32[8,8,32,128]{3,2,1,0:T(8,128)}), f32[8,8,32,128]{3,2,1,0:T(8,128)S(1)}, u32[]{:S(2)}, u32[]{:S(2)}) async-start(f32[8,8,32,128]{3,2,1,0:T(8,128)} %get-tuple-element.51), calls=%async_computation | async-start | bytes 2097152 | tf_op jit(solution)/shard_map/all_to_all | solution.py:450
  38.2 11.4 %shard_map.66 = (f32[32,1024]{1,0:T(8,128)}, f32[32,1024]{1,0:T(8,128)}, f32[8,24,32,128]{3,2,1,0:T(8,128)}) custom-call(s32[1]{0:T(128)} %bitcast.2.parity_ref, s32[1]{0:T(128)} %bitcast.4.core_ref, f32[8,24,32,128]{3,2,1,0:T(8,128)} %get-tuple-element.52.inner_ref, f32[32,32,1024]{2,1,0:T(8,128)} %get-tuple-element.45.turned_ref, ...), custom_call_target="tpu_custom_call" | custom-call | bytes 39000000 | tf_op jit(solution)/shard_map/pallas_call | solution.py:451
  49.6 3.0 %collective-permute-start.2 = (f32[32,1024]{1,0:T(8,128)}, f32[32,1024]{1,0:T(8,128)S(1)}, u32[]{:S(2)}, u32[]{:S(2)}) collective-permute-start(f32[32,1024]{1,0:T(8,128)} %get-tuple-element.57.refs_0_), channel_id=1, source_target_pairs={{0,64},{16,80},{32,96},{48,112},{64,0},{80,16},{96,32},{112,48},{1... | collective-permute-start | bytes 393224 | tf_op jit(solution)/shard_map/ppermute | solution.py:381
  52.8 2.4 %collective-permute-start.4 = (f32[32,1024]{1,0:T(8,128)}, f32[32,1024]{1,0:T(8,128)S(1)}, u32[]{:S(2)}, u32[]{:S(2)}) collective-permute-start(f32[32,1024]{1,0:T(8,128)} %get-tuple-element.57.refs_0_), channel_id=1, source_target_pairs={{0,96},{16,112},{32,0},{48,16},{64,32},{80,48},{96,64},{112,80},{1... | collective-permute-start | bytes 393224 | tf_op jit(solution)/shard_map/ppermute | solution.py:381
  56.5 4.1 %collective-permute-start.7 = (f32[32,1024]{1,0:T(8,128)}, f32[32,1024]{1,0:T(8,128)S(1)}, u32[]{:S(2)}, u32[]{:S(2)}) collective-permute-start(f32[32,1024]{1,0:T(8,128)} %get-tuple-element.56), channel_id=1, source_target_pairs={{0,112},{16,96},{32,16},{48,0},{64,48},{80,32},{96,80},{112,64},{1... | collective-permute-start | bytes 393224 | tf_op jit(solution)/shard_map/ppermute | solution.py:381
  62.6 2.9 %collective-permute-done.6.refs_5_ = f32[32,1024]{1,0:T(8,128)S(1)} collective-permute-done((f32[32,1024]{1,0:T(8,128)}, f32[32,1024]{1,0:T(8,128)S(1)}, u32[]{:S(2)}, u32[]{:S(2)}) %collective-permute-start.6) | collective-permute-done | bytes 131104 | tf_op jit(solution)/shard_map/ppermute | solution.py:381
  68.5 4.5 %all-to-all-start.2 = ((f32[8,24,32,128]{3,2,1,0:T(8,128)}), f32[8,24,32,128]{3,2,1,0:T(8,128)S(1)}, u32[]{:S(2)}, u32[]{:S(2)}) async-start(f32[8,24,32,128]{3,2,1,0:T(8,128)} %get-tuple-element.70), calls=%async_computation.2 | async-start | bytes 6291456 | tf_op jit(solution)/shard_map/all_to_all | solution.py:486
  74.6 5.0 %collective-permute-done.10 = f32[136,256]{1,0:T(8,128)S(1)} collective-permute-done((f32[136,256]{1,0:T(8,128)S(1)}, f32[136,256]{1,0:T(8,128)S(1)}, u32[]{:S(2)}, u32[]{:S(2)}) %collective-permute-start.10) | collective-permute-done | bytes 139296 | tf_op jit(solution)/shard_map/ppermute | solution.py:388
  79.8 5.6 %collective-permute-done.11 = f32[136,256]{1,0:T(8,128)S(1)} collective-permute-done((f32[136,256]{1,0:T(8,128)S(1)}, f32[136,256]{1,0:T(8,128)S(1)}, u32[]{:S(2)}, u32[]{:S(2)}) %collective-permute-start.11) | collective-permute-done | bytes 139296 | tf_op jit(solution)/shard_map/ppermute | solution.py:388
  85.5 4.2 %collective-permute-done.12 = f32[136,256]{1,0:T(8,128)S(1)} collective-permute-done((f32[136,256]{1,0:T(8,128)S(1)}, f32[136,256]{1,0:T(8,128)S(1)}, u32[]{:S(2)}, u32[]{:S(2)}) %collective-permute-start.12) | collective-permute-done | bytes 139296 | tf_op jit(solution)/shard_map/ppermute | solution.py:388
  90.1 5.1 %collective-permute-done.13 = f32[136,256]{1,0:T(8,128)S(1)} collective-permute-done((f32[136,256]{1,0:T(8,128)S(1)}, f32[136,256]{1,0:T(8,128)S(1)}, u32[]{:S(2)}, u32[]{:S(2)}) %collective-permute-start.13) | collective-permute-done | bytes 139296 | tf_op jit(solution)/shard_map/ppermute | solution.py:388
  95.2 4.1 %collective-permute-start.14 = (f32[136,256]{1,0:T(8,128)S(1)}, f32[136,256]{1,0:T(8,128)S(1)}, u32[]{:S(2)}, u32[]{:S(2)}) collective-permute-start(f32[136,256]{1,0:T(8,128)S(1)} %add.96.mine_ref), channel_id=1, source_target_pairs={{0,16},{16,0},{32,48},{48,32},{64,80},{80,64},{96,112},{112,96},{1... | collective-permute-start | bytes 417800 | tf_op jit(solution)/shard_map/ppermute | solution.py:388
  100.3 4.3 %shard_map.68.weights_ref = bf16[2,256,256]{2,1,0:T(8,128)(2,1)S(1)} custom-call(s32[1]{0:T(128)} %bitcast.1.mem_ref, f32[136,256]{1,0:T(8,128)S(1)} %add.96.mine_ref, f32[136,256]{1,0:T(8,128)S(1)} %collective-permute-done.14.other_ref), custom_call_target="tpu_custom_call" | custom-call | bytes 18000000 | tf_op jit(solution)/shard_map/pallas_call | solution.py:492
  104.5 6.1 %all-to-all-done.2.rest_ref = f32[8,24,32,128]{3,2,1,0:T(8,128)S(1)} async-done(((f32[8,24,32,128]{3,2,1,0:T(8,128)}), f32[8,24,32,128]{3,2,1,0:T(8,128)S(1)}, u32[]{:S(2)}, u32[]{:S(2)}) %all-to-all-start.2) | async-done | bytes 3145760 | tf_op jit(solution)/shard_map/all_to_all | solution.py:486
  111.9 4.0 %shard_map.69 = (f32[32,32,1024]{2,1,0:T(8,128)}, f32[32,32,128]{2,1,0:T(8,128)S(1)}, f32[32,32,128]{2,1,0:T(8,128)S(1)}, f32[32,32,128]{2,1,0:T(8,128)}, f32[32...) custom-call(s32[1]{0:T(128)} %bitcast.1.mem_ref, ...), custom_call_target="tpu_custom_call" | custom-call | bytes 18000000 | tf_op jit(solution)/shard_map/pallas_call | solution.py:335
  118.6 3.9 %collective-permute-start.18 = (f32[32,32,128]{2,1,0:T(8,128)}, f32[32,32,128]{2,1,0:T(8,128)S(1)}, u32[]{:S(2)}, u32[]{:S(2)}) collective-permute-start(f32[32,32,128]{2,1,0:T(8,128)} %get-tuple-element.74), channel_id=1, source_target_pairs={{0,80},{16,64},{32,112},{48,96},{64,16},{80,0},{96,48},{112,32},{1... | collective-permute-start | bytes 1572872 | tf_op jit(solution)/shard_map/ppermute | solution.py:381
  122.5 7.7 %collective-permute-done.20.x_ref = f32[32,32,128]{2,1,0:T(8,128)S(1)} collective-permute-done((f32[32,32,128]{2,1,0:T(8,128)S(1)}, f32[32,32,128]{2,1,0:T(8,128)S(1)}, u32[]{:S(2)}, u32[]{:S(2)}) %collective-permute-start.20) | collective-permute-done | bytes 524320 | tf_op jit(solution)/shard_map/ppermute | solution.py:381
  130.2 24.0 %collective-permute-start.16 = (f32[32,32,128]{2,1,0:T(8,128)}, f32[32,32,128]{2,1,0:T(8,128)S(1)}, u32[]{:S(2)}, u32[]{:S(2)}) collective-permute-start(f32[32,32,128]{2,1,0:T(8,128)} %get-tuple-element.72), channel_id=1, source_target_pairs={{0,112},{16,96},{32,16},{48,0},{64,48},{80,32},{96,80},{112,64},{1... | collective-permute-start | bytes 1572872 | tf_op jit(solution)/shard_map/ppermute | solution.py:381
  160.4 4.0 %collective-permute-done.17.x_ref = f32[32,32,128]{2,1,0:T(8,128)S(1)} collective-permute-done((f32[32,32,128]{2,1,0:T(8,128)}, f32[32,32,128]{2,1,0:T(8,128)S(1)}, u32[]{:S(2)}, u32[]{:S(2)}) %collective-permute-start.17) | collective-permute-done | bytes 524320 | tf_op jit(solution)/shard_map/ppermute | solution.py:381
  (73 shorter events, 23.2 us)
Async XLA Ops:
  6.5 26.7 %collective-permute-start = (f32[4,40,1024]{2,1,0:T(8,128)}, f32[4,40,1024]{2,1,0:T(8,128)S(1)}, u32[]{:S(2)}, u32[]{:S(2)}) collective-permute-start(f32[4,40,1024]{2,1,0:T(8,128)} %get-tuple-element.49), channel_id=1, source_target_pairs={{0,1},{1,0},{2,3},{3,2},{4,5},{5,4},{6,7},{7,6},{8,9},{9,8},{10,11... | collective-permute-start | bytes 1966088 | tf_op jit(solution)/shard_map/ppermute | solution.py:421
  9.1 24.2 %collective-permute-start.1 = (f32[4,40,1024]{2,1,0:T(8,128)}, f32[4,40,1024]{2,1,0:T(8,128)S(1)}, u32[]{:S(2)}, u32[]{:S(2)}) collective-permute-start(f32[4,40,1024]{2,1,0:T(8,128)} %get-tuple-element.50), channel_id=1, source_target_pairs={{0,15},{1,2},{2,1},{3,4},{4,3},{5,6},{6,5},{7,8},{8,7},{9,10},{10,... | collective-permute-start | bytes 1966088 | tf_op jit(solution)/shard_map/ppermute | solution.py:418
  14.6 18.7 %all-to-all-start.1 = ((f32[8,8,256]{2,1,0:T(8,128)}), f32[8,8,256]{2,1,0:T(8,128)S(1)}, u32[]{:S(2)}, u32[]{:S(2)}) async-start(f32[8,8,256]{2,1,0:T(8,128)} %broadcast_in_dim.10), calls=%async_computation.1 | async-start | bytes 131072 | tf_op jit(solution)/shard_map/all_to_all | solution.py:426
  33.3 32.2 %all-to-all-start = ((f32[8,8,32,128]{3,2,1,0:T(8,128)}), f32[8,8,32,128]{3,2,1,0:T(8,128)S(1)}, u32[]{:S(2)}, u32[]{:S(2)}) async-start(f32[8,8,32,128]{3,2,1,0:T(8,128)} %get-tuple-element.51), calls=%async_computation | async-start | bytes 2097152 | tf_op jit(solution)/shard_map/all_to_all | solution.py:450
  49.6 6.9 %collective-permute-start.2 = (f32[32,1024]{1,0:T(8,128)}, f32[32,1024]{1,0:T(8,128)S(1)}, u32[]{:S(2)}, u32[]{:S(2)}) collective-permute-start(f32[32,1024]{1,0:T(8,128)} %get-tuple-element.57.refs_0_), channel_id=1, source_target_pairs={{0,64},{16,80},{32,96},{48,112},{64,0},{80,16},{96,32},{112,48},{1... | collective-permute-start | bytes 393224 | tf_op jit(solution)/shard_map/ppermute | solution.py:381
  52.5 8.0 %collective-permute-start.3 = (f32[32,1024]{1,0:T(8,128)}, f32[32,1024]{1,0:T(8,128)S(1)}, u32[]{:S(2)}, u32[]{:S(2)}) collective-permute-start(f32[32,1024]{1,0:T(8,128)} %get-tuple-element.57.refs_0_), channel_id=1, source_target_pairs={{0,32},{16,48},{32,64},{48,80},{64,96},{80,112},{96,0},{112,16},{1... | collective-permute-start | bytes 393224 | tf_op jit(solution)/shard_map/ppermute | solution.py:381
  52.8 7.7 %collective-permute-start.4 = (f32[32,1024]{1,0:T(8,128)}, f32[32,1024]{1,0:T(8,128)S(1)}, u32[]{:S(2)}, u32[]{:S(2)}) collective-permute-start(f32[32,1024]{1,0:T(8,128)} %get-tuple-element.57.refs_0_), channel_id=1, source_target_pairs={{0,96},{16,112},{32,0},{48,16},{64,32},{80,48},{96,64},{112,80},{1... | collective-permute-start | bytes 393224 | tf_op jit(solution)/shard_map/ppermute | solution.py:381
  55.2 7.4 %collective-permute-start.5 = (f32[32,1024]{1,0:T(8,128)}, f32[32,1024]{1,0:T(8,128)S(1)}, u32[]{:S(2)}, u32[]{:S(2)}) collective-permute-start(f32[32,1024]{1,0:T(8,128)} %get-tuple-element.56), channel_id=1, source_target_pairs={{0,80},{16,64},{32,112},{48,96},{64,16},{80,0},{96,48},{112,32},{1... | collective-permute-start | bytes 393224 | tf_op jit(solution)/shard_map/ppermute | solution.py:381
  55.4 10.1 %collective-permute-start.6 = (f32[32,1024]{1,0:T(8,128)}, f32[32,1024]{1,0:T(8,128)S(1)}, u32[]{:S(2)}, u32[]{:S(2)}) collective-permute-start(f32[32,1024]{1,0:T(8,128)} %get-tuple-element.56), channel_id=1, source_target_pairs={{0,48},{16,32},{32,80},{48,64},{64,112},{80,96},{96,16},{112,0},{1... | collective-permute-start | bytes 393224 | tf_op jit(solution)/shard_map/ppermute | solution.py:381
  56.5 9.1 %collective-permute-start.7 = (f32[32,1024]{1,0:T(8,128)}, f32[32,1024]{1,0:T(8,128)S(1)}, u32[]{:S(2)}, u32[]{:S(2)}) collective-permute-start(f32[32,1024]{1,0:T(8,128)} %get-tuple-element.56), channel_id=1, source_target_pairs={{0,112},{16,96},{32,16},{48,0},{64,48},{80,32},{96,80},{112,64},{1... | collective-permute-start | bytes 393224 | tf_op jit(solution)/shard_map/ppermute | solution.py:381
  60.5 5.0 %collective-permute-start.8 = (f32[32,1024]{1,0:T(8,128)}, f32[32,1024]{1,0:T(8,128)S(1)}, u32[]{:S(2)}, u32[]{:S(2)}) collective-permute-start(f32[32,1024]{1,0:T(8,128)} %get-tuple-element.56), channel_id=1, source_target_pairs={{0,16},{16,0},{32,48},{48,32},{64,80},{80,64},{96,112},{112,96},{1... | collective-permute-start | bytes 393224 | tf_op jit(solution)/shard_map/ppermute | solution.py:381
  68.5 42.1 %all-to-all-start.2 = ((f32[8,24,32,128]{3,2,1,0:T(8,128)}), f32[8,24,32,128]{3,2,1,0:T(8,128)S(1)}, u32[]{:S(2)}, u32[]{:S(2)}) async-start(f32[8,24,32,128]{3,2,1,0:T(8,128)} %get-tuple-element.70), calls=%async_computation.2 | async-start | bytes 6291456 | tf_op jit(solution)/shard_map/all_to_all | solution.py:486
  74.5 5.1 %collective-permute-start.10 = (f32[136,256]{1,0:T(8,128)S(1)}, f32[136,256]{1,0:T(8,128)S(1)}, u32[]{:S(2)}, u32[]{:S(2)}) collective-permute-start(f32[136,256]{1,0:T(8,128)S(1)} %add.92), channel_id=1, source_target_pairs={{0,1},{1,0},{2,3},{3,2},{4,5},{5,4},{6,7},{7,6},{8,9},{9,8},{10,11... | collective-permute-start | bytes 417800 | tf_op jit(solution)/shard_map/ppermute | solution.py:388
  79.7 5.7 %collective-permute-start.11 = (f32[136,256]{1,0:T(8,128)S(1)}, f32[136,256]{1,0:T(8,128)S(1)}, u32[]{:S(2)}, u32[]{:S(2)}) collective-permute-start(f32[136,256]{1,0:T(8,128)S(1)} %add.93), channel_id=1, source_target_pairs={{0,2},{1,3},{2,0},{3,1},{4,6},{5,7},{6,4},{7,5},{8,10},{9,11},{10,... | collective-permute-start | bytes 417800 | tf_op jit(solution)/shard_map/ppermute | solution.py:388
  85.4 4.3 %collective-permute-start.12 = (f32[136,256]{1,0:T(8,128)S(1)}, f32[136,256]{1,0:T(8,128)S(1)}, u32[]{:S(2)}, u32[]{:S(2)}) collective-permute-start(f32[136,256]{1,0:T(8,128)S(1)} %add.94), channel_id=1, source_target_pairs={{0,4},{1,5},{2,6},{3,7},{4,0},{5,1},{6,2},{7,3},{8,12},{9,13},{10,... | collective-permute-start | bytes 417800 | tf_op jit(solution)/shard_map/ppermute | solution.py:388
  89.7 5.5 %collective-permute-start.13 = (f32[136,256]{1,0:T(8,128)S(1)}, f32[136,256]{1,0:T(8,128)S(1)}, u32[]{:S(2)}, u32[]{:S(2)}) collective-permute-start(f32[136,256]{1,0:T(8,128)S(1)} %add.95), channel_id=1, source_target_pairs={{0,8},{1,9},{2,10},{3,11},{4,12},{5,13},{6,14},{7,15},{8,0},{9,1},... | collective-permute-start | bytes 417800 | tf_op jit(solution)/shard_map/ppermute | solution.py:388
  95.2 5.1 %collective-permute-start.14 = (f32[136,256]{1,0:T(8,128)S(1)}, f32[136,256]{1,0:T(8,128)S(1)}, u32[]{:S(2)}, u32[]{:S(2)}) collective-permute-start(f32[136,256]{1,0:T(8,128)S(1)} %add.96.mine_ref), channel_id=1, source_target_pairs={{0,16},{16,0},{32,48},{48,32},{64,80},{80,64},{96,112},{112,96},{1... | collective-permute-start | bytes 417800 | tf_op jit(solution)/shard_map/ppermute | solution.py:388
  115.8 14.4 %collective-permute-start.20 = (f32[32,32,128]{2,1,0:T(8,128)S(1)}, f32[32,32,128]{2,1,0:T(8,128)S(1)}, u32[]{:S(2)}, u32[]{:S(2)}) collective-permute-start(f32[32,32,128]{2,1,0:T(8,128)S(1)} %get-tuple-element.76), channel_id=1, source_target_pairs={{0,32},{16,48},{32,64},{48,80},{64,96},{80,112},{96,0},{112,16},{1... | collective-permute-start | bytes 1572872 | tf_op jit(solution)/shard_map/ppermute | solution.py:381
  116.1 38.1 %collective-permute-start.21 = (f32[32,32,128]{2,1,0:T(8,128)S(1)}, f32[32,32,128]{2,1,0:T(8,128)S(1)}, u32[]{:S(2)}, u32[]{:S(2)}) collective-permute-start(f32[32,32,128]{2,1,0:T(8,128)S(1)} %get-tuple-element.77), channel_id=1, source_target_pairs={{0,64},{16,80},{32,96},{48,112},{64,0},{80,16},{96,32},{112,48},{1... | collective-permute-start | bytes 1572872 | tf_op jit(solution)/shard_map/ppermute | solution.py:381
  117.9 40.8 %collective-permute-start.19 = (f32[32,32,128]{2,1,0:T(8,128)}, f32[32,32,128]{2,1,0:T(8,128)S(1)}, u32[]{:S(2)}, u32[]{:S(2)}) collective-permute-start(f32[32,32,128]{2,1,0:T(8,128)} %get-tuple-element.75), channel_id=1, source_target_pairs={{0,96},{16,112},{32,0},{48,16},{64,32},{80,48},{96,64},{112,80},{1... | collective-permute-start | bytes 1572872 | tf_op jit(solution)/shard_map/ppermute | solution.py:381
  118.6 41.0 %collective-permute-start.18 = (f32[32,32,128]{2,1,0:T(8,128)}, f32[32,32,128]{2,1,0:T(8,128)S(1)}, u32[]{:S(2)}, u32[]{:S(2)}) collective-permute-start(f32[32,32,128]{2,1,0:T(8,128)} %get-tuple-element.74), channel_id=1, source_target_pairs={{0,80},{16,64},{32,112},{48,96},{64,16},{80,0},{96,48},{112,32},{1... | collective-permute-start | bytes 1572872 | tf_op jit(solution)/shard_map/ppermute | solution.py:381
  122.5 41.9 %collective-permute-start.17 = (f32[32,32,128]{2,1,0:T(8,128)}, f32[32,32,128]{2,1,0:T(8,128)S(1)}, u32[]{:S(2)}, u32[]{:S(2)}) collective-permute-start(f32[32,32,128]{2,1,0:T(8,128)} %get-tuple-element.73), channel_id=1, source_target_pairs={{0,48},{16,32},{32,80},{48,64},{64,112},{80,96},{96,16},{112,0},{1... | collective-permute-start | bytes 1572872 | tf_op jit(solution)/shard_map/ppermute | solution.py:381
  130.2 35.0 %collective-permute-start.16 = (f32[32,32,128]{2,1,0:T(8,128)}, f32[32,32,128]{2,1,0:T(8,128)S(1)}, u32[]{:S(2)}, u32[]{:S(2)}) collective-permute-start(f32[32,32,128]{2,1,0:T(8,128)} %get-tuple-element.72), channel_id=1, source_target_pairs={{0,112},{16,96},{32,16},{48,0},{64,48},{80,32},{96,80},{112,64},{1... | collective-permute-start | bytes 1572872 | tf_op jit(solution)/shard_map/ppermute | solution.py:381
  155.1 11.0 %collective-permute-start.15 = (f32[32,32,128]{2,1,0:T(8,128)}, f32[32,32,128]{2,1,0:T(8,128)S(1)}, u32[]{:S(2)}, u32[]{:S(2)}) collective-permute-start(f32[32,32,128]{2,1,0:T(8,128)} %get-tuple-element.71), channel_id=1, source_target_pairs={{0,16},{16,0},{32,48},{48,32},{64,80},{80,64},{96,112},{112,96},{1... | collective-permute-start | bytes 1572872 | tf_op jit(solution)/shard_map/ppermute | solution.py:381
  (13 other events, 65.4 us)

commit v9 on v8

--- a/solution.py
+++ b/solution.py
@@ -96,7 +96,8 @@
 
 
 def turn_kernel(
-    parity_ref, prior_ref, h_ref, v_ref, a_ref, b_ref, turned_ref, given, one, sems, out_sems
+    parity_ref, prior_ref, h_ref, v_ref, index_ref, value_ref, weight_ref,
+    a_ref, b_ref, facts_ref, turned_ref, given, one, sems, out_sems,
 ):
     loads = [
         pltpu.make_async_copy(
@@ -106,12 +107,16 @@
     ]
     for load in loads:
         load.start()
+    for n in range(N_MEM):
+        facts_ref[n] = jnp.zeros((SUB, OBS), jnp.float32)
+        facts_ref[n, 0:1] = index_ref[...].astype(jnp.float32)
+        facts_ref[n, 1:2] = value_ref[...]
+        facts_ref[n, 2:3] = weight_ref[...]
     stores = []
     for j in range(GROUPS):
         at = slice(j * LANES, (j + 1) * LANES)
         loads[j].wait()
-        for i in range(ROWS):
-            one[i, :, at] = given[j, pl.ds(i, OWN, stride=ROWS), :]
+        one[:, :, at] = jnp.swapaxes(given[j].reshape(OWN, ROWS, LANES), 0, 1)
         stores.append(
             pltpu.make_async_copy(one.at[:, :, at], turned_ref.at[:, :, at], out_sems.at[j])
         )
@@ -173,7 +178,7 @@
 
 def edge_kernel(
     parity_ref, core_ref, inner_ref, turned_ref, a_ref, b_ref, h_ref, v_ref, facts_ref,
-    same_ref, flip_ref, rest_ref, obs_ref, field, ones, two, coef_ref, in_sem, out_sems, own_sems,
+    same_ref, flip_ref, own_ref, rest_ref, obs_ref, field, ones, two, coef_ref, in_sem, out_sems, own_sems,
 ):
     load = pltpu.make_async_copy(inner_ref, field.at[:, HALO : ROWS - HALO], in_sem)
     load.start()
@@ -234,19 +239,21 @@
             obs_ref[lax.rem(core_ref[0] + g // 4, 2), :, at : at + LANES] = total
     same_ref[...] = obs_ref[0]
     flip_ref[...] = obs_ref[1]
+    own_ref[:OWN] = obs_ref[0]
+    own_ref[OWN:] = jnp.concatenate([facts_ref[4 * core_ref[0] + q] for q in range(4)], axis=1)
     for store in stores:
         store.wait()
 
 
 def gram_kernel(mem_ref, *refs):
-    *from_refs, facts_ref, keep_ref, send_ref, obs_ref = refs
+    *from_refs, keep_ref, send_ref, obs_ref = refs
     mem = mem_ref[0]
     core = lax.rem(mem, 2)
     for (a, b), ref in zip(PATHS, from_refs):
         source = lax.rem(mem // 2 + 4 - a, 4) * 2 + lax.rem(core + b, 2)
-        obs_ref[pl.ds(pl.multiple_of(source * OWN, OWN), OWN), :] = ref[...]
+        obs_ref[pl.ds(pl.multiple_of(source * OWN, OWN), OWN), :] = ref[:OWN]
     obs = obs_ref[...]
-    facts = jnp.concatenate([facts_ref[4 * core + q] for q in range(4)], axis=1)
+    facts = from_refs[0][OWN:]
     mean = jnp.sum(obs, axis=0, keepdims=True) * (1.0 / MEMBERS)
     anomalies = obs - mean
     weighted = split(anomalies * facts[2:3])
@@ -401,11 +408,12 @@
     ]
     mem = mem.reshape(1)
 
-    halo_a, halo_b, turned = pl.pallas_call(
+    halo_a, halo_b, facts, turned = pl.pallas_call(
         turn_kernel,
-        out_shape=[f32(HALO, OWN + SUB, WIDTH)] * 2 + [f32(ROWS, OWN, WIDTH)],
-        in_specs=[SMEM, anywhere, VMEM, VMEM],
-        out_specs=[VMEM, VMEM, anywhere],
+        out_shape=[f32(HALO, OWN + SUB, WIDTH)] * 2
+        + [f32(N_MEM, SUB, OBS), f32(ROWS, OWN, WIDTH)],
+        in_specs=[SMEM, anywhere] + [VMEM] * 5,
+        out_specs=[VMEM, VMEM, VMEM, anywhere],
         scratch_shapes=[
             pltpu.VMEM((GROUPS, OWN * ROWS, LANES), jnp.float32),
             pltpu.VMEM((ROWS, OWN, WIDTH), jnp.float32),
@@ -413,19 +421,16 @@
             pltpu.SemaphoreType.DMA((GROUPS,)),
         ],
         compiler_params=params(56),
-    )(parity, prior_samples.reshape(OWN * ROWS, WIDTH), h, v)
+    )(
+        parity, prior_samples.reshape(OWN * ROWS, WIDTH), h, v, obs_index, obs_value, obs_weight
+    )
     halo_a, halo_b, turned, h, v = lax.optimization_barrier((halo_a, halo_b, turned, h, v))
     halo_b = lax.ppermute(
         halo_b, "reg", [(i, (i - 1 if i % 2 == 0 else i + 1) % N_REG) for i in range(N_REG)]
     )
     halo_a = lax.ppermute(halo_a, "reg", [(i, i ^ 1) for i in range(N_REG)])
 
-    facts = jnp.concatenate(
-        [obs_index.astype(jnp.float32), obs_value, obs_weight, jnp.zeros((SUB - 3, OBS))], axis=0
-    )
-    facts = lax.all_to_all(
-        jnp.broadcast_to(facts[None], (N_MEM, SUB, OBS)), "mem", 0, 0, tiled=True
-    )
+    facts = lax.all_to_all(facts, "mem", 0, 0, tiled=True)
 
     inner, early = pl.pallas_call(
         interior_kernel,
@@ -448,15 +453,16 @@
     )(turned, h, v)
     early, halo_a, halo_b = lax.optimization_barrier((early, halo_a, halo_b))
     early = lax.all_to_all(early, "mem", 0, 0, tiled=True)
-    same, flip, rest = pl.pallas_call(
+    same, flip, own, rest = pl.pallas_call(
         edge_kernel,
         out_shape=[
             f32(OWN, HALF_OBS),
             f32(OWN, HALF_OBS),
+            f32(OWN + SUB, HALF_OBS),
             f32(GROUPS, ROWS - CHUNK, OWN, LANES),
         ],
         in_specs=[SMEM, SMEM, anywhere, anywhere] + [VMEM] * 5,
-        out_specs=[VMEM, VMEM, anywhere],
+        out_specs=[VMEM, VMEM, VMEM, anywhere],
         scratch_shapes=[
             pltpu.VMEM((2, OWN, HALF_OBS), jnp.float32),
             pltpu.VMEM((GROUPS, ROWS, OWN, LANES), jnp.float32),
@@ -470,18 +476,18 @@
         compiler_params=params(56),
         cost_estimate=cost(13),
     )(parity, core, inner, turned, halo_a, halo_b, h, v, facts)
-    obs = [same] + [send_on(flip if b else same, a, b) for a, b in PATHS[1:]]
+    obs = [own] + [send_on(flip if b else same, a, b) for a, b in PATHS[1:]]
     early, *obs = lax.optimization_barrier((early, *obs))
 
     keep, send = pl.pallas_call(
         gram_kernel,
         out_shape=[f32(MEMBERS // 2 + 8, MEMBERS)] * 2,
-        in_specs=[SMEM] + [VMEM] * (N_MEM + 1),
+        in_specs=[SMEM] + [VMEM] * N_MEM,
         out_specs=[VMEM, VMEM],
         scratch_shapes=[pltpu.VMEM((MEMBERS, HALF_OBS), jnp.float32)],
         compiler_params=params(12),
         cost_estimate=cost(3),
-    )(mem, *obs, facts)
+    )(mem, *obs)
     rest, send = lax.optimization_barrier((rest, send))
     rest = lax.all_to_all(rest, "mem", 0, 0, tiled=True)
     total = keep + swap(send, "mem", 1)

time: 168 us -> 166 us (0.988)
    unnamed x24 -> x16, local copies, waits for them, and re-layouts: 4.92 us -> 4.16 us
  transfers between devices with their start and end apart: 25 -> 25, of which waited for: 12 -> 12; matrix products, arithmetic and copies ran while one was open for 1% -> 0% of each run, Pallas kernels for 20% -> 21%
where the time goes in v9:
time: 166 us; the launch traced here: 165 us
  starting transfers between devices  69.1 us (42%)
  Pallas kernels  45.9 us (28%)
  waiting for transfers between devices  45.5 us (27%)
  local copies, waits for them, and re-layouts  4.16 us (3%)
    ppermute x14, starting transfers between devices, send_on(): lax.ppermute(x, 'mem', [(i, (i // 2 + a) % 4 * 2 + (i + b) % 2) for i in...  42.3 us
    ppermute x6, waiting for transfers between devices, swap(): return lax.ppermute(x, axis, [(i, i ^ bit) for i in range(count)])  22.3 us
    ppermute x14, waiting for transfers between devices, send_on(): lax.ppermute(x, 'mem', [(i, (i // 2 + a) % 4 * 2 + (i + b) % 2) for i in...  17.1 us
    pallas_call x1, Pallas kernels, local(): pl.pallas_call(interior_kernel, out_shape=[f32(GROUPS, ROWS - EDGE, OWN,...  13.2 us
    pallas_call x1, Pallas kernels, local(): pl.pallas_call(edge_kernel, out_shape=[f32(OWN, HALF_OBS), f32(OWN, HALF_...  11.9 us
    all_to_all x1, waiting for transfers between devices, local(): rest = lax.all_to_all(rest, 'mem', 0, 0, tiled=True)  6.1 us
    pallas_call x7, Pallas kernels, place(): pl.pallas_call(place_kernel, grid_spec=pltpu.PrefetchScalarGridSpec(num_s...  5.79 us
    pallas_call x1, Pallas kernels, local(): pl.pallas_call(turn_kernel, out_shape=[f32(HALO, OWN + SUB, WIDTH)] * 2 +...  5.72 us
  transfers between devices with their start and end apart: 25, of which 12 were waited for; matrix products, arithmetic and copies ran while one was open for 0% of the time, Pallas kernels for 21%

profile of v9, /device:TPU:1, one launch (start us, length us, event | category | flops | bytes accessed | tf_op | source)
XLA Modules:
  0.0 165.0 jit_solution(17243346605887517266)
XLA Ops:
  0.0 5.7 %shard_map.64 = (f32[4,40,1024]{2,1,0:T(8,128)}, f32[4,40,1024]{2,1,0:T(8,128)}, f32[8,8,256]{2,1,0:T(8,128)}, f32[32,32,1024]{2,1,0:T(8,128)}) custom-call(s32[1]{0:T(128)} %bitcast.2.parity_ref, f32[1024,1024]{1,0:T(8,128)} %bitcast.11, f32[32,1024]{1,0:T(8,128)} %h_ref.3, f32[32,1024]{1,0:T(8,128)} %v_ref.3, s32[1,256]{1,0:T(1,128)} %index_ref.1, ...), custom_call_target="tpu_custom_call" | custom-call | tf_op jit(solution)/shard_map/pallas_call | solution.py:411
  5.7 2.5 %collective-permute-start = (f32[4,40,1024]{2,1,0:T(8,128)}, f32[4,40,1024]{2,1,0:T(8,128)S(1)}, u32[]{:S(2)}, u32[]{:S(2)}) collective-permute-start(f32[4,40,1024]{2,1,0:T(8,128)} %get-tuple-element.51), channel_id=1, source_target_pairs={{0,1},{1,0},{2,3},{3,2},{4,5},{5,4},{6,7},{7,6},{8,9},{9,8},{10,11... | collective-permute-start | bytes 1966088 | tf_op jit(solution)/shard_map/ppermute | solution.py:431
  8.3 4.7 %collective-permute-start.1 = (f32[4,40,1024]{2,1,0:T(8,128)}, f32[4,40,1024]{2,1,0:T(8,128)S(1)}, u32[]{:S(2)}, u32[]{:S(2)}) collective-permute-start(f32[4,40,1024]{2,1,0:T(8,128)} %get-tuple-element.52), channel_id=1, source_target_pairs={{0,15},{1,2},{2,1},{3,4},{4,3},{5,6},{6,5},{7,8},{8,7},{9,10},{10,... | collective-permute-start | bytes 1966088 | tf_op jit(solution)/shard_map/ppermute | solution.py:428
  13.0 5.5 %all-to-all-start.1 = ((f32[8,8,256]{2,1,0:T(8,128)}), f32[8,8,256]{2,1,0:T(8,128)S(1)}, u32[]{:S(2)}, u32[]{:S(2)}) async-start(f32[8,8,256]{2,1,0:T(8,128)} %get-tuple-element.57), calls=%async_computation.1 | async-start | bytes 131072 | tf_op jit(solution)/shard_map/all_to_all | solution.py:433
  18.5 13.2 %shard_map.65 = (f32[8,24,32,128]{3,2,1,0:T(8,128)}, f32[8,8,32,128]{3,2,1,0:T(8,128)}) custom-call(f32[32,32,1024]{2,1,0:T(8,128)} %get-tuple-element.47.turned_ref, f32[32,1024]{1,0:T(8,128)} %h_ref.3, f32[32,1024]{1,0:T(8,128)} %v_ref.3), custom_call_target="tpu_custom_call" | custom-call | bytes 39000000 | tf_op jit(solution)/shard_map/pallas_call | solution.py:435
  31.7 4.8 %all-to-all-start = ((f32[8,8,32,128]{3,2,1,0:T(8,128)}), f32[8,8,32,128]{3,2,1,0:T(8,128)S(1)}, u32[]{:S(2)}, u32[]{:S(2)}) async-start(f32[8,8,32,128]{3,2,1,0:T(8,128)} %get-tuple-element.53), calls=%async_computation | async-start | bytes 2097152 | tf_op jit(solution)/shard_map/all_to_all | solution.py:455
  36.6 11.9 %shard_map.66 = (f32[32,1024]{1,0:T(8,128)}, f32[32,1024]{1,0:T(8,128)}, f32[40,1024]{1,0:T(8,128)}, f32[8,24,32,128]{3,2,1,0:T(8,128)}) custom-call(s32[1]{0:T(128)} %bitcast.2.parity_ref, s32[1]{0:T(128)} %bitcast.4.core_ref, f32[8,24,32,128]{3,2,1,0:T(8,128)} %get-tuple-element.54.inner_ref, f32[32,32,1024]{2,1,0:T(8,128)} %get-tuple-element.47.turned_ref, ...), custom_call_target="tpu_custom_call" | custom-call | bytes 39000000 | tf_op jit(solution)/shard_map/pallas_call | solution.py:456
  48.4 3.0 %collective-permute-start.2 = (f32[32,1024]{1,0:T(8,128)}, f32[32,1024]{1,0:T(8,128)S(1)}, u32[]{:S(2)}, u32[]{:S(2)}) collective-permute-start(f32[32,1024]{1,0:T(8,128)} %get-tuple-element.59), channel_id=1, source_target_pairs={{0,64},{16,80},{32,96},{48,112},{64,0},{80,16},{96,32},{112,48},{1... | collective-permute-start | bytes 393224 | tf_op jit(solution)/shard_map/ppermute | solution.py:388
  51.7 2.4 %collective-permute-start.4 = (f32[32,1024]{1,0:T(8,128)}, f32[32,1024]{1,0:T(8,128)S(1)}, u32[]{:S(2)}, u32[]{:S(2)}) collective-permute-start(f32[32,1024]{1,0:T(8,128)} %get-tuple-element.59), channel_id=1, source_target_pairs={{0,96},{16,112},{32,0},{48,16},{64,32},{80,48},{96,64},{112,80},{1... | collective-permute-start | bytes 393224 | tf_op jit(solution)/shard_map/ppermute | solution.py:388
  55.3 4.1 %collective-permute-start.7 = (f32[32,1024]{1,0:T(8,128)}, f32[32,1024]{1,0:T(8,128)S(1)}, u32[]{:S(2)}, u32[]{:S(2)}) collective-permute-start(f32[32,1024]{1,0:T(8,128)} %get-tuple-element.60), channel_id=1, source_target_pairs={{0,112},{16,96},{32,16},{48,0},{64,48},{80,32},{96,80},{112,64},{1... | collective-permute-start | bytes 393224 | tf_op jit(solution)/shard_map/ppermute | solution.py:388
  61.5 2.9 %collective-permute-done.6.refs_5_ = f32[32,1024]{1,0:T(8,128)S(1)} collective-permute-done((f32[32,1024]{1,0:T(8,128)}, f32[32,1024]{1,0:T(8,128)S(1)}, u32[]{:S(2)}, u32[]{:S(2)}) %collective-permute-start.6) | collective-permute-done | bytes 131104 | tf_op jit(solution)/shard_map/ppermute | solution.py:388
  66.7 4.5 %all-to-all-start.2 = ((f32[8,24,32,128]{3,2,1,0:T(8,128)}), f32[8,24,32,128]{3,2,1,0:T(8,128)S(1)}, u32[]{:S(2)}, u32[]{:S(2)}) async-start(f32[8,24,32,128]{3,2,1,0:T(8,128)} %get-tuple-element.74), calls=%async_computation.2 | async-start | bytes 6291456 | tf_op jit(solution)/shard_map/all_to_all | solution.py:492
  72.8 5.0 %collective-permute-done.10 = f32[136,256]{1,0:T(8,128)S(1)} collective-permute-done((f32[136,256]{1,0:T(8,128)S(1)}, f32[136,256]{1,0:T(8,128)S(1)}, u32[]{:S(2)}, u32[]{:S(2)}) %collective-permute-start.10) | collective-permute-done | bytes 139296 | tf_op jit(solution)/shard_map/ppermute | solution.py:395
  77.9 5.6 %collective-permute-done.11 = f32[136,256]{1,0:T(8,128)S(1)} collective-permute-done((f32[136,256]{1,0:T(8,128)S(1)}, f32[136,256]{1,0:T(8,128)S(1)}, u32[]{:S(2)}, u32[]{:S(2)}) %collective-permute-start.11) | collective-permute-done | bytes 139296 | tf_op jit(solution)/shard_map/ppermute | solution.py:395
  83.6 4.2 %collective-permute-done.12 = f32[136,256]{1,0:T(8,128)S(1)} collective-permute-done((f32[136,256]{1,0:T(8,128)S(1)}, f32[136,256]{1,0:T(8,128)S(1)}, u32[]{:S(2)}, u32[]{:S(2)}) %collective-permute-start.12) | collective-permute-done | bytes 139296 | tf_op jit(solution)/shard_map/ppermute | solution.py:395
  88.3 5.1 %collective-permute-done.13 = f32[136,256]{1,0:T(8,128)S(1)} collective-permute-done((f32[136,256]{1,0:T(8,128)S(1)}, f32[136,256]{1,0:T(8,128)S(1)}, u32[]{:S(2)}, u32[]{:S(2)}) %collective-permute-start.13) | collective-permute-done | bytes 139296 | tf_op jit(solution)/shard_map/ppermute | solution.py:395
  93.4 4.1 %collective-permute-start.14 = (f32[136,256]{1,0:T(8,128)S(1)}, f32[136,256]{1,0:T(8,128)S(1)}, u32[]{:S(2)}, u32[]{:S(2)}) collective-permute-start(f32[136,256]{1,0:T(8,128)S(1)} %add.96.mine_ref), channel_id=1, source_target_pairs={{0,16},{16,0},{32,48},{48,32},{64,80},{80,64},{96,112},{112,96},{1... | collective-permute-start | bytes 417800 | tf_op jit(solution)/shard_map/ppermute | solution.py:395
  98.4 4.3 %shard_map.68.weights_ref = bf16[2,256,256]{2,1,0:T(8,128)(2,1)S(1)} custom-call(s32[1]{0:T(128)} %bitcast.1.mem_ref, f32[136,256]{1,0:T(8,128)S(1)} %add.96.mine_ref, f32[136,256]{1,0:T(8,128)S(1)} %collective-permute-done.14.other_ref), custom_call_target="tpu_custom_call" | custom-call | bytes 18000000 | tf_op jit(solution)/shard_map/pallas_call | solution.py:498
  102.7 6.1 %all-to-all-done.2.rest_ref = f32[8,24,32,128]{3,2,1,0:T(8,128)S(1)} async-done(((f32[8,24,32,128]{3,2,1,0:T(8,128)}), f32[8,24,32,128]{3,2,1,0:T(8,128)S(1)}, u32[]{:S(2)}, u32[]{:S(2)}) %all-to-all-start.2) | async-done | bytes 3145760 | tf_op jit(solution)/shard_map/all_to_all | solution.py:492
  110.0 3.9 %shard_map.69 = (f32[32,32,1024]{2,1,0:T(8,128)}, f32[32,32,128]{2,1,0:T(8,128)S(1)}, f32[32,32,128]{2,1,0:T(8,128)S(1)}, f32[32,32,128]{2,1,0:T(8,128)}, f32[32...) custom-call(s32[1]{0:T(128)} %bitcast.1.mem_ref, ...), custom_call_target="tpu_custom_call" | custom-call | bytes 18000000 | tf_op jit(solution)/shard_map/pallas_call | solution.py:342
  116.7 3.9 %collective-permute-start.18 = (f32[32,32,128]{2,1,0:T(8,128)}, f32[32,32,128]{2,1,0:T(8,128)S(1)}, u32[]{:S(2)}, u32[]{:S(2)}) collective-permute-start(f32[32,32,128]{2,1,0:T(8,128)} %get-tuple-element.78), channel_id=1, source_target_pairs={{0,80},{16,64},{32,112},{48,96},{64,16},{80,0},{96,48},{112,32},{1... | collective-permute-start | bytes 1572872 | tf_op jit(solution)/shard_map/ppermute | solution.py:388
  120.6 7.7 %collective-permute-done.20.x_ref = f32[32,32,128]{2,1,0:T(8,128)S(1)} collective-permute-done((f32[32,32,128]{2,1,0:T(8,128)S(1)}, f32[32,32,128]{2,1,0:T(8,128)S(1)}, u32[]{:S(2)}, u32[]{:S(2)}) %collective-permute-start.20) | collective-permute-done | bytes 524320 | tf_op jit(solution)/shard_map/ppermute | solution.py:388
  128.3 24.0 %collective-permute-start.16 = (f32[32,32,128]{2,1,0:T(8,128)}, f32[32,32,128]{2,1,0:T(8,128)S(1)}, u32[]{:S(2)}, u32[]{:S(2)}) collective-permute-start(f32[32,32,128]{2,1,0:T(8,128)} %get-tuple-element.76), channel_id=1, source_target_pairs={{0,112},{16,96},{32,16},{48,0},{64,48},{80,32},{96,80},{112,64},{1... | collective-permute-start | bytes 1572872 | tf_op jit(solution)/shard_map/ppermute | solution.py:388
  158.5 4.0 %collective-permute-done.17.x_ref = f32[32,32,128]{2,1,0:T(8,128)S(1)} collective-permute-done((f32[32,32,128]{2,1,0:T(8,128)}, f32[32,32,128]{2,1,0:T(8,128)S(1)}, u32[]{:S(2)}, u32[]{:S(2)}) %collective-permute-start.17) | collective-permute-done | bytes 524320 | tf_op jit(solution)/shard_map/ppermute | solution.py:388
  (60 shorter events, 21.7 us)
Async XLA Ops:
  5.7 26.0 %collective-permute-start = (f32[4,40,1024]{2,1,0:T(8,128)}, f32[4,40,1024]{2,1,0:T(8,128)S(1)}, u32[]{:S(2)}, u32[]{:S(2)}) collective-permute-start(f32[4,40,1024]{2,1,0:T(8,128)} %get-tuple-element.51), channel_id=1, source_target_pairs={{0,1},{1,0},{2,3},{3,2},{4,5},{5,4},{6,7},{7,6},{8,9},{9,8},{10,11... | collective-permute-start | bytes 1966088 | tf_op jit(solution)/shard_map/ppermute | solution.py:431
  8.3 23.4 %collective-permute-start.1 = (f32[4,40,1024]{2,1,0:T(8,128)}, f32[4,40,1024]{2,1,0:T(8,128)S(1)}, u32[]{:S(2)}, u32[]{:S(2)}) collective-permute-start(f32[4,40,1024]{2,1,0:T(8,128)} %get-tuple-element.52), channel_id=1, source_target_pairs={{0,15},{1,2},{2,1},{3,4},{4,3},{5,6},{6,5},{7,8},{8,7},{9,10},{10,... | collective-permute-start | bytes 1966088 | tf_op jit(solution)/shard_map/ppermute | solution.py:428
  13.0 18.8 %all-to-all-start.1 = ((f32[8,8,256]{2,1,0:T(8,128)}), f32[8,8,256]{2,1,0:T(8,128)S(1)}, u32[]{:S(2)}, u32[]{:S(2)}) async-start(f32[8,8,256]{2,1,0:T(8,128)} %get-tuple-element.57), calls=%async_computation.1 | async-start | bytes 131072 | tf_op jit(solution)/shard_map/all_to_all | solution.py:433
  31.7 32.7 %all-to-all-start = ((f32[8,8,32,128]{3,2,1,0:T(8,128)}), f32[8,8,32,128]{3,2,1,0:T(8,128)S(1)}, u32[]{:S(2)}, u32[]{:S(2)}) async-start(f32[8,8,32,128]{3,2,1,0:T(8,128)} %get-tuple-element.53), calls=%async_computation | async-start | bytes 2097152 | tf_op jit(solution)/shard_map/all_to_all | solution.py:455
  48.4 6.9 %collective-permute-start.2 = (f32[32,1024]{1,0:T(8,128)}, f32[32,1024]{1,0:T(8,128)S(1)}, u32[]{:S(2)}, u32[]{:S(2)}) collective-permute-start(f32[32,1024]{1,0:T(8,128)} %get-tuple-element.59), channel_id=1, source_target_pairs={{0,64},{16,80},{32,96},{48,112},{64,0},{80,16},{96,32},{112,48},{1... | collective-permute-start | bytes 393224 | tf_op jit(solution)/shard_map/ppermute | solution.py:388
  51.4 8.0 %collective-permute-start.3 = (f32[32,1024]{1,0:T(8,128)}, f32[32,1024]{1,0:T(8,128)S(1)}, u32[]{:S(2)}, u32[]{:S(2)}) collective-permute-start(f32[32,1024]{1,0:T(8,128)} %get-tuple-element.59), channel_id=1, source_target_pairs={{0,32},{16,48},{32,64},{48,80},{64,96},{80,112},{96,0},{112,16},{1... | collective-permute-start | bytes 393224 | tf_op jit(solution)/shard_map/ppermute | solution.py:388
  51.7 7.7 %collective-permute-start.4 = (f32[32,1024]{1,0:T(8,128)}, f32[32,1024]{1,0:T(8,128)S(1)}, u32[]{:S(2)}, u32[]{:S(2)}) collective-permute-start(f32[32,1024]{1,0:T(8,128)} %get-tuple-element.59), channel_id=1, source_target_pairs={{0,96},{16,112},{32,0},{48,16},{64,32},{80,48},{96,64},{112,80},{1... | collective-permute-start | bytes 393224 | tf_op jit(solution)/shard_map/ppermute | solution.py:388
  54.1 7.4 %collective-permute-start.5 = (f32[32,1024]{1,0:T(8,128)}, f32[32,1024]{1,0:T(8,128)S(1)}, u32[]{:S(2)}, u32[]{:S(2)}) collective-permute-start(f32[32,1024]{1,0:T(8,128)} %get-tuple-element.60), channel_id=1, source_target_pairs={{0,80},{16,64},{32,112},{48,96},{64,16},{80,0},{96,48},{112,32},{1... | collective-permute-start | bytes 393224 | tf_op jit(solution)/shard_map/ppermute | solution.py:388
  54.3 10.1 %collective-permute-start.6 = (f32[32,1024]{1,0:T(8,128)}, f32[32,1024]{1,0:T(8,128)S(1)}, u32[]{:S(2)}, u32[]{:S(2)}) collective-permute-start(f32[32,1024]{1,0:T(8,128)} %get-tuple-element.60), channel_id=1, source_target_pairs={{0,48},{16,32},{32,80},{48,64},{64,112},{80,96},{96,16},{112,0},{1... | collective-permute-start | bytes 393224 | tf_op jit(solution)/shard_map/ppermute | solution.py:388
  55.3 9.1 %collective-permute-start.7 = (f32[32,1024]{1,0:T(8,128)}, f32[32,1024]{1,0:T(8,128)S(1)}, u32[]{:S(2)}, u32[]{:S(2)}) collective-permute-start(f32[32,1024]{1,0:T(8,128)} %get-tuple-element.60), channel_id=1, source_target_pairs={{0,112},{16,96},{32,16},{48,0},{64,48},{80,32},{96,80},{112,64},{1... | collective-permute-start | bytes 393224 | tf_op jit(solution)/shard_map/ppermute | solution.py:388
  59.4 5.0 %collective-permute-start.8 = (f32[32,1024]{1,0:T(8,128)}, f32[32,1024]{1,0:T(8,128)S(1)}, u32[]{:S(2)}, u32[]{:S(2)}) collective-permute-start(f32[32,1024]{1,0:T(8,128)} %get-tuple-element.60), channel_id=1, source_target_pairs={{0,16},{16,0},{32,48},{48,32},{64,80},{80,64},{96,112},{112,96},{1... | collective-permute-start | bytes 393224 | tf_op jit(solution)/shard_map/ppermute | solution.py:388
  66.7 42.1 %all-to-all-start.2 = ((f32[8,24,32,128]{3,2,1,0:T(8,128)}), f32[8,24,32,128]{3,2,1,0:T(8,128)S(1)}, u32[]{:S(2)}, u32[]{:S(2)}) async-start(f32[8,24,32,128]{3,2,1,0:T(8,128)} %get-tuple-element.74), calls=%async_computation.2 | async-start | bytes 6291456 | tf_op jit(solution)/shard_map/all_to_all | solution.py:492
  72.7 5.1 %collective-permute-start.10 = (f32[136,256]{1,0:T(8,128)S(1)}, f32[136,256]{1,0:T(8,128)S(1)}, u32[]{:S(2)}, u32[]{:S(2)}) collective-permute-start(f32[136,256]{1,0:T(8,128)S(1)} %add.92), channel_id=1, source_target_pairs={{0,1},{1,0},{2,3},{3,2},{4,5},{5,4},{6,7},{7,6},{8,9},{9,8},{10,11... | collective-permute-start | bytes 417800 | tf_op jit(solution)/shard_map/ppermute | solution.py:395
  77.8 5.7 %collective-permute-start.11 = (f32[136,256]{1,0:T(8,128)S(1)}, f32[136,256]{1,0:T(8,128)S(1)}, u32[]{:S(2)}, u32[]{:S(2)}) collective-permute-start(f32[136,256]{1,0:T(8,128)S(1)} %add.93), channel_id=1, source_target_pairs={{0,2},{1,3},{2,0},{3,1},{4,6},{5,7},{6,4},{7,5},{8,10},{9,11},{10,... | collective-permute-start | bytes 417800 | tf_op jit(solution)/shard_map/ppermute | solution.py:395
  83.6 4.3 %collective-permute-start.12 = (f32[136,256]{1,0:T(8,128)S(1)}, f32[136,256]{1,0:T(8,128)S(1)}, u32[]{:S(2)}, u32[]{:S(2)}) collective-permute-start(f32[136,256]{1,0:T(8,128)S(1)} %add.94), channel_id=1, source_target_pairs={{0,4},{1,5},{2,6},{3,7},{4,0},{5,1},{6,2},{7,3},{8,12},{9,13},{10,... | collective-permute-start | bytes 417800 | tf_op jit(solution)/shard_map/ppermute | solution.py:395
  87.9 5.5 %collective-permute-start.13 = (f32[136,256]{1,0:T(8,128)S(1)}, f32[136,256]{1,0:T(8,128)S(1)}, u32[]{:S(2)}, u32[]{:S(2)}) collective-permute-start(f32[136,256]{1,0:T(8,128)S(1)} %add.95), channel_id=1, source_target_pairs={{0,8},{1,9},{2,10},{3,11},{4,12},{5,13},{6,14},{7,15},{8,0},{9,1},... | collective-permute-start | bytes 417800 | tf_op jit(solution)/shard_map/ppermute | solution.py:395
  93.4 5.1 %collective-permute-start.14 = (f32[136,256]{1,0:T(8,128)S(1)}, f32[136,256]{1,0:T(8,128)S(1)}, u32[]{:S(2)}, u32[]{:S(2)}) collective-permute-start(f32[136,256]{1,0:T(8,128)S(1)} %add.96.mine_ref), channel_id=1, source_target_pairs={{0,16},{16,0},{32,48},{48,32},{64,80},{80,64},{96,112},{112,96},{1... | collective-permute-start | bytes 417800 | tf_op jit(solution)/shard_map/ppermute | solution.py:395
  114.0 14.4 %collective-permute-start.20 = (f32[32,32,128]{2,1,0:T(8,128)S(1)}, f32[32,32,128]{2,1,0:T(8,128)S(1)}, u32[]{:S(2)}, u32[]{:S(2)}) collective-permute-start(f32[32,32,128]{2,1,0:T(8,128)S(1)} %get-tuple-element.80), channel_id=1, source_target_pairs={{0,32},{16,48},{32,64},{48,80},{64,96},{80,112},{96,0},{112,16},{1... | collective-permute-start | bytes 1572872 | tf_op jit(solution)/shard_map/ppermute | solution.py:388
  114.3 38.1 %collective-permute-start.21 = (f32[32,32,128]{2,1,0:T(8,128)S(1)}, f32[32,32,128]{2,1,0:T(8,128)S(1)}, u32[]{:S(2)}, u32[]{:S(2)}) collective-permute-start(f32[32,32,128]{2,1,0:T(8,128)S(1)} %get-tuple-element.81), channel_id=1, source_target_pairs={{0,64},{16,80},{32,96},{48,112},{64,0},{80,16},{96,32},{112,48},{1... | collective-permute-start | bytes 1572872 | tf_op jit(solution)/shard_map/ppermute | solution.py:388
  116.0 40.8 %collective-permute-start.19 = (f32[32,32,128]{2,1,0:T(8,128)}, f32[32,32,128]{2,1,0:T(8,128)S(1)}, u32[]{:S(2)}, u32[]{:S(2)}) collective-permute-start(f32[32,32,128]{2,1,0:T(8,128)} %get-tuple-element.79), channel_id=1, source_target_pairs={{0,96},{16,112},{32,0},{48,16},{64,32},{80,48},{96,64},{112,80},{1... | collective-permute-start | bytes 1572872 | tf_op jit(solution)/shard_map/ppermute | solution.py:388
  116.7 41.0 %collective-permute-start.18 = (f32[32,32,128]{2,1,0:T(8,128)}, f32[32,32,128]{2,1,0:T(8,128)S(1)}, u32[]{:S(2)}, u32[]{:S(2)}) collective-permute-start(f32[32,32,128]{2,1,0:T(8,128)} %get-tuple-element.78), channel_id=1, source_target_pairs={{0,80},{16,64},{32,112},{48,96},{64,16},{80,0},{96,48},{112,32},{1... | collective-permute-start | bytes 1572872 | tf_op jit(solution)/shard_map/ppermute | solution.py:388
  120.6 41.9 %collective-permute-start.17 = (f32[32,32,128]{2,1,0:T(8,128)}, f32[32,32,128]{2,1,0:T(8,128)S(1)}, u32[]{:S(2)}, u32[]{:S(2)}) collective-permute-start(f32[32,32,128]{2,1,0:T(8,128)} %get-tuple-element.77), channel_id=1, source_target_pairs={{0,48},{16,32},{32,80},{48,64},{64,112},{80,96},{96,16},{112,0},{1... | collective-permute-start | bytes 1572872 | tf_op jit(solution)/shard_map/ppermute | solution.py:388
  128.3 35.0 %collective-permute-start.16 = (f32[32,32,128]{2,1,0:T(8,128)}, f32[32,32,128]{2,1,0:T(8,128)S(1)}, u32[]{:S(2)}, u32[]{:S(2)}) collective-permute-start(f32[32,32,128]{2,1,0:T(8,128)} %get-tuple-element.76), channel_id=1, source_target_pairs={{0,112},{16,96},{32,16},{48,0},{64,48},{80,32},{96,80},{112,64},{1... | collective-permute-start | bytes 1572872 | tf_op jit(solution)/shard_map/ppermute | solution.py:388
  153.2 11.0 %collective-permute-start.15 = (f32[32,32,128]{2,1,0:T(8,128)}, f32[32,32,128]{2,1,0:T(8,128)S(1)}, u32[]{:S(2)}, u32[]{:S(2)}) collective-permute-start(f32[32,32,128]{2,1,0:T(8,128)} %get-tuple-element.75), channel_id=1, source_target_pairs={{0,16},{16,0},{32,48},{48,32},{64,80},{80,64},{96,112},{112,96},{1... | collective-permute-start | bytes 1572872 | tf_op jit(solution)/shard_map/ppermute | solution.py:388
  (9 other events, 22.4 us)
